TPU v7x, 32 devices: a whole 2x2x4 slice. The times are simulated.
32 devices in a mesh: scen: 4 (over y, x), blk: 8 (over z, core).
Axes of the slice: x: 2, y: 2, z: 4, core: 2. Of those that a mesh axis runs over, the one named last changes fastest.
Arguments:
- link: bfloat16 [16, 256, 4096], P('scen', None, 'blk'), may hold values from -0.3125 to 0.3125
- leaf_inverse: bfloat16 [16, 256, 256], P('scen'), as said below
- leaf_rhs: float32 [16, 256], P('scen'), may hold values from -6 to 6
- node_rhs: float32 [2, 4096], P(None, 'blk'), may hold values from -6 to 6
- node_diag: float32 [2, 4096], P(None, 'blk'), may hold values from 0.5 to 4
- parent: int32 [16], P('scen'), may hold values from 0 to 1
- tile_mask: int32 [16, 8], P('scen', 'blk'), may hold values 0 or 1
Outputs:
- node_solution: float32 [2, 4096], P(None, 'blk')
- leaf_solution: float32 [16, 256], P('scen')
- schur: float32 [2, 4096, 4096], P(None, 'blk', 'scen')
Inputs may be any that keep to these rules, and one draw needn't show every extreme that they name: `leaf_inverse`: its diagonal entries lie within 1 to 2.
All inputs are finite; a program needn't handle non-finite values. No bound on the sum of `tile_mask` on one device may be relied on, other than what follows from the above.
Results may differ from a plain program's by a relative error of at most 0.0017.
Values may be sent and summed in bfloat16 or wider, within the bound.
No kernel may reach another device: no remote copies, remote signals or barrier semaphores. Data moves between devices by JAX's collectives and lax.ppermute only.
A program may use at most 256 MiB of HBM per device.

v0:
```python
import jax
import jax.numpy as jnp
from jax import lax
from jax.sharding import PartitionSpec as P

ITERS = 4


highest = lax.Precision.HIGHEST
damping = 0.4


def body(link, leaf_inverse, leaf_rhs, node_rhs, node_diag, parent, tile_mask):
    leaf_count, width_leaf, tile_width = link.shape
    node_count = node_rhs.shape[0]
    blk_index = lax.axis_index("blk")
    node_ids = lax.broadcasted_iota(jnp.int32, (leaf_count, node_count), 1)
    member = parent[:, None] == node_ids
    member_f = member.astype(jnp.float32)
    masked = link * tile_mask.astype(jnp.bfloat16)[:, :, None]
    solved = jnp.einsum(
        "lnm,lmc->lnc", leaf_inverse, masked, preferred_element_type=jnp.float32
    ).astype(jnp.bfloat16)
    chosen = masked[None] * member.astype(jnp.bfloat16).T[:, :, None, None]
    chosen = chosen.reshape(node_count, leaf_count * width_leaf, tile_width)
    portion = lax.all_gather(solved, "blk", axis=2, tiled=True)
    stacked = portion.reshape(leaf_count * width_leaf, portion.shape[2])
    partial_value = jnp.einsum("pkr,kc->prc", chosen, stacked, preferred_element_type=jnp.float32)
    diagonal_tile = lax.dynamic_slice_in_dim(partial_value, blk_index * tile_width, tile_width, 2)
    diag_terms = jnp.diagonal(diagonal_tile, axis1=1, axis2=2)
    inverse_f = leaf_inverse.astype(jnp.float32)
    masked_f = masked.astype(jnp.float32)
    leaf_solve = jnp.einsum("lnm,lm->ln", inverse_f, leaf_rhs, precision=highest)
    leaf_terms = jnp.einsum("lnc,ln->lc", masked_f, leaf_solve, precision=highest)
    rhs_terms = jnp.dot(member_f.T, leaf_terms, precision=highest)
    rhs_sum, diag_sum = lax.psum((rhs_terms, diag_terms), "scen")
    reduced = node_rhs - rhs_sum
    scaling = node_diag + diag_sum
    schur_rows = lax.psum_scatter(partial_value, "scen", scatter_dimension=1, tiled=True)
    schur_out = lax.all_to_all(schur_rows, "scen", split_axis=2, concat_axis=1, tiled=True)
    solved_f = solved.astype(jnp.float32)
    current = reduced / scaling
    for sweep in range(ITERS):
        parent_tile = jnp.dot(member_f, current, precision=highest)
        local_image = jnp.einsum("lnc,lc->ln", solved_f, parent_tile, precision=highest)
        leaf_image = lax.psum(local_image, "blk")
        spread = jnp.einsum("lnc,ln->lc", masked_f, leaf_image, precision=highest)
        node_terms = jnp.dot(member_f.T, spread, precision=highest)
        coupled = lax.psum(node_terms, "scen")
        product = node_diag * current + coupled
        current = current + damping * (reduced - product) / scaling
    parent_values = jnp.dot(member_f, current, precision=highest)
    link_term = jnp.einsum("lnc,lc->ln", masked_f, parent_values, precision=highest)
    summed = lax.psum(link_term, "blk")
    leaf_solution = jnp.einsum("lnm,lm->ln", inverse_f, leaf_rhs - summed, precision=highest)
    return (current, leaf_solution, schur_out)


def solution(mesh):
    in_specs = (
        P("scen", None, "blk"),
        P("scen", None, None),
        P("scen", None),
        P(None, "blk"),
        P(None, "blk"),
        P("scen"),
        P("scen", "blk"),
    )
    out_specs = (P(None, "blk"), P("scen", None), P(None, "blk", "scen"))
    return jax.shard_map(body, mesh=mesh, in_specs=in_specs, out_specs=out_specs, check_vma=False)
```

profile of v0, /device:TPU:0, one launch (start us, length us, event | category | flops | bytes accessed | tf_op | source)
XLA Modules:
  0.0 381.5 jit_solution(2528303058364519275)
XLA Ops:
  7.2 0.7 convert_bitcast_fusion
  7.9 1.4 broadcast_multiply_fusion
  9.3 1.5 convolution_convert_fusion
  10.9 0.5 copy.22
  11.5 84.3 %all-gather.2.cloned.1.call-done = bf16[4,256,4096]{1,2,0:T(8,128)(2,1)} async-done(((bf16[4,256,512]{1,2,0:T(8,128)(2,1)}), bf16[4,256,4096]{1,2,0:T(8,128)(2,1)}) %all-gather.2.cloned.1.call-update) | async-done | bytes 8388624 | tf_op jit(solution)/shard_map/all_gather | solution.py:26
  95.8 14.5 %convolution_bitcast_fusion = f32[2,512,4096]{2,1,0:T(8,128)} fusion(bf16[4,256,4096]{1,2,0:T(8,128)(2,1)} %all-gather.2.cloned.1.call-done, bf16[2,4]{1,0:T(2,128)(2,1)S(1)} %compare_convert_fusion, bf16[4,256,512]{1,2,0:T(8,128)(2,1)S(1)} %copy.22), kind=kOutput, calls=%fused_computation.1 | convolution fusion | flops 8590983168 | bytes 26214416 | tf_op jit(solution)/shard_map/pkr,kc->prc/dot_general | solution.py:28
  110.3 0.7 copy-done.3
  111.5 0.5 fusion.39
  112.2 3.1 constant_dynamic-slice_fusion
  115.3 60.2 %copy.25 = f32[2,512,512]{0,2,1:T(8,128)} copy(f32[2,512,512]{2,1,0:T(8,128)} %constant_dynamic-slice_fusion) | data formatting | bytes 4194304 | tf_op jit(solution)/shard_map/dynamic_slice | solution.py:29
  175.5 5.9 %gather_fusion = f32[512,2]{1,0:T(8,128)S(1)} fusion(f32[2,512,512]{0,2,1:T(8,128)} %copy.25, s32[512]{0:T(512)S(1)} %bitcast.89), kind=kCustom, calls=%fused_computation | custom fusion | bytes 12288 | tf_op jit(solution)/shard_map/jit(diagonal)/gather | solution.py:30
  181.6 10.2 %all-reduce = (f32[2,512]{1,0:T(2,128)S(1)}, f32[2,512]{1,0:T(2,128)S(1)}) all-reduce(f32[2,512]{1,0:T(2,128)S(1)} %fusion.12, f32[2,512]{1,0:T(2,128)S(1)} %bitcast.93), channel_id=1, replica_groups=mesh['scen'=4,'blk'=8] {'scen'}, use_global_device_ids=true, to_apply=%region_0.1 | all-reduce | flops 2048 | bytes 16384 | tf_op jit(solution)/shard_map/psum | solution.py:36
  192.0 0.5 fusion.26
  192.5 13.6 %psum.79 = f32[4,256]{1,0:T(4,128)S(1)} all-reduce(f32[4,256]{1,0:T(4,128)S(1)} %bitcast.98), channel_id=1, replica_groups=mesh['scen'=4,'blk'=8] {'blk'}, use_global_device_ids=true, to_apply=%region_2.3 | all-reduce | flops 1024 | bytes 8192 | tf_op jit(solution)/shard_map/psum | solution.py:46
  206.1 0.5 fusion.37
  206.9 8.0 %psum.80 = f32[2,512]{1,0:T(2,128)S(1)} all-reduce(f32[2,512]{1,0:T(2,128)S(1)} %fusion.10), channel_id=1, replica_groups=mesh['scen'=4,'blk'=8] {'scen'}, use_global_device_ids=true, to_apply=%region_3.4 | all-reduce | flops 1024 | bytes 8192 | tf_op jit(solution)/shard_map/psum | solution.py:49
  215.2 0.5 fusion.23
  215.7 13.6 %psum.81 = f32[4,256]{1,0:T(4,128)S(1)} all-reduce(f32[4,256]{1,0:T(4,128)S(1)} %bitcast.99), channel_id=1, replica_groups=mesh['scen'=4,'blk'=8] {'blk'}, use_global_device_ids=true, to_apply=%region_4.5 | all-reduce | flops 1024 | bytes 8192 | tf_op jit(solution)/shard_map/psum | solution.py:46
  230.1 9.4 %psum.82 = f32[2,512]{1,0:T(2,128)S(1)} all-reduce(f32[2,512]{1,0:T(2,128)S(1)} %fusion.8), channel_id=1, replica_groups=mesh['scen'=4,'blk'=8] {'scen'}, use_global_device_ids=true, to_apply=%region_5.6 | all-reduce | flops 1024 | bytes 8192 | tf_op jit(solution)/shard_map/psum | solution.py:49
  239.4 24.1 %reduce-scatter.2.cloned.1.call-done = f32[2,128,4096]{2,1,0:T(8,128)} async-done(((f32[2,512,4096]{2,1,0:T(8,128)}), f32[2,128,4096]{2,1,0:T(8,128)}) %reduce-scatter.2.cloned.1.call-update) | async-done | bytes 4194320 | tf_op jit(solution)/shard_map/reduce_scatter | solution.py:39
  263.6 7.2 %copy.27 = f32[2,128,4096]{1,0,2:T(2,128)} copy(f32[2,128,4096]{2,1,0:T(8,128)} %reduce-scatter.2.cloned.1.call-done) | data formatting | bytes 8388608 | tf_op jit(solution)/shard_map/reduce_scatter | solution.py:39
  270.7 4.9 %all-to-all-start = ((f32[2,128,4096]{1,0,2:T(2,128)}), f32[2,128,4096]{1,0,2:T(2,128)}, u32[]{:S(2)}, u32[]{:S(2)}) async-start(f32[2,128,4096]{1,0,2:T(2,128)} %copy.27), calls=%async_computation.1 | async-start | bytes 8388608 | tf_op jit(solution)/shard_map/all_to_all | solution.py:40
  275.8 0.5 fusion.20
  276.3 16.3 %psum.83 = f32[4,256]{1,0:T(4,128)S(1)} all-reduce(f32[4,256]{1,0:T(4,128)S(1)} %bitcast.100), channel_id=1, replica_groups=mesh['scen'=4,'blk'=8] {'blk'}, use_global_device_ids=true, to_apply=%region_6.7 | all-reduce | flops 1024 | bytes 8192 | tf_op jit(solution)/shard_map/psum | solution.py:46
  293.5 32.9 %psum.84 = f32[2,512]{1,0:T(2,128)S(1)} all-reduce(f32[2,512]{1,0:T(2,128)S(1)} %fusion.6), channel_id=1, replica_groups=mesh['scen'=4,'blk'=8] {'scen'}, use_global_device_ids=true, to_apply=%region_7.8 | all-reduce | flops 1024 | bytes 8192 | tf_op jit(solution)/shard_map/psum | solution.py:49
  326.5 0.5 fusion.17
  327.1 14.8 %psum.85 = f32[4,256]{1,0:T(4,128)S(1)} all-reduce(f32[4,256]{1,0:T(4,128)S(1)} %bitcast.101), channel_id=1, replica_groups=mesh['scen'=4,'blk'=8] {'blk'}, use_global_device_ids=true, to_apply=%region_8.9 | all-reduce | flops 1024 | bytes 8192 | tf_op jit(solution)/shard_map/psum | solution.py:46
  342.7 8.9 %psum.86 = f32[2,512]{1,0:T(2,128)S(1)} all-reduce(f32[2,512]{1,0:T(2,128)S(1)} %fusion.4), channel_id=1, replica_groups=mesh['scen'=4,'blk'=8] {'scen'}, use_global_device_ids=true, to_apply=%region_9.10 | all-reduce | flops 1024 | bytes 8192 | tf_op jit(solution)/shard_map/psum | solution.py:49
  351.8 0.9 fusion.14
  352.7 13.6 %psum.87 = f32[4,256]{1,0:T(4,128)S(1)} all-reduce(f32[4,256]{1,0:T(4,128)S(1)} %bitcast.102), channel_id=1, replica_groups=mesh['scen'=4,'blk'=8] {'blk'}, use_global_device_ids=true, to_apply=%region_10.11 | all-reduce | flops 1024 | bytes 8192 | tf_op jit(solution)/shard_map/psum | solution.py:54
  366.9 0.6 copy.108
  367.5 7.2 %copy.28 = f32[2,4,128,1024]{3,2,1,0:T(8,128)} copy(f32[2,4,128,1024]{2,0,3,1:T(2,128)} %bitcast.32) | data formatting | bytes 8388608 | tf_op jit(solution)/shard_map/all_to_all | solution.py:40
  (48 shorter events, 5.2 us)
Async XLA Ops:
  7.2 2.1 copy-start
  7.2 4.3 %copy-start.6 = (s32[4]{0:T(128)S(1)}, s32[4]{0:T(128)}, u32[]{:S(2)}) copy-start(s32[4]{0:T(128)} %param.12) | copy-start | bytes 52
  7.2 88.6 %all-gather.2.cloned.1.call-start = ((), (), s32[]{:S(2)}) async-start(), calls=%async_computation.2 | async-start | bytes 9437184 | tf_op jit(solution)/shard_map/all_gather | solution.py:26
  10.9 252.7 %reduce-scatter.2.cloned.1.call-start = ((), (), s32[]{:S(2)}) async-start(), calls=%async_computation.3 | async-start | bytes 20971520 | tf_op jit(solution)/shard_map/reduce_scatter | solution.py:39
  110.2 0.7 copy-start.3
  115.3 76.5 %copy-start.2 = (f32[2,512]{1,0:T(2,128)S(1)}, f32[2,512]{1,0:T(2,128)}, u32[]{:S(2)}) copy-start(f32[2,512]{1,0:T(2,128)} %param.11) | copy-start | bytes 12292
  115.3 76.5 %copy-start.4 = (f32[2,512]{1,0:T(2,128)S(1)}, f32[2,512]{1,0:T(2,128)}, u32[]{:S(2)}) copy-start(f32[2,512]{1,0:T(2,128)} %param.10) | copy-start | bytes 12292
  115.3 76.7 %copy-start.1 = (bf16[4,512,256]{2,1,0:T(8,128)(2,1)S(1)}, bf16[4,512,256]{2,1,0:T(8,128)(2,1)}, u32[]{:S(2)}) copy-start(bf16[4,512,256]{2,1,0:T(8,128)(2,1)} %convolution_convert_fusion) | copy-start | bytes 3145732
  270.7 96.7 %all-to-all-start = ((f32[2,128,4096]{1,0,2:T(2,128)}), f32[2,128,4096]{1,0,2:T(2,128)}, u32[]{:S(2)}, u32[]{:S(2)}) async-start(f32[2,128,4096]{1,0,2:T(2,128)} %copy.27), calls=%async_computation.1 | async-start | bytes 8388608 | tf_op jit(solution)/shard_map/all_to_all | solution.py:40
  351.6 23.0 %copy-start.5 = (f32[2,512]{1,0:T(2,128)}, f32[2,512]{1,0:T(2,128)S(1)}, u32[]{:S(2)}) copy-start(f32[2,512]{1,0:T(2,128)S(1)} %divide_add_fusion) | copy-start | bytes 12292
Sparse Core Ops, SparseCore 0:
  11.0 84.7 all-gather.1
  110.4 153.1 reduce-scatter.1
where the time goes:
time: 384 us; the launch traced here: 382 us
  blocking collectives  141 us (37%)
  waiting for transfers between devices  108 us (28%)
  local copies, waits for them, and re-layouts  85.5 us (22%)
  matrix products  24.8 us (6%)
  between operations  14.2 us (4%)
  starting transfers between devices  4.94 us (1%)
    all_gather x1, waiting for transfers between devices, body(): portion = lax.all_gather(solved, 'blk', axis=2, tiled=True)  84.3 us
    dynamic_slice x2, local copies, waits for them, and re-layouts, body(): lax.dynamic_slice_in_dim(partial_value, blk_index * tile_width, tile_widt...  63.3 us
    psum x4, blocking collectives, body(): coupled = lax.psum(node_terms, 'scen')  59.2 us
    psum x4, blocking collectives, body(): leaf_image = lax.psum(local_image, 'blk')  58.4 us
    reduce_scatter x1, waiting for transfers between devices, body(): lax.psum_scatter(partial_value, 'scen', scatter_dimension=1, tiled=True)  24.1 us
    dot_general x1, matrix products, body(): jnp.einsum('pkr,kc->prc', chosen, stacked, preferred_element_type=jnp.flo...  14.5 us
    psum x1, blocking collectives, body(): summed = lax.psum(link_term, 'blk')  13.6 us
    psum x1, blocking collectives, body(): rhs_sum, diag_sum = lax.psum((rhs_terms, diag_terms), 'scen')  10.2 us
  transfers between devices with their start and end apart: 3, of which 2 were waited for; matrix products, arithmetic and copies ran while one was open for 21% of the time, Pallas kernels for 0%

commit v1 on v0

v1 whole, which is shorter than its diff:
```python
import functools

import jax
import jax.numpy as jnp
from jax import lax
from jax.experimental import pallas as pl
from jax.experimental.pallas import tpu as pltpu
from jax.sharding import PartitionSpec as P

ITERS = 4
highest = lax.Precision.HIGHEST
damping = 0.4
F32 = jnp.float32
BF16 = jnp.bfloat16
MIB = 1 << 20

VM = pl.BlockSpec(memory_space=pltpu.VMEM)
SM = pl.BlockSpec(memory_space=pltpu.SMEM)
HB = pl.BlockSpec(memory_space=pl.ANY)
NO_COST = pl.CostEstimate(flops=0, bytes_accessed=0, transcendentals=0)


def general_body(link, leaf_inverse, leaf_rhs, node_rhs, node_diag, parent, tile_mask):
    leaf_count, width_leaf, tile_width = link.shape
    node_count = node_rhs.shape[0]
    blk_index = lax.axis_index("blk")
    node_ids = lax.broadcasted_iota(jnp.int32, (leaf_count, node_count), 1)
    member = parent[:, None] == node_ids
    member_f = member.astype(F32)
    masked = link * tile_mask.astype(BF16)[:, :, None]
    solved = jnp.einsum("lnm,lmc->lnc", leaf_inverse, masked, preferred_element_type=F32).astype(BF16)
    chosen = masked[None] * member.astype(BF16).T[:, :, None, None]
    chosen = chosen.reshape(node_count, leaf_count * width_leaf, tile_width)
    portion = lax.all_gather(solved, "blk", axis=2, tiled=True)
    stacked = portion.reshape(leaf_count * width_leaf, portion.shape[2])
    partial_value = jnp.einsum("pkr,kc->prc", chosen, stacked, preferred_element_type=F32)
    diagonal_tile = lax.dynamic_slice_in_dim(partial_value, blk_index * tile_width, tile_width, 2)
    diag_terms = jnp.diagonal(diagonal_tile, axis1=1, axis2=2)
    inverse_f = leaf_inverse.astype(F32)
    masked_f = masked.astype(F32)
    leaf_solve = jnp.einsum("lnm,lm->ln", inverse_f, leaf_rhs, precision=highest)
    leaf_terms = jnp.einsum("lnc,ln->lc", masked_f, leaf_solve, precision=highest)
    rhs_terms = jnp.dot(member_f.T, leaf_terms, precision=highest)
    rhs_sum, diag_sum = lax.psum((rhs_terms, diag_terms), "scen")
    reduced = node_rhs - rhs_sum
    scaling = node_diag + diag_sum
    schur_rows = lax.psum_scatter(partial_value, "scen", scatter_dimension=1, tiled=True)
    schur_out = lax.all_to_all(schur_rows, "scen", split_axis=2, concat_axis=1, tiled=True)
    solved_f = solved.astype(F32)
    current = reduced / scaling
    for sweep in range(ITERS):
        parent_tile = jnp.dot(member_f, current, precision=highest)
        local_image = jnp.einsum("lnc,lc->ln", solved_f, parent_tile, precision=highest)
        leaf_image = lax.psum(local_image, "blk")
        spread = jnp.einsum("lnc,ln->lc", masked_f, leaf_image, precision=highest)
        node_terms = jnp.dot(member_f.T, spread, precision=highest)
        coupled = lax.psum(node_terms, "scen")
        product = node_diag * current + coupled
        current = current + damping * (reduced - product) / scaling
    parent_values = jnp.dot(member_f, current, precision=highest)
    link_term = jnp.einsum("lnc,lc->ln", masked_f, parent_values, precision=highest)
    summed = lax.psum(link_term, "blk")
    leaf_solution = jnp.einsum("lnm,lm->ln", inverse_f, leaf_rhs - summed, precision=highest)
    return (current, leaf_solution, schur_out)


def split3(x):
    hi = x.astype(BF16)
    rest = x - hi.astype(F32)
    mid = rest.astype(BF16)
    low = (rest - mid.astype(F32)).astype(BF16)
    row = lax.broadcasted_iota(jnp.int32, (8, x.shape[1]), 0)
    wide = lambda v: jnp.broadcast_to(v.astype(F32), (8, x.shape[1]))
    out = jnp.where(row == 0, wide(hi), jnp.where(row == 1, wide(mid), jnp.where(row == 2, wide(low), 0.0)))
    return out.astype(BF16)


def rowdot(x, mat, transposed):
    dims = (((1,), (1 if transposed else 0,)), ((), ()))
    return jnp.sum(lax.dot_general(split3(x), mat, dims, preferred_element_type=F32), axis=0, keepdims=True)


def start_kernel(leaves, width, core_ref, mask_ref, parent_ref, link_ref, inverse_ref, rhs_ref, bundle_ref, notes_ref):
    half = leaves // 2
    base = leaves * width
    for i in range(half):
        bundle_ref[pl.ds(base, width), pl.ds(i * width, width)] = inverse_ref[core_ref[0] * half + i]
    notes_ref[...] = jnp.zeros_like(notes_ref)
    value = rhs_ref[...]
    for n in range(3):
        term = value.astype(BF16).astype(F32)
        notes_ref[pl.ds(n * leaves, leaves), pl.ds(0, width)] = term
        value = value - term
    for l in range(leaves):
        notes_ref[pl.ds(3 * leaves + l, 1), :] = jnp.full((1, notes_ref.shape[1]), parent_ref[l].astype(F32))
    bundle_ref[pl.ds(base + width, 4 * leaves), :] = notes_ref[...].astype(BF16)
    for l in range(leaves):
        rows = pl.ds(l * width, width)
        tile = jnp.where(mask_ref[l] != 0, link_ref[l].astype(F32), 0.0).astype(BF16)
        bundle_ref[rows, :] = tile


def solved_kernel(leaves, width, bundle_ref, inverse_ref, solved_ref):
    for l in range(leaves):
        rows = pl.ds(l * width, width)
        solved_ref[rows, :] = jnp.dot(inverse_ref[l], bundle_ref[rows, :], preferred_element_type=F32).astype(BF16)


def cut_kernel(x_hbm, y_hbm, *refs):
    top_ref, end_ref, sem = refs[-3:]
    cut = top_ref.shape[0]
    copies = [pltpu.make_async_copy(x_hbm.at[pl.ds(0, cut)], top_ref, sem.at[0]),
              pltpu.make_async_copy(y_hbm.at[pl.ds(cut, end_ref.shape[0])], end_ref, sem.at[1])]
    for copy in copies:
        copy.start()
    for copy in copies:
        copy.wait()


def node_add(acc, parent, value):
    return [jnp.where(parent == p, a + value, a) for p, a in enumerate(acc)]


def tree(groups):
    while len(groups) > 1:
        groups = [[a + b for a, b in zip(groups[i], groups[i + 1])] for i in range(0, len(groups), 2)]
    return groups[0]


def image_rows(mat_ref, at, split, parent):
    lhs = split[0]
    for q in range(1, len(split)):
        lhs = jnp.where(parent == q, split[q].astype(F32), lhs.astype(F32)).astype(BF16)
    out = lax.dot_general(lhs, mat_ref[at, :], (((1,), (1,)), ((), ())), preferred_element_type=F32)
    return jnp.sum(out, axis=0, keepdims=True)


def group_work(leaves, width, first_leaf, group, tile_of, inv_of, m_ref, km_ref, rhs_ref, parent_ref, nodes, cols):
    zero = jnp.zeros((1, cols), F32)
    diag, right = [zero] * nodes, [zero] * nodes
    for i in range(leaves):
        l = first_leaf + i
        rows = pl.ds((group * leaves + i) * width, width)
        inv, tile = inv_of(i), tile_of(i)
        m_ref[rows, :] = tile
        solved = jnp.dot(inv, tile, preferred_element_type=F32).astype(BF16)
        km_ref[rows, :] = solved
        p = parent_ref[l]
        diag = node_add(diag, p, jnp.sum(tile.astype(F32) * solved.astype(F32), axis=0, keepdims=True))
        leaf = rowdot(rhs_ref[pl.ds(l, 1), :], inv, True)
        right = node_add(right, p, rowdot(leaf, tile, False))
    return diag, right


def tile_in(leaves, width, cut, top_ref, end_ref):
    def tile(i):
        top = min(max(cut - i * width, 0), width)
        parts = []
        if top:
            parts.append(top_ref[pl.ds(i * width, top), :])
        if top < width:
            parts.append(end_ref[pl.ds(i * width + top - cut, width - top), :])
        return parts[0] if len(parts) == 1 else jnp.concatenate(parts, axis=0)
    return tile


def pair_in(leaves, width, core_ref, own, other):
    first = core_ref[0] == 0
    own, other = own.astype(F32), other.astype(F32)
    pair = [jnp.where(first, own, other).astype(BF16), jnp.where(first, other, own).astype(BF16)]
    def inv(i):
        h, j = divmod(i, leaves // 2)
        return pair[h][:, j * width:(j + 1) * width]
    return inv


def early_kernel(leaves, width, nodes, core_ref, parent_ref, rhs_ref, inverse_ref, own_ref, x_ref, y_ref, swap_ref, m_ref, km_ref,
                 diag_ref, right_ref):
    base, cols = leaves * width, own_ref.shape[1]
    for k, ref in enumerate((own_ref, x_ref, y_ref)):
        if k:
            inv = pair_in(leaves, width, core_ref, ref[pl.ds(base, width), :], swap_ref[pl.ds((k - 1) * width, width), :])
        else:
            inv = lambda i: inverse_ref[i]
        tile = lambda i: ref[pl.ds(i * width, width), :]
        diag, right = group_work(leaves, width, k * leaves, k, tile, inv, m_ref, km_ref, rhs_ref, parent_ref, nodes, cols)
        for p in range(nodes):
            diag_ref[pl.ds(k * nodes + p, 1), :] = diag[p]
            right_ref[pl.ds(k * nodes + p, 1), :] = right[p]


def late_kernel(leaves, width, cut, core_ref, parent_ref, rhs_ref, node_rhs_ref, node_diag_ref, da_ref, db_ref, swap_ref, early_ref,
                diag_ref, right_ref, token_ref, m_ref, km_ref, reduced_ref, scaling_ref, x_ref, part_ref):
    del token_ref
    nodes, cols = node_rhs_ref.shape
    base = leaves * width
    inv = pair_in(leaves, width, core_ref, db_ref[pl.ds(base - cut, width), :], swap_ref[...])
    diag, right = group_work(leaves, width, 3 * leaves, 0, tile_in(leaves, width, cut, da_ref, db_ref), inv, m_ref, km_ref, rhs_ref,
                             parent_ref, nodes, cols)
    rows = lambda ref: [[ref[pl.ds(k * nodes + p, 1), :] for p in range(nodes)] for k in range(3)]
    diag, right = tree(rows(diag_ref) + [diag]), tree(rows(right_ref) + [right])
    start = []
    for p in range(nodes):
        at = pl.ds(p, 1)
        reduced = node_rhs_ref[at, :] - right[p]
        scaling = node_diag_ref[at, :] + diag[p]
        reduced_ref[at, :] = reduced
        scaling_ref[at, :] = scaling
        start.append(split3(reduced / scaling))
        x_ref[at, :] = reduced / scaling
    image(leaves, width, early_ref, km_ref, start, parent_ref, part_ref)


def image(leaves, width, early_ref, late_ref, split, parent_ref, part_ref):
    for l in range(4 * leaves):
        ref, at = (early_ref, l) if l < 3 * leaves else (late_ref, l - 3 * leaves)
        row = image_rows(ref, pl.ds(at * width, width), split, parent_ref[l])
        part_ref[pl.ds(l, 1), :] = row


def sweep_kernel(leaves, width, last, ties, parent_ref, y_ref, z_ref, reduced_ref, scaling_ref, diag_ref, x_in_ref, m_ref, km_ref, m3_ref,
                 km3_ref, *refs):
    x_ref, part_ref = refs[ties:]
    nodes = x_in_ref.shape[0]
    whole = y_ref[...] + z_ref[...]
    zero = jnp.zeros((1, x_in_ref.shape[1]), F32)
    groups = []
    for k in range(4):
        acc = [zero] * nodes
        for i in range(leaves):
            l = k * leaves + i
            mat = m_ref[pl.ds(l * width, width), :] if k < 3 else m3_ref[pl.ds(i * width, width), :]
            acc = node_add(acc, parent_ref[l], rowdot(whole[l:l + 1, :], mat, False))
        groups.append(acc)
    coupled = tree(groups)
    new = []
    for p in range(nodes):
        at = pl.ds(p, 1)
        x = x_in_ref[at, :]
        x = x + damping * (reduced_ref[at, :] - diag_ref[at, :] * x - coupled[p]) / scaling_ref[at, :]
        x_ref[at, :] = x
        new.append(split3(x))
    if last:
        for l in range(leaves):
            row = image_rows(m_ref, pl.ds(l * width, width), new, parent_ref[l])
            part_ref[pl.ds(l, 1), :] = row
    else:
        image(leaves, width, km_ref, km3_ref, new, parent_ref, part_ref)


def leaf_kernel(leaves, y_ref, z_ref, rhs_ref, inverse_ref, *refs):
    out_ref = refs[-1]
    rest = rhs_ref[...] - (y_ref[...] + z_ref[...])
    for l in range(leaves):
        out_ref[pl.ds(l, 1), :] = rowdot(rest[l:l + 1, :], inverse_ref[l], True)


def pick(places, sources, ties):
    shape = jax.ShapeDtypeStruct(sources[0].shape, sources[0].dtype)
    count = places.shape[0]

    def kernel(place_ref, *refs):
        first = len(sources) + len(ties)
        ins, outs, token_ref = refs[:len(sources)], refs[first:first + count], refs[first + count]
        held, sem_in, sem_out = refs[first + count + 1:]
        token_ref[...] = jnp.zeros_like(token_ref)
        for n in range(count):
            for i, source in enumerate(ins):
                @pl.when(place_ref[n] == i)
                def _():
                    pltpu.make_async_copy(source, held.at[n], sem_in.at[n]).start()
        for n in range(count):
            @pl.when(place_ref[n] >= 0)
            def _():
                pltpu.make_async_copy(ins[0], held.at[n], sem_in.at[n]).wait()
                pltpu.make_async_copy(held.at[n], outs[n], sem_out.at[n]).start()
        for n in range(count):
            @pl.when(place_ref[n] >= 0)
            def _():
                pltpu.make_async_copy(held.at[n], outs[n], sem_out.at[n]).wait()

    return pl.pallas_call(
        kernel,
        out_shape=[shape] * count + [jax.ShapeDtypeStruct((8, 128), F32)],
        in_specs=[SM] + [HB] * (len(sources) + len(ties)),
        out_specs=[HB] * count + [VM],
        scratch_shapes=[pltpu.VMEM((count,) + shape.shape, shape.dtype), pltpu.SemaphoreType.DMA((count,)),
                        pltpu.SemaphoreType.DMA((count,))],
        compiler_params=pltpu.CompilerParams(vmem_limit_bytes=56 * MIB),
        cost_estimate=NO_COST,
    )(places, *sources, *ties)


def product_kernel(leaves, width, info_ref, parent_ref, m_hbm, m3_hbm, *refs):
    near, far = refs[:8], refs[8:16]
    out_hbm, m_ref, u_ref, acc_ref, sem, out_sem = refs[16:]
    cols = m_ref.shape[1]
    base = leaves * width
    core, is_far = info_ref[0], info_ref[1]
    m_copies = [pltpu.make_async_copy(m_hbm, m_ref.at[pl.ds(0, 3 * base)], sem.at[8]),
                pltpu.make_async_copy(m3_hbm, m_ref.at[pl.ds(3 * base, base)], sem.at[9])]
    for copy in m_copies:
        copy.start()
    for n in range(8):
        for flag, group in ((0, near), (1, far)):
            @pl.when(is_far == flag)
            def _():
                pltpu.make_async_copy(group[n], u_ref.at[n], sem.at[n]).start()
    acc_ref[...] = jnp.zeros_like(acc_ref)
    for copy in m_copies:
        copy.wait()
    for side in range(2):
        for k in range(4):
            n = side * 4 + k
            pltpu.make_async_copy(near[n], u_ref.at[n], sem.at[n]).wait()

            @pl.loop(0, leaves)
            def _(i):
                tile = m_ref[pl.ds((k * leaves + i) * width, width), :]
                unit = u_ref[n, pl.ds(i * width, width), :]
                value = lax.dot_general(tile, unit, (((0,), (0,)), ((), ())), preferred_element_type=F32)
                acc_ref[side, parent_ref[k * leaves + i]] += value

        where = core if side == 0 else 1 - core
        for half in range(2):
            @pl.when(where == half)
            def _():
                pltpu.make_async_copy(acc_ref.at[side], out_hbm.at[:, :, pl.ds(half * cols, cols)], out_sem.at[side]).start()
    for side in range(2):
        pltpu.make_async_copy(acc_ref.at[side], out_hbm.at[:, :, pl.ds(0, cols)], out_sem.at[side]).wait()


def plane_body(scen, blk, link, leaf_inverse, leaf_rhs, node_rhs, node_diag, parent, tile_mask):
    leaves, width, cols = link.shape
    nodes = node_rhs.shape[0]
    base = leaves * width
    planes = blk // 2
    s, b = lax.axis_index("scen"), lax.axis_index("blk")
    z, core = b // 2, b % 2
    core1 = core.reshape(1)

    def over_scen(x, k):
        return lax.ppermute(x, "scen", [(i, i ^ k) for i in range(scen)])

    def over_z(x, step, sources):
        return lax.ppermute(x, "blk", [(2 * i + c, 2 * (i + step) + c) for i in sources for c in range(2)])

    def flip_z(x, k):
        return lax.ppermute(x, "blk", [(i, i ^ (2 * k)) for i in range(blk)])

    def flip_core(x):
        return lax.ppermute(x, "blk", [(i, i ^ 1) for i in range(blk)])

    def distance(i, j):
        return abs(i - j)

    def in_plane(x, k, far):
        pairs = [((i ^ k) * blk + 2 * j + c, i * blk + 2 * j + c) for i in range(scen) for j in range(planes) for c in range(2)
                 if (distance(i, j) == planes - 1) == far]
        return lax.ppermute(x, ("scen", "blk"), pairs)

    def flip_far(x):
        pairs = [(i * blk + 2 * j + c, i * blk + 2 * j + 1 - c) for i in range(scen) for j in range(planes) for c in range(2)
                 if distance(i, j) == planes - 1]
        return lax.ppermute(x, ("scen", "blk"), pairs)

    masks = tile_mask.reshape(leaves)
    total = base + width + 4 * leaves
    cut = base // 2 + width // 2
    call = functools.partial(pl.pallas_call, cost_estimate=NO_COST)
    struct = jax.ShapeDtypeStruct
    bundle = call(
        functools.partial(start_kernel, leaves, width),
        out_shape=struct((total, cols), BF16),
        in_specs=[SM, SM, SM, VM, VM, VM],
        out_specs=VM,
        scratch_shapes=[pltpu.VMEM((4 * leaves, cols), F32)],
    )(core1, masks, parent, link, leaf_inverse, leaf_rhs)

    bx, by = over_scen(bundle, 1), over_scen(bundle, 2)
    solved = call(
        functools.partial(solved_kernel, leaves, width),
        out_shape=struct((base, cols), BF16),
        in_specs=[VM, VM],
        out_specs=VM,
    )(bundle, leaf_inverse)
    up = {1: over_z(solved, 1, range(planes - 1))}
    down = {1: over_z(solved, -1, range(1, planes))}
    top, end = call(
        cut_kernel,
        out_shape=[struct((cut, cols), BF16), struct((total - cut, cols), BF16)],
        in_specs=[HB] * 4,
        out_specs=[VM, VM],
        scratch_shapes=[pltpu.SemaphoreType.DMA((2,))],
    )(bx, by, up[1], down[1])
    da, db = over_scen(top, 2), over_scen(end, 1)
    for step in range(2, planes - 1):
        up[step] = over_z(up[step - 1], 1, range(step - 1, planes - 1))
        down[step] = over_z(down[step - 1], -1, range(1, planes - step + 1))
    sources = [solved] + [up[i] for i in range(1, planes - 1)] + [down[i] for i in range(1, planes - 1)]

    tops = [bx[base:], by[base:], db[base - cut:]]
    swap = flip_core(jnp.concatenate([t[:width] for t in tops[:2]], axis=0))
    swap3 = flip_core(tops[2][:width])
    notes = [t[width:, :width].astype(F32) for t in tops]
    owners = [parent] + [n[3 * leaves:, 0].astype(jnp.int32) for n in notes]
    parents = jnp.concatenate(owners)
    sides = [leaf_rhs] + [n[:leaves] + n[leaves:2 * leaves] + n[2 * leaves:3 * leaves] for n in notes]
    rights, rights3 = jnp.concatenate(sides[:3], axis=0), jnp.concatenate(sides, axis=0)

    count = scen * leaves
    node_shape = struct((nodes, cols), F32)
    part_shape = struct((count, width), F32)
    early_shape, late_shape = struct((3 * base, cols), BF16), struct((base, cols), BF16)
    m_all, km_all, diag, right = call(
        functools.partial(early_kernel, leaves, width, nodes),
        out_shape=[early_shape, early_shape, struct((3 * nodes, cols), F32), struct((3 * nodes, cols), F32)],
        in_specs=[SM, SM] + [VM] * 6,
        out_specs=[VM] * 4,
        compiler_params=pltpu.CompilerParams(vmem_limit_bytes=56 * MIB),
    )(core1, jnp.concatenate(owners[:3]), rights, leaf_inverse, bundle, bx, by, swap)
    def place(column):
        away = z - column
        near = jnp.where(away >= 0, away, planes - 2 - away)
        return jnp.where(jnp.abs(away) == planes - 1, -1, near)

    edge = jnp.where(z == 1, 2 * (planes - 2), planes - 2)
    own_line, send1, send2, send3, onward, picked = pick(
        jnp.stack([place(s), place(s ^ 1), place(s ^ 2), place(s ^ 3), edge]).astype(jnp.int32), sources, [da, db, km_all])
    far0 = lax.ppermute(onward, "blk", [(2 * i + c, 2 * j + c) for i, j in ((1, 0), (planes - 2, planes - 1)) for c in range(2)])
    near = [own_line] + [in_plane(x, k + 1, False) for k, x in enumerate((send1, send2, send3))]
    far = [far0] + [in_plane(far0, k, True) for k in (1, 2, 3)]
    near_other = [flip_core(x) for x in near]
    far_other = [flip_far(x) for x in far]

    m3, km3, reduced, scaling, current, part = call(
        functools.partial(late_kernel, leaves, width, cut),
        out_shape=[late_shape, late_shape, node_shape, node_shape, node_shape, part_shape],
        in_specs=[SM, SM] + [VM] * 10,
        out_specs=[VM] * 6,
        compiler_params=pltpu.CompilerParams(vmem_limit_bytes=56 * MIB),
    )(core1, parents, rights3, node_rhs, node_diag, da, db, swap3, km_all, diag, right, picked)

    def exchange(x):
        x = x + flip_core(x)
        for step in range(planes.bit_length() - 2):
            x = x + flip_z(x, 1 << step)
        return x, flip_z(x, planes // 2)

    ties = [[far0, near[1]], near[2:3], near[3:] + near_other[:2], far[1:3] + near_other[2:3], far[3:] + near_other[3:]]
    for sweep in range(ITERS):
        last = sweep == ITERS - 1
        current, part = call(
            functools.partial(sweep_kernel, leaves, width, last, len(ties[sweep])),
            out_shape=[node_shape, struct((leaves, width), F32) if last else part_shape],
            in_specs=[SM] + [VM] * 10 + [HB] * len(ties[sweep]),
            out_specs=[VM] * 2,
            compiler_params=pltpu.CompilerParams(vmem_limit_bytes=24 * MIB),
        )(parents, *exchange(part), reduced, scaling, node_diag, current, m_all, km_all, m3, km3, *ties[sweep])
    leaf_solution = call(
        functools.partial(leaf_kernel, leaves),
        out_shape=struct((leaves, width), F32),
        in_specs=[VM] * 4 + [HB] * len(ties[ITERS]),
        out_specs=VM,
    )(*exchange(part), leaf_rhs, leaf_inverse, *ties[ITERS])

    schur = pl.pallas_call(
        functools.partial(product_kernel, leaves, width),
        out_shape=jax.ShapeDtypeStruct((nodes, cols, 2 * cols), F32),
        in_specs=[SM, SM] + [HB] * 18,
        out_specs=HB,
        scratch_shapes=[
            pltpu.VMEM((scen * base, cols), BF16),
            pltpu.VMEM((8, base, cols), BF16),
            pltpu.VMEM((2, nodes, cols, cols), F32),
            pltpu.SemaphoreType.DMA((10,)),
            pltpu.SemaphoreType.DMA((2,)),
        ],
        compiler_params=pltpu.CompilerParams(vmem_limit_bytes=56 * MIB),
        cost_estimate=NO_COST,
    )(jnp.stack([core, (jnp.abs(z - s) == planes - 1).astype(core.dtype)]).astype(jnp.int32), parents, m_all, m3,
      *near, *near_other, *far, *far_other)
    return current, leaf_solution, schur


def solution(mesh):
    scen, blk = mesh.shape["scen"], mesh.shape["blk"]
    in_specs = (
        P("scen", None, "blk"),
        P("scen", None, None),
        P("scen", None),
        P(None, "blk"),
        P(None, "blk"),
        P("scen"),
        P("scen", "blk"),
    )
    out_specs = (P(None, "blk"), P("scen", None), P(None, "blk", "scen"))
    body = functools.partial(plane_body, scen, blk) if scen == 4 and blk == 2 * scen else general_body
    return jax.shard_map(body, mesh=mesh, in_specs=in_specs, out_specs=out_specs, check_vma=False)
```

time: 384 us -> 227 us (0.59)
  blocking collectives: 141 us -> 0 us
  starting transfers between devices: 4.94 us -> 85.8 us
  local copies, waits for them, and re-layouts: 85.5 us -> 12.3 us
  Pallas kernels: 0 us -> 52.4 us
  waiting for transfers between devices: 108 us -> 67 us
  matrix products: 24.8 us -> 0 us
  between operations: 14.2 us -> 1.27 us
    psum x10 -> x0, blocking collectives: 141 us -> none  [the longest x4 59.2 us: body(): coupled = lax.psum(node_terms, 'scen')]
    ppermute x0 -> x40, starting transfers between devices: none -> 85.8 us  [the longest x10 51 us: flip_z(): return lax.ppermute(x, 'blk', [(i, i ^ 2 * k) for i in range(blk)])]
    all_gather x1 -> x0, waiting for transfers between devices: 84.3 us -> none  [body(): portion = lax.all_gather(solved, 'blk', axis=2, tiled=True)]
    ppermute x0 -> x40, waiting for transfers between devices: none -> 67 us  [the longest x4 26 us: over_z(): lax.ppermute(x, 'blk', [(2 * i + c, 2 * (i + step) + c) for i in sources...]
    dynamic_slice x2 -> x0, local copies, waits for them, and re-layouts: 63.3 us -> none  [body(): lax.dynamic_slice_in_dim(partial_value, blk_index * tile_width, tile_widt...]
    pallas_call x0 -> x12, Pallas kernels: none -> 52.4 us  [the longest x1 15 us: plane_body(): pl.pallas_call(functools.partial(product_kernel, leaves, width), out_shap...]
    dot_general x24 -> x0, matrix products: 24.8 us -> none  [the longest x1 14.5 us: body(): jnp.einsum('pkr,kc->prc', chosen, stacked, preferred_element_type=jnp.flo...]
    reduce_scatter x1 -> x0, waiting for transfers between devices: 24.1 us -> none  [body(): lax.psum_scatter(partial_value, 'scen', scatter_dimension=1, tiled=True)]
  transfers between devices with their start and end apart: 3 -> 40, of which waited for: 2 -> 16; matrix products, arithmetic and copies ran while one was open for 21% -> 4% of each run, Pallas kernels for 0% -> 15%
where the time goes in v1:
time: 227 us; the launch traced here: 224 us
  starting transfers between devices  85.8 us (38%)
  waiting for transfers between devices  67 us (30%)
  Pallas kernels  52.4 us (23%)
  local copies, waits for them, and re-layouts  12.3 us (5%)
  other arithmetic  5.64 us (2%)
    ppermute x10, starting transfers between devices, flip_z(): return lax.ppermute(x, 'blk', [(i, i ^ 2 * k) for i in range(blk)])  51 us
    ppermute x4, waiting for transfers between devices, over_z(): lax.ppermute(x, 'blk', [(2 * i + c, 2 * (i + step) + c) for i in sources...  26 us
    ppermute x10, waiting for transfers between devices, flip_z(): return lax.ppermute(x, 'blk', [(i, i ^ 2 * k) for i in range(blk)])  21.4 us
    pallas_call x1, Pallas kernels, plane_body(): pl.pallas_call(functools.partial(product_kernel, leaves, width), out_shap...  15 us
    ppermute x6, waiting for transfers between devices, in_plane(): return lax.ppermute(x, ('scen', 'blk'), pairs)  14.4 us
    ppermute x6, starting transfers between devices, in_plane(): return lax.ppermute(x, ('scen', 'blk'), pairs)  12.6 us
    unnamed x52, local copies, waits for them, and re-layouts  9.75 us
    pallas_call x4, Pallas kernels, plane_body(): call(functools.partial(sweep_kernel, leaves, width, last, len(ties[sweep]...  8.98 us
  transfers between devices with their start and end apart: 40, of which 16 were waited for; matrix products, arithmetic and copies ran while one was open for 4% of the time, Pallas kernels for 15%

profile of v1, /device:TPU:0, one launch (start us, length us, event | category | flops | bytes accessed | tf_op | source)
XLA Modules:
  0.0 224.3 jit_solution(17333786457051757234)
XLA Ops:
  0.6 2.8 %shard_map.94.bundle_ref.own_ref = bf16[1296,512]{1,0:T(8,128)(2,1)} custom-call(s32[1]{0:T(128)} %bitcast.core_ref, s32[4]{0:T(128)} %bitcast.8, s32[4]{0:T(128)} %parent_ref.1, bf16[4,256,512]{2,1,0:T(8,128)(2,1)} %link_ref.1, bf16[4,256,256]{2,1,0:T(8,128)(2,1)} %inverse_ref.7, f32[4,256]{1,0:T(4,128)} %rhs_ref.3), custom_call_target="tpu_custom_call" | custom-call | tf_op jit(solution)/shard_map/pallas_call | solution.py:372
  3.5 2.9 %collective-permute-start = (bf16[1296,512]{1,0:T(8,128)(2,1)}, bf16[1296,512]{1,0:T(8,128)(2,1)S(1)}, u32[]{:S(2)}, u32[]{:S(2)}) collective-permute-start(bf16[1296,512]{1,0:T(8,128)(2,1)} %shard_map.94.bundle_ref.own_ref), channel_id=1, source_target_pairs={{0,8},{8,0},{16,24},{24,16},{1,9},{9,1},{17,25},{25,17},{2,10},{10... | collective-permute-start | bytes 3981320 | tf_op jit(solution)/shard_map/ppermute | solution.py:343
  7.9 2.9 %shard_map.95.refs_0_ = bf16[1024,512]{1,0:T(8,128)(2,1)} custom-call(bf16[1296,512]{1,0:T(8,128)(2,1)} %shard_map.94.bundle_ref.own_ref, bf16[4,256,256]{2,1,0:T(8,128)(2,1)} %inverse_ref.7), custom_call_target="tpu_custom_call" | custom-call | tf_op jit(solution)/shard_map/pallas_call | solution.py:381
  10.8 4.5 %collective-permute-start.2 = (bf16[1024,512]{1,0:T(8,128)(2,1)}, bf16[1024,512]{1,0:T(8,128)(2,1)}, u32[]{:S(2)}, u32[]{:S(2)}) collective-permute-start(bf16[1024,512]{1,0:T(8,128)(2,1)} %shard_map.95.refs_0_), channel_id=1, source_target_pairs={{0,2},{1,3},{2,4},{3,5},{4,6},{5,7},{8,10},{9,11},{10,12},{11,13},... | collective-permute-start | bytes 3145736 | tf_op jit(solution)/shard_map/ppermute | solution.py:346
  17.3 19.2 %collective-permute-done.2.refs_0_.refs_1_ = bf16[1024,512]{1,0:T(8,128)(2,1)} collective-permute-done((bf16[1024,512]{1,0:T(8,128)(2,1)}, bf16[1024,512]{1,0:T(8,128)(2,1)}, u32[]{:S(2)}, u32[]{:S(2)}) %collective-permute-start.2) | collective-permute-done | bytes 1048608 | tf_op jit(solution)/shard_map/ppermute | solution.py:346
  38.1 3.5 %collective-permute-done.3.refs_1_.refs_3_ = bf16[1024,512]{1,0:T(8,128)(2,1)} collective-permute-done((bf16[1024,512]{1,0:T(8,128)(2,1)}, bf16[1024,512]{1,0:T(8,128)(2,1)}, u32[]{:S(2)}, u32[]{:S(2)}) %collective-permute-start.3) | collective-permute-done | bytes 1048608 | tf_op jit(solution)/shard_map/ppermute | solution.py:346
  45.0 2.4 %shard_map.96 = (bf16[640,512]{1,0:T(8,128)(2,1)}, bf16[656,512]{1,0:T(8,128)(2,1)}) custom-call(bf16[1296,512]{1,0:T(8,128)(2,1)} %copy-done.13, bf16[1296,512]{1,0:T(8,128)(2,1)} %copy-done.14, bf16[1024,512]{1,0:T(8,128)(2,1)} %collective-permute-done.2.refs_0_.refs_1_, bf16[1024,512]{1,0:T(8,128)(2,1)} %collective-permute-done.3.refs_1_.refs_3_), custom_call_target="tpu_custom_call" | custom-call | tf_op jit(solution)/shard_map/pallas_call | solution.py:389
  54.3 8.0 %shard_map.97 = (bf16[3072,512]{1,0:T(8,128)(2,1)}, bf16[3072,512]{1,0:T(8,128)(2,1)}, f32[6,512]{1,0:T(8,128)}, f32[6,512]{1,0:T(8,128)}) custom-call(s32[1]{0:T(128)} %bitcast.core_ref, s32[12]{0:T(128)} %pad_add_fusion.1.parent_ref, f32[12,256]{1,0:T(8,128)} %pad_maximum_fusion.2.rhs_ref, bf16[4,256,256]{2,1,0:T(8,128)(2,1)} %inverse_ref.7, ...), custom_call_target="tpu_custom_call" | custom-call | tf_op jit(solution)/shard_map/pallas_call | solution.py:415
  63.6 3.4 %collective-permute-done.9.refs_4_ = bf16[1024,512]{1,0:T(8,128)(2,1)} collective-permute-done((bf16[1024,512]{1,0:T(8,128)(2,1)}, bf16[1024,512]{1,0:T(8,128)(2,1)}, u32[]{:S(2)}, u32[]{:S(2)}) %collective-permute-start.9) | collective-permute-done | bytes 1048608 | tf_op jit(solution)/shard_map/ppermute | solution.py:346
  67.0 4.8 %shard_map.98 = (bf16[1024,512]{1,0:T(8,128)(2,1)}, bf16[1024,512]{1,0:T(8,128)(2,1)}, bf16[1024,512]{1,0:T(8,128)(2,1)}, bf16[1024,512]{1,0:T(8,128)(2,1)}, bf1...) custom-call(s32[5]{0:T(128)} %stack.33.place_ref, bf16[1024,512]{1,0:T(8,128)(2,1)} %shard_map.95.refs_0_, ...), custom_call_target="tpu_custom_call" | custom-call | tf_op jit(solution)/shard_map/pallas_call | solution.py:282
  73.1 2.5 %collective-permute-start.14 = (bf16[1024,512]{1,0:T(8,128)(2,1)}, bf16[1024,512]{1,0:T(8,128)(2,1)}, u32[]{:S(2)}, u32[]{:S(2)}) collective-permute-start(bf16[1024,512]{1,0:T(8,128)(2,1)} %get-tuple-element.43), channel_id=1, source_target_pairs={{8,0},{9,1},{10,2},{11,3},{12,4},{13,5},{0,8},{1,9},{2,10},{3,11},... | collective-permute-start | bytes 3145736 | tf_op jit(solution)/shard_map/ppermute | solution.py:360
  77.0 5.5 %shard_map.99 = (bf16[1024,512]{1,0:T(8,128)(2,1)}, bf16[1024,512]{1,0:T(8,128)(2,1)}, f32[2,512]{1,0:T(2,128)}, f32[2,512]{1,0:T(2,128)}, f32[2,512]{1,0:T(2,128)}, /*index=5*/f32[16,256]{1,0:T(8,128)}) custom-call(s32[1]{0:T(128)} %bitcast.core_ref, s32[16]{0:T(128)} %pad_add_fusion.parent_ref, f32[16,256]{1,0:T(8,128)} %pad_maximum_fusion.1.rhs_ref, ...), custom_call_target="tpu_custom_call" | custom-call | tf_op jit(solution)/shard_map/pallas_call | solution.py:436
  82.5 1.9 collective-permute-start.18
  85.2 4.6 %collective-permute-start.11 = (f32[16,256]{1,0:T(8,128)S(1)}, f32[16,256]{1,0:T(8,128)S(1)}, u32[]{:S(2)}, u32[]{:S(2)}) collective-permute-start(f32[16,256]{1,0:T(8,128)S(1)} %add.60), channel_id=1, source_target_pairs={{0,2},{1,3},{2,0},{3,1},{4,6},{5,7},{6,4},{7,5},{8,10},{9,11},{10,... | collective-permute-start | bytes 49160 | tf_op jit(solution)/shard_map/ppermute | solution.py:349
  89.8 8.7 %collective-permute-done.11 = f32[16,256]{1,0:T(8,128)S(1)} collective-permute-done((f32[16,256]{1,0:T(8,128)S(1)}, f32[16,256]{1,0:T(8,128)S(1)}, u32[]{:S(2)}, u32[]{:S(2)}) %collective-permute-start.11) | collective-permute-done | bytes 16416 | tf_op jit(solution)/shard_map/ppermute | solution.py:349
  108.3 2.4 %shard_map.100 = (f32[2,512]{1,0:T(2,128)S(1)}, f32[16,256]{1,0:T(8,128)S(1)}) custom-call(s32[16]{0:T(128)S(1)} %copy-done.11, f32[16,256]{1,0:T(8,128)S(1)} %add.61.y_ref, f32[16,256]{1,0:T(8,128)S(1)} %collective-permute-done.12.z_ref, f32[2,512]{1,0:T(2,128)S(1)} %copy-done.9, f32[2,512]{1,0:T(2,128)S(1)} %copy-done.10, f32[2,512]{1,0:T(2,128)S(1)} %copy-done.8, ...), custom_call_target="tpu_custom_call" | custom-call | tf_op jit(solution)/shard_map/pallas_call | solution.py:453
  111.9 3.7 %collective-permute-start.16 = (f32[16,256]{1,0:T(8,128)S(1)}, f32[16,256]{1,0:T(8,128)S(1)}, u32[]{:S(2)}, u32[]{:S(2)}) collective-permute-start(f32[16,256]{1,0:T(8,128)S(1)} %add.62), channel_id=1, source_target_pairs={{0,2},{1,3},{2,0},{3,1},{4,6},{5,7},{6,4},{7,5},{8,10},{9,11},{10,... | collective-permute-start | bytes 49160 | tf_op jit(solution)/shard_map/ppermute | solution.py:349
  115.6 1.7 collective-permute-done.16
  118.3 14.4 %collective-permute-done.18.refs_0_.refs_2_ = bf16[1024,512]{1,0:T(8,128)(2,1)S(1)} collective-permute-done((bf16[1024,512]{1,0:T(8,128)(2,1)}, bf16[1024,512]{1,0:T(8,128)(2,1)S(1)}, u32[]{:S(2)}, u32[]{:S(2)}) %collective-permute-start.18) | collective-permute-done | bytes 1048608 | tf_op jit(solution)/shard_map/ppermute | solution.py:360
  132.6 2.4 %shard_map.101 = (f32[2,512]{1,0:T(2,128)S(1)}, f32[16,256]{1,0:T(8,128)S(1)}) custom-call(s32[16]{0:T(128)S(1)} %copy-done.11, f32[16,256]{1,0:T(8,128)S(1)} %add.63.y_ref, f32[16,256]{1,0:T(8,128)S(1)} %collective-permute-done.17.z_ref, f32[2,512]{1,0:T(2,128)S(1)} %copy-done.9, f32[2,512]{1,0:T(2,128)S(1)} %copy-done.10, f32[2,512]{1,0:T(2,128)S(1)} %copy-done.8, ...), custom_call_target="tpu_custom_call" | custom-call | tf_op jit(solution)/shard_map/pallas_call | solution.py:453
  136.3 3.8 %collective-permute-start.20 = (f32[16,256]{1,0:T(8,128)S(1)}, f32[16,256]{1,0:T(8,128)S(1)}, u32[]{:S(2)}, u32[]{:S(2)}) collective-permute-start(f32[16,256]{1,0:T(8,128)S(1)} %add.64), channel_id=1, source_target_pairs={{0,2},{1,3},{2,0},{3,1},{4,6},{5,7},{6,4},{7,5},{8,10},{9,11},{10,... | collective-permute-start | bytes 49160 | tf_op jit(solution)/shard_map/ppermute | solution.py:349
  141.8 3.6 %collective-permute-start.21 = (f32[16,256]{1,0:T(8,128)S(1)}, f32[16,256]{1,0:T(8,128)S(1)}, u32[]{:S(2)}, u32[]{:S(2)}) collective-permute-start(f32[16,256]{1,0:T(8,128)S(1)} %add.65.y_ref), channel_id=1, source_target_pairs={{0,4},{1,5},{2,6},{3,7},{4,0},{5,1},{6,2},{7,3},{8,12},{9,13},{10,... | collective-permute-start | bytes 49160 | tf_op jit(solution)/shard_map/ppermute | solution.py:349
  145.4 1.7 collective-permute-start.29
  147.2 3.6 %collective-permute-start.34 = (bf16[1024,512]{1,0:T(8,128)(2,1)}, bf16[1024,512]{1,0:T(8,128)(2,1)S(1)}, u32[]{:S(2)}, u32[]{:S(2)}) collective-permute-start(bf16[1024,512]{1,0:T(8,128)(2,1)} %collective-permute-done.13.refs_0_.refs_8_), channel_id=1, source_target_pairs={{30,6},{31,7},{0,24},{1,25}} | collective-permute-start | bytes 3145736 | tf_op jit(solution)/shard_map/ppermute | solution.py:360
  150.8 2.4 %shard_map.102 = (f32[2,512]{1,0:T(2,128)S(1)}, f32[16,256]{1,0:T(8,128)S(1)}) custom-call(s32[16]{0:T(128)S(1)} %copy-done.11, f32[16,256]{1,0:T(8,128)S(1)} %add.65.y_ref, f32[16,256]{1,0:T(8,128)S(1)} %collective-permute-done.21.z_ref, f32[2,512]{1,0:T(2,128)S(1)} %copy-done.9, f32[2,512]{1,0:T(2,128)S(1)} %copy-done.10, f32[2,512]{1,0:T(2,128)S(1)} %copy-done.8, ...), custom_call_target="tpu_custom_call" | custom-call | tf_op jit(solution)/shard_map/pallas_call | solution.py:453
  154.5 3.7 %collective-permute-done.26 = f32[16,256]{1,0:T(8,128)S(1)} collective-permute-done((f32[16,256]{1,0:T(8,128)S(1)}, f32[16,256]{1,0:T(8,128)S(1)}, u32[]{:S(2)}, u32[]{:S(2)}) %collective-permute-start.26) | collective-permute-done | bytes 16416 | tf_op jit(solution)/shard_map/ppermute | solution.py:349
  158.5 4.4 %collective-permute-done.27.z_ref = f32[16,256]{1,0:T(8,128)S(1)} collective-permute-done((f32[16,256]{1,0:T(8,128)S(1)}, f32[16,256]{1,0:T(8,128)S(1)}, u32[]{:S(2)}, u32[]{:S(2)}) %collective-permute-start.27) | collective-permute-done | bytes 16416 | tf_op jit(solution)/shard_map/ppermute | solution.py:349
  162.9 1.8 shard_map.103
  165.9 9.6 %collective-permute-start.32 = (f32[4,256]{1,0:T(4,128)S(1)}, f32[4,256]{1,0:T(4,128)S(1)}, u32[]{:S(2)}, u32[]{:S(2)}) collective-permute-start(f32[4,256]{1,0:T(4,128)S(1)} %add.68), channel_id=1, source_target_pairs={{0,2},{1,3},{2,0},{3,1},{4,6},{5,7},{6,4},{7,5},{8,10},{9,11},{10,... | collective-permute-start | bytes 12296 | tf_op jit(solution)/shard_map/ppermute | solution.py:349
  181.3 22.8 %collective-permute-start.33 = (f32[4,256]{1,0:T(4,128)S(1)}, f32[4,256]{1,0:T(4,128)S(1)}, u32[]{:S(2)}, u32[]{:S(2)}) collective-permute-start(f32[4,256]{1,0:T(4,128)S(1)} %add.69.y_ref), channel_id=1, source_target_pairs={{0,4},{1,5},{2,6},{3,7},{4,0},{5,1},{6,2},{7,3},{8,12},{9,13},{10,... | collective-permute-start | bytes 12296 | tf_op jit(solution)/shard_map/ppermute | solution.py:349
  206.2 1.9 shard_map.104
  209.1 15.0 %shard_map.105 = f32[2,512,1024]{2,1,0:T(8,128)} custom-call(s32[2]{0:T(128)} %pad_add_fusion.2.info_ref, s32[16]{0:T(128)} %pad_add_fusion.parent_ref, bf16[3072,512]{1,0:T(8,128)(2,1)} %get-tuple-element.39.m_ref.m_hbm, bf16[1024,512]{1,0:T(8,128)(2,1)} %get-tuple-element.40.m3_ref.m3_hbm, bf16[1024,512]{1,0:T(8,128)(2,1)} %get-tuple-element.50.refs_0_, ...), custom_call_target="tpu_custom_call" | custom-call | tf_op jit(solution)/shard_map/pallas_call | solution.py:467
  (141 shorter events, 46.4 us)
Async XLA Ops:
  3.5 39.4 %collective-permute-start = (bf16[1296,512]{1,0:T(8,128)(2,1)}, bf16[1296,512]{1,0:T(8,128)(2,1)S(1)}, u32[]{:S(2)}, u32[]{:S(2)}) collective-permute-start(bf16[1296,512]{1,0:T(8,128)(2,1)} %shard_map.94.bundle_ref.own_ref), channel_id=1, source_target_pairs={{0,8},{8,0},{16,24},{24,16},{1,9},{9,1},{17,25},{25,17},{2,10},{10... | collective-permute-start | bytes 3981320 | tf_op jit(solution)/shard_map/ppermute | solution.py:343
  6.4 36.5 %collective-permute-start.1 = (bf16[1296,512]{1,0:T(8,128)(2,1)}, bf16[1296,512]{1,0:T(8,128)(2,1)S(1)}, u32[]{:S(2)}, u32[]{:S(2)}) collective-permute-start(bf16[1296,512]{1,0:T(8,128)(2,1)} %shard_map.94.bundle_ref.own_ref), channel_id=1, source_target_pairs={{0,16},{8,24},{16,0},{24,8},{1,17},{9,25},{17,1},{25,9},{2,18},{10... | collective-permute-start | bytes 3981320 | tf_op jit(solution)/shard_map/ppermute | solution.py:343
  10.8 25.6 %collective-permute-start.2 = (bf16[1024,512]{1,0:T(8,128)(2,1)}, bf16[1024,512]{1,0:T(8,128)(2,1)}, u32[]{:S(2)}, u32[]{:S(2)}) collective-permute-start(bf16[1024,512]{1,0:T(8,128)(2,1)} %shard_map.95.refs_0_), channel_id=1, source_target_pairs={{0,2},{1,3},{2,4},{3,5},{4,6},{5,7},{8,10},{9,11},{10,12},{11,13},... | collective-permute-start | bytes 3145736 | tf_op jit(solution)/shard_map/ppermute | solution.py:346
  15.3 26.3 %collective-permute-start.3 = (bf16[1024,512]{1,0:T(8,128)(2,1)}, bf16[1024,512]{1,0:T(8,128)(2,1)}, u32[]{:S(2)}, u32[]{:S(2)}) collective-permute-start(bf16[1024,512]{1,0:T(8,128)(2,1)} %shard_map.95.refs_0_), channel_id=1, source_target_pairs={{2,0},{3,1},{4,2},{5,3},{6,4},{7,5},{10,8},{11,9},{12,10},{13,11},... | collective-permute-start | bytes 3145736 | tf_op jit(solution)/shard_map/ppermute | solution.py:346
  36.5 27.2 %collective-permute-start.8 = (bf16[1024,512]{1,0:T(8,128)(2,1)}, bf16[1024,512]{1,0:T(8,128)(2,1)}, u32[]{:S(2)}, u32[]{:S(2)}) collective-permute-start(bf16[1024,512]{1,0:T(8,128)(2,1)} %collective-permute-done.2.refs_0_.refs_1_), channel_id=1, source_target_pairs={{2,4},{3,5},{4,6},{5,7},{10,12},{11,13},{12,14},{13,15},{18,20},{1... | collective-permute-start | bytes 3145736 | tf_op jit(solution)/shard_map/ppermute | solution.py:346
  41.6 25.4 %collective-permute-start.9 = (bf16[1024,512]{1,0:T(8,128)(2,1)}, bf16[1024,512]{1,0:T(8,128)(2,1)}, u32[]{:S(2)}, u32[]{:S(2)}) collective-permute-start(bf16[1024,512]{1,0:T(8,128)(2,1)} %collective-permute-done.3.refs_1_.refs_3_), channel_id=1, source_target_pairs={{2,0},{3,1},{4,2},{5,3},{10,8},{11,9},{12,10},{13,11},{18,16},{19,... | collective-permute-start | bytes 3145736 | tf_op jit(solution)/shard_map/ppermute | solution.py:346
  47.4 15.3 %collective-permute-start.4 = (bf16[656,512]{1,0:T(8,128)(2,1)}, bf16[656,512]{1,0:T(8,128)(2,1)S(1)}, u32[]{:S(2)}, u32[]{:S(2)}) collective-permute-start(bf16[656,512]{1,0:T(8,128)(2,1)} %get-tuple-element.29), channel_id=1, source_target_pairs={{0,8},{8,0},{16,24},{24,16},{1,9},{9,1},{17,25},{25,17},{2,10},{10... | collective-permute-start | bytes 2015240 | tf_op jit(solution)/shard_map/ppermute | solution.py:343
  48.7 14.9 %collective-permute-start.5 = (bf16[640,512]{1,0:T(8,128)(2,1)}, bf16[640,512]{1,0:T(8,128)(2,1)S(1)}, u32[]{:S(2)}, u32[]{:S(2)}) collective-permute-start(bf16[640,512]{1,0:T(8,128)(2,1)} %get-tuple-element.30), channel_id=1, source_target_pairs={{0,16},{8,24},{16,0},{24,8},{1,17},{9,25},{17,1},{25,9},{2,18},{10... | collective-permute-start | bytes 1966088 | tf_op jit(solution)/shard_map/ppermute | solution.py:343
  62.8 13.5 %collective-permute-start.6 = (bf16[256,512]{1,0:T(8,128)(2,1)S(1)}, bf16[256,512]{1,0:T(8,128)(2,1)S(1)}, u32[]{:S(2)}, u32[]{:S(2)}) collective-permute-start(bf16[256,512]{1,0:T(8,128)(2,1)S(1)} %slice.96), channel_id=1, source_target_pairs={{0,1},{1,0},{2,3},{3,2},{4,5},{5,4},{6,7},{7,6},{8,9},{9,8},{10,11... | collective-permute-start | bytes 786440 | tf_op jit(solution)/shard_map/ppermute | solution.py:352
  71.8 31.9 %collective-permute-start.13 = (bf16[1024,512]{1,0:T(8,128)(2,1)}, bf16[1024,512]{1,0:T(8,128)(2,1)}, u32[]{:S(2)}, u32[]{:S(2)}) collective-permute-start(bf16[1024,512]{1,0:T(8,128)(2,1)} %get-tuple-element.42), channel_id=1, source_target_pairs={{2,0},{3,1},{4,6},{5,7},{10,8},{11,9},{12,14},{13,15},{18,16},{19,... | collective-permute-start | bytes 3145736 | tf_op jit(solution)/shard_map/ppermute | solution.py:430
  73.1 30.1 %collective-permute-start.14 = (bf16[1024,512]{1,0:T(8,128)(2,1)}, bf16[1024,512]{1,0:T(8,128)(2,1)}, u32[]{:S(2)}, u32[]{:S(2)}) collective-permute-start(bf16[1024,512]{1,0:T(8,128)(2,1)} %get-tuple-element.43), channel_id=1, source_target_pairs={{8,0},{9,1},{10,2},{11,3},{12,4},{13,5},{0,8},{1,9},{2,10},{3,11},... | collective-permute-start | bytes 3145736 | tf_op jit(solution)/shard_map/ppermute | solution.py:360
  82.5 50.1 %collective-permute-start.18 = (bf16[1024,512]{1,0:T(8,128)(2,1)}, bf16[1024,512]{1,0:T(8,128)(2,1)S(1)}, u32[]{:S(2)}, u32[]{:S(2)}) collective-permute-start(bf16[1024,512]{1,0:T(8,128)(2,1)} %get-tuple-element.46), channel_id=1, source_target_pairs={{16,0},{17,1},{18,2},{19,3},{20,4},{21,5},{24,8},{25,9},{26,10},{2... | collective-permute-start | bytes 3145736 | tf_op jit(solution)/shard_map/ppermute | solution.py:360
  85.2 13.4 %collective-permute-start.11 = (f32[16,256]{1,0:T(8,128)S(1)}, f32[16,256]{1,0:T(8,128)S(1)}, u32[]{:S(2)}, u32[]{:S(2)}) collective-permute-start(f32[16,256]{1,0:T(8,128)S(1)} %add.60), channel_id=1, source_target_pairs={{0,2},{1,3},{2,0},{3,1},{4,6},{5,7},{6,4},{7,5},{8,10},{9,11},{10,... | collective-permute-start | bytes 49160 | tf_op jit(solution)/shard_map/ppermute | solution.py:349
  100.2 45.2 %collective-permute-start.22 = (bf16[1024,512]{1,0:T(8,128)(2,1)}, bf16[1024,512]{1,0:T(8,128)(2,1)}, u32[]{:S(2)}, u32[]{:S(2)}) collective-permute-start(bf16[1024,512]{1,0:T(8,128)(2,1)} %get-tuple-element.49), channel_id=1, source_target_pairs={{24,0},{25,1},{26,2},{27,3},{28,4},{29,5},{16,8},{17,9},{18,10},{1... | collective-permute-start | bytes 3145736 | tf_op jit(solution)/shard_map/ppermute | solution.py:360
  103.2 43.9 %collective-permute-start.23 = (bf16[1024,512]{1,0:T(8,128)(2,1)S(1)}, bf16[1024,512]{1,0:T(8,128)(2,1)S(1)}, u32[]{:S(2)}, u32[]{:S(2)}) collective-permute-start(bf16[1024,512]{1,0:T(8,128)(2,1)S(1)} %copy-done.18), channel_id=1, source_target_pairs={{0,1},{1,0},{2,3},{3,2},{4,5},{5,4},{6,7},{7,6},{8,9},{9,8},{10,11... | collective-permute-start | bytes 3145736 | tf_op jit(solution)/shard_map/ppermute | solution.py:352
  103.2 47.6 %collective-permute-start.24 = (bf16[1024,512]{1,0:T(8,128)(2,1)}, bf16[1024,512]{1,0:T(8,128)(2,1)S(1)}, u32[]{:S(2)}, u32[]{:S(2)}) collective-permute-start(bf16[1024,512]{1,0:T(8,128)(2,1)} %collective-permute-done.14.refs_1_), channel_id=1, source_target_pairs={{0,1},{1,0},{2,3},{3,2},{4,5},{5,4},{6,7},{7,6},{8,9},{9,8},{10,11... | collective-permute-start | bytes 3145736 | tf_op jit(solution)/shard_map/ppermute | solution.py:352
  111.9 5.4 %collective-permute-start.16 = (f32[16,256]{1,0:T(8,128)S(1)}, f32[16,256]{1,0:T(8,128)S(1)}, u32[]{:S(2)}, u32[]{:S(2)}) collective-permute-start(f32[16,256]{1,0:T(8,128)S(1)} %add.62), channel_id=1, source_target_pairs={{0,2},{1,3},{2,0},{3,1},{4,6},{5,7},{6,4},{7,5},{8,10},{9,11},{10,... | collective-permute-start | bytes 49160 | tf_op jit(solution)/shard_map/ppermute | solution.py:349
  117.4 15.3 %collective-permute-start.17 = (f32[16,256]{1,0:T(8,128)S(1)}, f32[16,256]{1,0:T(8,128)S(1)}, u32[]{:S(2)}, u32[]{:S(2)}) collective-permute-start(f32[16,256]{1,0:T(8,128)S(1)} %add.63.y_ref), channel_id=1, source_target_pairs={{0,4},{1,5},{2,6},{3,7},{4,0},{5,1},{6,2},{7,3},{8,12},{9,13},{10,... | collective-permute-start | bytes 49160 | tf_op jit(solution)/shard_map/ppermute | solution.py:349
  136.3 5.5 %collective-permute-start.20 = (f32[16,256]{1,0:T(8,128)S(1)}, f32[16,256]{1,0:T(8,128)S(1)}, u32[]{:S(2)}, u32[]{:S(2)}) collective-permute-start(f32[16,256]{1,0:T(8,128)S(1)} %add.64), channel_id=1, source_target_pairs={{0,2},{1,3},{2,0},{3,1},{4,6},{5,7},{6,4},{7,5},{8,10},{9,11},{10,... | collective-permute-start | bytes 49160 | tf_op jit(solution)/shard_map/ppermute | solution.py:349
  140.1 18.1 %collective-permute-start.28 = (bf16[1024,512]{1,0:T(8,128)(2,1)}, bf16[1024,512]{1,0:T(8,128)(2,1)}, u32[]{:S(2)}, u32[]{:S(2)}) collective-permute-start(bf16[1024,512]{1,0:T(8,128)(2,1)} %collective-permute-done.13.refs_0_.refs_8_), channel_id=1, source_target_pairs={{14,6},{15,7},{16,24},{17,25}} | collective-permute-start | bytes 3145736 | tf_op jit(solution)/shard_map/ppermute | solution.py:360
  141.8 5.3 %collective-permute-start.21 = (f32[16,256]{1,0:T(8,128)S(1)}, f32[16,256]{1,0:T(8,128)S(1)}, u32[]{:S(2)}, u32[]{:S(2)}) collective-permute-start(f32[16,256]{1,0:T(8,128)S(1)} %add.65.y_ref), channel_id=1, source_target_pairs={{0,4},{1,5},{2,6},{3,7},{4,0},{5,1},{6,2},{7,3},{8,12},{9,13},{10,... | collective-permute-start | bytes 49160 | tf_op jit(solution)/shard_map/ppermute | solution.py:349
  145.4 13.1 %collective-permute-start.29 = (bf16[1024,512]{1,0:T(8,128)(2,1)}, bf16[1024,512]{1,0:T(8,128)(2,1)}, u32[]{:S(2)}, u32[]{:S(2)}) collective-permute-start(bf16[1024,512]{1,0:T(8,128)(2,1)} %collective-permute-done.13.refs_0_.refs_8_), channel_id=1, source_target_pairs={{22,6},{23,7},{8,24},{9,25}} | collective-permute-start | bytes 3145736 | tf_op jit(solution)/shard_map/ppermute | solution.py:360
  147.1 11.3 %collective-permute-start.30 = (bf16[1024,512]{1,0:T(8,128)(2,1)S(1)}, bf16[1024,512]{1,0:T(8,128)(2,1)S(1)}, u32[]{:S(2)}, u32[]{:S(2)}) collective-permute-start(bf16[1024,512]{1,0:T(8,128)(2,1)S(1)} %collective-permute-done.18.refs_0_.refs_2_), channel_id=1, source_target_pairs={{0,1},{1,0},{2,3},{3,2},{4,5},{5,4},{6,7},{7,6},{8,9},{9,8},{10,11... | collective-permute-start | bytes 3145736 | tf_op jit(solution)/shard_map/ppermute | solution.py:352
  147.2 30.8 %collective-permute-start.34 = (bf16[1024,512]{1,0:T(8,128)(2,1)}, bf16[1024,512]{1,0:T(8,128)(2,1)S(1)}, u32[]{:S(2)}, u32[]{:S(2)}) collective-permute-start(bf16[1024,512]{1,0:T(8,128)(2,1)} %collective-permute-done.13.refs_0_.refs_8_), channel_id=1, source_target_pairs={{30,6},{31,7},{0,24},{1,25}} | collective-permute-start | bytes 3145736 | tf_op jit(solution)/shard_map/ppermute | solution.py:360
  158.2 23.1 %collective-permute-start.35 = (bf16[1024,512]{1,0:T(8,128)(2,1)}, bf16[1024,512]{1,0:T(8,128)(2,1)}, u32[]{:S(2)}, u32[]{:S(2)}) collective-permute-start(bf16[1024,512]{1,0:T(8,128)(2,1)} %collective-permute-done.22.refs_0_.refs_3_), channel_id=1, source_target_pairs={{0,1},{1,0},{2,3},{3,2},{4,5},{5,4},{6,7},{7,6},{8,9},{9,8},{10,11... | collective-permute-start | bytes 3145736 | tf_op jit(solution)/shard_map/ppermute | solution.py:352
  158.2 4.7 %collective-permute-start.27 = (f32[16,256]{1,0:T(8,128)S(1)}, f32[16,256]{1,0:T(8,128)S(1)}, u32[]{:S(2)}, u32[]{:S(2)}) collective-permute-start(f32[16,256]{1,0:T(8,128)S(1)} %add.67.y_ref), channel_id=1, source_target_pairs={{0,4},{1,5},{2,6},{3,7},{4,0},{5,1},{6,2},{7,3},{8,12},{9,13},{10,... | collective-permute-start | bytes 49160 | tf_op jit(solution)/shard_map/ppermute | solution.py:349
  165.9 13.7 %collective-permute-start.32 = (f32[4,256]{1,0:T(4,128)S(1)}, f32[4,256]{1,0:T(4,128)S(1)}, u32[]{:S(2)}, u32[]{:S(2)}) collective-permute-start(f32[4,256]{1,0:T(4,128)S(1)} %add.68), channel_id=1, source_target_pairs={{0,2},{1,3},{2,0},{3,1},{4,6},{5,7},{6,4},{7,5},{8,10},{9,11},{10,... | collective-permute-start | bytes 12296 | tf_op jit(solution)/shard_map/ppermute | solution.py:349
  175.5 32.6 %collective-permute-start.36 = (bf16[1024,512]{1,0:T(8,128)(2,1)}, bf16[1024,512]{1,0:T(8,128)(2,1)S(1)}, u32[]{:S(2)}, u32[]{:S(2)}) collective-permute-start(bf16[1024,512]{1,0:T(8,128)(2,1)} %collective-permute-done.13.refs_0_.refs_8_), channel_id=1, source_target_pairs={{6,7},{7,6},{24,25},{25,24}} | collective-permute-start | bytes 3145736 | tf_op jit(solution)/shard_map/ppermute | solution.py:365
  176.3 31.9 %collective-permute-start.37 = (bf16[1024,512]{1,0:T(8,128)(2,1)}, bf16[1024,512]{1,0:T(8,128)(2,1)}, u32[]{:S(2)}, u32[]{:S(2)}) collective-permute-start(bf16[1024,512]{1,0:T(8,128)(2,1)} %collective-permute-done.28.refs_0_.refs_9_), channel_id=1, source_target_pairs={{6,7},{7,6},{24,25},{25,24}} | collective-permute-start | bytes 3145736 | tf_op jit(solution)/shard_map/ppermute | solution.py:365
  178.0 30.2 %collective-permute-start.38 = (bf16[1024,512]{1,0:T(8,128)(2,1)}, bf16[1024,512]{1,0:T(8,128)(2,1)}, u32[]{:S(2)}, u32[]{:S(2)}) collective-permute-start(bf16[1024,512]{1,0:T(8,128)(2,1)} %collective-permute-done.29.refs_1_.refs_10_), channel_id=1, source_target_pairs={{6,7},{7,6},{24,25},{25,24}} | collective-permute-start | bytes 3145736 | tf_op jit(solution)/shard_map/ppermute | solution.py:365
  179.6 28.5 %collective-permute-start.39 = (bf16[1024,512]{1,0:T(8,128)(2,1)S(1)}, bf16[1024,512]{1,0:T(8,128)(2,1)}, u32[]{:S(2)}, u32[]{:S(2)}) collective-permute-start(bf16[1024,512]{1,0:T(8,128)(2,1)S(1)} %collective-permute-done.34.refs_0_.refs_11_), channel_id=1, source_target_pairs={{6,7},{7,6},{24,25},{25,24}} | collective-permute-start | bytes 3145736 | tf_op jit(solution)/shard_map/ppermute | solution.py:365
  181.3 24.3 %collective-permute-start.33 = (f32[4,256]{1,0:T(4,128)S(1)}, f32[4,256]{1,0:T(4,128)S(1)}, u32[]{:S(2)}, u32[]{:S(2)}) collective-permute-start(f32[4,256]{1,0:T(4,128)S(1)} %add.69.y_ref), channel_id=1, source_target_pairs={{0,4},{1,5},{2,6},{3,7},{4,0},{5,1},{6,2},{7,3},{8,12},{9,13},{10,... | collective-permute-start | bytes 12296 | tf_op jit(solution)/shard_map/ppermute | solution.py:349
  (34 other events, 269.7 us)

commit v2 on v1

--- a/solution.py
+++ b/solution.py
@@ -16,7 +16,7 @@
 
 VM = pl.BlockSpec(memory_space=pltpu.VMEM)
 SM = pl.BlockSpec(memory_space=pltpu.SMEM)
-HB = pl.BlockSpec(memory_space=pl.ANY)
+HB = pl.BlockSpec(memory_space=pltpu.HBM)
 NO_COST = pl.CostEstimate(flops=0, bytes_accessed=0, transcendentals=0)
 
 
@@ -95,26 +95,20 @@
         notes_ref[pl.ds(3 * leaves + l, 1), :] = jnp.full((1, notes_ref.shape[1]), parent_ref[l].astype(F32))
     bundle_ref[pl.ds(base + width, 4 * leaves), :] = notes_ref[...].astype(BF16)
     for l in range(leaves):
-        rows = pl.ds(l * width, width)
-        tile = jnp.where(mask_ref[l] != 0, link_ref[l].astype(F32), 0.0).astype(BF16)
-        bundle_ref[rows, :] = tile
-
-
-def solved_kernel(leaves, width, bundle_ref, inverse_ref, solved_ref):
-    for l in range(leaves):
-        rows = pl.ds(l * width, width)
-        solved_ref[rows, :] = jnp.dot(inverse_ref[l], bundle_ref[rows, :], preferred_element_type=F32).astype(BF16)
-
-
-def cut_kernel(x_hbm, y_hbm, *refs):
-    top_ref, end_ref, sem = refs[-3:]
-    cut = top_ref.shape[0]
-    copies = [pltpu.make_async_copy(x_hbm.at[pl.ds(0, cut)], top_ref, sem.at[0]),
-              pltpu.make_async_copy(y_hbm.at[pl.ds(cut, end_ref.shape[0])], end_ref, sem.at[1])]
-    for copy in copies:
-        copy.start()
-    for copy in copies:
-        copy.wait()
+        bundle_ref[pl.ds(l * width, width), :] = masked_tile(mask_ref, link_ref, l)
+
+
+def masked_tile(mask_ref, link_ref, l):
+    return jnp.where(mask_ref[l] != 0, link_ref[l].astype(F32), 0.0).astype(BF16)
+
+
+def solved_kernel(leaves, width, inverse_ref, bundle_ref, *refs):
+    l = 0
+    for ref in refs:
+        for i in range(ref.shape[0] // width):
+            tile = bundle_ref[pl.ds(l * width, width), :]
+            ref[pl.ds(i * width, width), :] = jnp.dot(inverse_ref[l], tile, preferred_element_type=F32).astype(BF16)
+            l += 1
 
 
 def node_add(acc, parent, value):
@@ -174,8 +168,8 @@
     return inv
 
 
-def early_kernel(leaves, width, nodes, core_ref, parent_ref, rhs_ref, inverse_ref, own_ref, x_ref, y_ref, swap_ref, m_ref, km_ref,
-                 diag_ref, right_ref):
+def early_kernel(leaves, width, nodes, core_ref, parent_ref, rhs_ref, inverse_ref, own_ref, x_ref, y_ref, swap_ref, *refs):
+    m_ref, km_ref, diag_ref, right_ref = refs[-4:]
     base, cols = leaves * width, own_ref.shape[1]
     for k, ref in enumerate((own_ref, x_ref, y_ref)):
         if k:
@@ -190,8 +184,7 @@
 
 
 def late_kernel(leaves, width, cut, core_ref, parent_ref, rhs_ref, node_rhs_ref, node_diag_ref, da_ref, db_ref, swap_ref, early_ref,
-                diag_ref, right_ref, token_ref, m_ref, km_ref, reduced_ref, scaling_ref, x_ref, part_ref):
-    del token_ref
+                diag_ref, right_ref, m_ref, km_ref, reduced_ref, scaling_ref, x_ref, part_ref):
     nodes, cols = node_rhs_ref.shape
     base = leaves * width
     inv = pair_in(leaves, width, core_ref, db_ref[pl.ds(base - cut, width), :], swap_ref[...])
@@ -255,67 +248,88 @@
         out_ref[pl.ds(l, 1), :] = rowdot(rest[l:l + 1, :], inverse_ref[l], True)
 
 
-def pick(places, sources, ties):
-    shape = jax.ShapeDtypeStruct(sources[0].shape, sources[0].dtype)
-    count = places.shape[0]
-
-    def kernel(place_ref, *refs):
-        first = len(sources) + len(ties)
-        ins, outs, token_ref = refs[:len(sources)], refs[first:first + count], refs[first + count]
+def join(blocks, tie):
+    rows = blocks[0].shape[0]
+
+    def kernel(*refs):
+        out_ref = refs[-1]
+        for n in range(len(blocks)):
+            out_ref[pl.ds(n * rows, rows), :] = refs[n][...]
+
+    return pl.pallas_call(
+        kernel,
+        out_shape=jax.ShapeDtypeStruct((len(blocks) * rows, blocks[0].shape[1]), blocks[0].dtype),
+        in_specs=[VM] * (len(blocks) + 1),
+        out_specs=VM,
+        compiler_params=pltpu.CompilerParams(vmem_limit_bytes=16 * MIB),
+        cost_estimate=NO_COST,
+    )(*blocks, tie)
+
+
+def pick(places, source, ties):
+    shape = jax.ShapeDtypeStruct(source.shape[1:], source.dtype)
+    count = len(places)
+
+    def kernel(place_ref, source_ref, *refs):
+        first = len(ties)
+        outs, token_ref = refs[first:first + count], refs[first + count]
         held, sem_in, sem_out = refs[first + count + 1:]
         token_ref[...] = jnp.zeros_like(token_ref)
-        for n in range(count):
-            for i, source in enumerate(ins):
-                @pl.when(place_ref[n] == i)
-                def _():
-                    pltpu.make_async_copy(source, held.at[n], sem_in.at[n]).start()
-        for n in range(count):
-            @pl.when(place_ref[n] >= 0)
-            def _():
-                pltpu.make_async_copy(ins[0], held.at[n], sem_in.at[n]).wait()
-                pltpu.make_async_copy(held.at[n], outs[n], sem_out.at[n]).start()
-        for n in range(count):
-            @pl.when(place_ref[n] >= 0)
-            def _():
-                pltpu.make_async_copy(held.at[n], outs[n], sem_out.at[n]).wait()
+        reads = [pltpu.make_async_copy(source_ref.at[place_ref[n]], held.at[n], sem_in.at[n]) for n in range(count)]
+        writes = [pltpu.make_async_copy(held.at[n], outs[n], sem_out.at[n]) for n in range(count)]
+        for read in reads:
+            read.start()
+        for read, write in zip(reads, writes):
+            read.wait()
+            write.start()
+        for write in writes:
+            write.wait()
 
     return pl.pallas_call(
         kernel,
         out_shape=[shape] * count + [jax.ShapeDtypeStruct((8, 128), F32)],
-        in_specs=[SM] + [HB] * (len(sources) + len(ties)),
+        in_specs=[SM, HB] + [VM] * len(ties),
         out_specs=[HB] * count + [VM],
         scratch_shapes=[pltpu.VMEM((count,) + shape.shape, shape.dtype), pltpu.SemaphoreType.DMA((count,)),
                         pltpu.SemaphoreType.DMA((count,))],
-        compiler_params=pltpu.CompilerParams(vmem_limit_bytes=56 * MIB),
+        compiler_params=pltpu.CompilerParams(vmem_limit_bytes=48 * MIB),
         cost_estimate=NO_COST,
-    )(places, *sources, *ties)
-
-
-def product_kernel(leaves, width, info_ref, parent_ref, m_hbm, m3_hbm, *refs):
-    near, far = refs[:8], refs[8:16]
-    out_hbm, m_ref, u_ref, acc_ref, sem, out_sem = refs[16:]
+    )(jnp.stack(places).astype(jnp.int32), source, *ties)
+
+
+def product_kernel(leaves, width, parts, info_ref, parent_ref, m_hbm, m3_hbm, *refs):
+    count = len(parts)
+    gathered, same, other = refs[:count], refs[count:4 * count], refs[4 * count:5 * count]
+    out_hbm, m_ref, u_ref, acc_ref, sem, out_sem = refs[5 * count:]
     cols = m_ref.shape[1]
     base = leaves * width
-    core, is_far = info_ref[0], info_ref[1]
-    m_copies = [pltpu.make_async_copy(m_hbm, m_ref.at[pl.ds(0, 3 * base)], sem.at[8]),
-                pltpu.make_async_copy(m3_hbm, m_ref.at[pl.ds(3 * base, base)], sem.at[9])]
+    core, column = info_ref[0], info_ref[1]
+    m_copies = [pltpu.make_async_copy(m_hbm, m_ref.at[pl.ds(0, 3 * base)], sem.at[8, 0]),
+                pltpu.make_async_copy(m3_hbm, m_ref.at[pl.ds(3 * base, base)], sem.at[8, 1])]
     for copy in m_copies:
         copy.start()
-    for n in range(8):
-        for flag, group in ((0, near), (1, far)):
-            @pl.when(is_far == flag)
-            def _():
-                pltpu.make_async_copy(group[n], u_ref.at[n], sem.at[n]).start()
+    loads = {}
+    for side in range(2):
+        place = 2 * column + (core if side == 0 else 1 - core)
+        for k in range(4):
+            for h in range(count):
+                if k == 0:
+                    source = gathered[h].at[place]
+                else:
+                    source = other[h].at[pl.ds((k - 1) * parts[h], parts[h])] if side else same[h * 3 + k - 1]
+                n = side * 4 + k
+                loads[n, h] = pltpu.make_async_copy(source, u_ref.at[n, pl.ds(sum(parts[:h]), parts[h])], sem.at[n, h])
+                loads[n, h].start()
     acc_ref[...] = jnp.zeros_like(acc_ref)
     for copy in m_copies:
         copy.wait()
     for side in range(2):
         for k in range(4):
             n = side * 4 + k
-            pltpu.make_async_copy(near[n], u_ref.at[n], sem.at[n]).wait()
-
-            @pl.loop(0, leaves)
-            def _(i):
+            for h in range(count):
+                loads[n, h].wait()
+
+            for i in range(leaves):
                 tile = m_ref[pl.ds((k * leaves + i) * width, width), :]
                 unit = u_ref[n, pl.ds(i * width, width), :]
                 value = lax.dot_general(tile, unit, (((0,), (0,)), ((), ())), preferred_element_type=F32)
@@ -342,32 +356,16 @@
     def over_scen(x, k):
         return lax.ppermute(x, "scen", [(i, i ^ k) for i in range(scen)])
 
-    def over_z(x, step, sources):
-        return lax.ppermute(x, "blk", [(2 * i + c, 2 * (i + step) + c) for i in sources for c in range(2)])
-
     def flip_z(x, k):
         return lax.ppermute(x, "blk", [(i, i ^ (2 * k)) for i in range(blk)])
 
     def flip_core(x):
         return lax.ppermute(x, "blk", [(i, i ^ 1) for i in range(blk)])
-
-    def distance(i, j):
-        return abs(i - j)
-
-    def in_plane(x, k, far):
-        pairs = [((i ^ k) * blk + 2 * j + c, i * blk + 2 * j + c) for i in range(scen) for j in range(planes) for c in range(2)
-                 if (distance(i, j) == planes - 1) == far]
-        return lax.ppermute(x, ("scen", "blk"), pairs)
-
-    def flip_far(x):
-        pairs = [(i * blk + 2 * j + c, i * blk + 2 * j + 1 - c) for i in range(scen) for j in range(planes) for c in range(2)
-                 if distance(i, j) == planes - 1]
-        return lax.ppermute(x, ("scen", "blk"), pairs)
 
     masks = tile_mask.reshape(leaves)
     total = base + width + 4 * leaves
     cut = base // 2 + width // 2
-    call = functools.partial(pl.pallas_call, cost_estimate=NO_COST)
+    call = functools.partial(pl.pallas_call, cost_estimate=NO_COST, compiler_params=pltpu.CompilerParams(vmem_limit_bytes=16 * MIB))
     struct = jax.ShapeDtypeStruct
     bundle = call(
         functools.partial(start_kernel, leaves, width),
@@ -376,29 +374,17 @@
         out_specs=VM,
         scratch_shapes=[pltpu.VMEM((4 * leaves, cols), F32)],
     )(core1, masks, parent, link, leaf_inverse, leaf_rhs)
-
-    bx, by = over_scen(bundle, 1), over_scen(bundle, 2)
+    parts = [base - base // 4, base // 4]
     solved = call(
         functools.partial(solved_kernel, leaves, width),
-        out_shape=struct((base, cols), BF16),
+        out_shape=[struct((rows, cols), BF16) for rows in parts],
         in_specs=[VM, VM],
-        out_specs=VM,
-    )(bundle, leaf_inverse)
-    up = {1: over_z(solved, 1, range(planes - 1))}
-    down = {1: over_z(solved, -1, range(1, planes))}
-    top, end = call(
-        cut_kernel,
-        out_shape=[struct((cut, cols), BF16), struct((total - cut, cols), BF16)],
-        in_specs=[HB] * 4,
-        out_specs=[VM, VM],
-        scratch_shapes=[pltpu.SemaphoreType.DMA((2,))],
-    )(bx, by, up[1], down[1])
-    da, db = over_scen(top, 2), over_scen(end, 1)
-    for step in range(2, planes - 1):
-        up[step] = over_z(up[step - 1], 1, range(step - 1, planes - 1))
-        down[step] = over_z(down[step - 1], -1, range(1, planes - step + 1))
-    sources = [solved] + [up[i] for i in range(1, planes - 1)] + [down[i] for i in range(1, planes - 1)]
-
+        out_specs=[VM] * len(parts),
+    )(leaf_inverse, bundle)
+    gathered = [lax.all_gather(part, "blk") for part in solved]
+
+    bx, by = over_scen(bundle, 1), over_scen(bundle, 2)
+    da, db = over_scen(bx[:cut], 2), over_scen(by[cut:], 1)
     tops = [bx[base:], by[base:], db[base - cut:]]
     swap = flip_core(jnp.concatenate([t[:width] for t in tops[:2]], axis=0))
     swap3 = flip_core(tops[2][:width])
@@ -409,37 +395,27 @@
     rights, rights3 = jnp.concatenate(sides[:3], axis=0), jnp.concatenate(sides, axis=0)
 
     count = scen * leaves
-    node_shape = struct((nodes, cols), F32)
-    part_shape = struct((count, width), F32)
-    early_shape, late_shape = struct((3 * base, cols), BF16), struct((base, cols), BF16)
+    node_shape, part_shape = pltpu.VMEM((nodes, cols), F32), pltpu.VMEM((count, width), F32)
+    early_shape, late_shape = pltpu.VMEM((3 * base, cols), BF16), pltpu.VMEM((base, cols), BF16)
+    terms_shape = pltpu.VMEM((3 * nodes, cols), F32)
     m_all, km_all, diag, right = call(
         functools.partial(early_kernel, leaves, width, nodes),
-        out_shape=[early_shape, early_shape, struct((3 * nodes, cols), F32), struct((3 * nodes, cols), F32)],
+        out_shape=[early_shape, early_shape, terms_shape, terms_shape],
         in_specs=[SM, SM] + [VM] * 6,
         out_specs=[VM] * 4,
-        compiler_params=pltpu.CompilerParams(vmem_limit_bytes=56 * MIB),
+        compiler_params=pltpu.CompilerParams(vmem_limit_bytes=20 * MIB),
     )(core1, jnp.concatenate(owners[:3]), rights, leaf_inverse, bundle, bx, by, swap)
-    def place(column):
-        away = z - column
-        near = jnp.where(away >= 0, away, planes - 2 - away)
-        return jnp.where(jnp.abs(away) == planes - 1, -1, near)
-
-    edge = jnp.where(z == 1, 2 * (planes - 2), planes - 2)
-    own_line, send1, send2, send3, onward, picked = pick(
-        jnp.stack([place(s), place(s ^ 1), place(s ^ 2), place(s ^ 3), edge]).astype(jnp.int32), sources, [da, db, km_all])
-    far0 = lax.ppermute(onward, "blk", [(2 * i + c, 2 * j + c) for i, j in ((1, 0), (planes - 2, planes - 1)) for c in range(2)])
-    near = [own_line] + [in_plane(x, k + 1, False) for k, x in enumerate((send1, send2, send3))]
-    far = [far0] + [in_plane(far0, k, True) for k in (1, 2, 3)]
-    near_other = [flip_core(x) for x in near]
-    far_other = [flip_far(x) for x in far]
+    def to_columns(gathered, ties):
+        *blocks, token = pick([2 * (s ^ k) + core for k in (1, 2, 3)], gathered, ties)
+        return [over_scen(x, k + 1) for k, x in enumerate(blocks)], token
 
     m3, km3, reduced, scaling, current, part = call(
         functools.partial(late_kernel, leaves, width, cut),
         out_shape=[late_shape, late_shape, node_shape, node_shape, node_shape, part_shape],
-        in_specs=[SM, SM] + [VM] * 10,
+        in_specs=[SM, SM] + [VM] * 9,
         out_specs=[VM] * 6,
-        compiler_params=pltpu.CompilerParams(vmem_limit_bytes=56 * MIB),
-    )(core1, parents, rights3, node_rhs, node_diag, da, db, swap3, km_all, diag, right, picked)
+        compiler_params=pltpu.CompilerParams(vmem_limit_bytes=16 * MIB),
+    )(core1, parents, rights3, node_rhs, node_diag, da, db, swap3, km_all, diag, right)
 
     def exchange(x):
         x = x + flip_core(x)
@@ -447,39 +423,49 @@
             x = x + flip_z(x, 1 << step)
         return x, flip_z(x, planes // 2)
 
-    ties = [[far0, near[1]], near[2:3], near[3:] + near_other[:2], far[1:3] + near_other[2:3], far[3:] + near_other[3:]]
+    arrived = exchange(part)
+    first, token = to_columns(gathered[0], [arrived[1]])
+    ties = [token]
     for sweep in range(ITERS):
         last = sweep == ITERS - 1
         current, part = call(
-            functools.partial(sweep_kernel, leaves, width, last, len(ties[sweep])),
-            out_shape=[node_shape, struct((leaves, width), F32) if last else part_shape],
-            in_specs=[SM] + [VM] * 10 + [HB] * len(ties[sweep]),
+            functools.partial(sweep_kernel, leaves, width, last, len(ties)),
+            out_shape=[struct((nodes, cols), F32), pltpu.VMEM((leaves, width), F32)] if last else [node_shape, part_shape],
+            in_specs=[SM] + [VM] * 10 + [VM if tie.dtype == F32 else HB for tie in ties],
             out_specs=[VM] * 2,
-            compiler_params=pltpu.CompilerParams(vmem_limit_bytes=24 * MIB),
-        )(parents, *exchange(part), reduced, scaling, node_diag, current, m_all, km_all, m3, km3, *ties[sweep])
+            compiler_params=pltpu.CompilerParams(vmem_limit_bytes=16 * MIB),
+        )(parents, *arrived, reduced, scaling, node_diag, current, m_all, km_all, m3, km3, *ties)
+        arrived = exchange(part)
+        ties = []
+        if sweep == 1:
+            ties = first
+        elif sweep == 2:
+            others = [flip_core(join(first, part))]
+            second, token = to_columns(gathered[1], [part])
+            ties = [token]
+    ties = others + second
     leaf_solution = call(
         functools.partial(leaf_kernel, leaves),
         out_shape=struct((leaves, width), F32),
-        in_specs=[VM] * 4 + [HB] * len(ties[ITERS]),
+        in_specs=[VM] * 4 + [HB] * len(ties),
         out_specs=VM,
-    )(*exchange(part), leaf_rhs, leaf_inverse, *ties[ITERS])
-
-    schur = pl.pallas_call(
-        functools.partial(product_kernel, leaves, width),
-        out_shape=jax.ShapeDtypeStruct((nodes, cols, 2 * cols), F32),
-        in_specs=[SM, SM] + [HB] * 18,
+    )(*arrived, leaf_rhs, leaf_inverse, *ties)
+
+    others.append(flip_core(join(second, leaf_solution)))
+    schur = call(
+        functools.partial(product_kernel, leaves, width, parts),
+        out_shape=struct((nodes, cols, 2 * cols), F32),
+        in_specs=[SM, SM] + [HB] * (2 + 5 * len(parts)),
         out_specs=HB,
         scratch_shapes=[
             pltpu.VMEM((scen * base, cols), BF16),
             pltpu.VMEM((8, base, cols), BF16),
             pltpu.VMEM((2, nodes, cols, cols), F32),
-            pltpu.SemaphoreType.DMA((10,)),
+            pltpu.SemaphoreType.DMA((9, len(parts))),
             pltpu.SemaphoreType.DMA((2,)),
         ],
-        compiler_params=pltpu.CompilerParams(vmem_limit_bytes=56 * MIB),
-        cost_estimate=NO_COST,
-    )(jnp.stack([core, (jnp.abs(z - s) == planes - 1).astype(core.dtype)]).astype(jnp.int32), parents, m_all, m3,
-      *near, *near_other, *far, *far_other)
+        compiler_params=pltpu.CompilerParams(vmem_limit_bytes=32 * MIB),
+    )(jnp.stack([core, s]).astype(jnp.int32), parents, m_all, m3, *gathered, *first, *second, *others)
     return current, leaf_solution, schur
 
 

time: 227 us -> 178 us (0.78)
  starting transfers between devices: 85.8 us -> 32.1 us
  Pallas kernels: 52.4 us -> 33.6 us
  between operations: 1.27 us -> 14.5 us
  waiting for transfers between devices: 67 us -> 78.5 us
  local copies, waits for them, and re-layouts: 12.3 us -> 17 us
  other arithmetic: 5.64 us -> 1.49 us
    ppermute x4 -> x10, waiting for transfers between devices: 0.52 us -> 43.3 us  [over_scen(): return lax.ppermute(x, 'scen', [(i, i ^ k) for i in range(scen)])]
    ppermute x15 -> x0, waiting for transfers between devices: 40.4 us -> none  [the longest x4 26 us: over_z(): lax.ppermute(x, 'blk', [(2 * i + c, 2 * (i + step) + c) for i in sources...]
    ppermute x10, starting transfers between devices: 51 us -> 16.7 us  [flip_z(): return lax.ppermute(x, 'blk', [(i, i ^ 2 * k) for i in range(blk)])]
    ppermute x15 -> x0, starting transfers between devices: 28.2 us -> none  [the longest x6 12.6 us: in_plane(): return lax.ppermute(x, ('scen', 'blk'), pairs)]
    ppermute x4 -> x10, starting transfers between devices: 5.57 us -> 15 us  [over_scen(): return lax.ppermute(x, 'scen', [(i, i ^ k) for i in range(scen)])]
    pallas_call x7 -> x8, Pallas kernels: 29.3 us -> 21.1 us  [the longest x1 9.16 us: plane_body(): call(functools.partial(product_kernel, leaves, width, parts), out_shape=s...]
    ppermute x10, waiting for transfers between devices: 21.4 us -> 27 us  [flip_z(): return lax.ppermute(x, 'blk', [(i, i ^ 2 * k) for i in range(blk)])]
    unnamed x52 -> x70, local copies, waits for them, and re-layouts: 9.75 us -> 14.7 us
  transfers between devices with their start and end apart: 40 -> 31, of which waited for: 16 -> 20; matrix products, arithmetic and copies ran while one was open for 4% -> 2% of each run, Pallas kernels for 15% -> 12%
where the time goes in v2:
time: 178 us; the launch traced here: 177 us
  waiting for transfers between devices  78.5 us (44%)
  Pallas kernels  33.6 us (19%)
  starting transfers between devices  32.1 us (18%)
  local copies, waits for them, and re-layouts  17 us (10%)
  between operations  14.5 us (8%)
    ppermute x10, waiting for transfers between devices, over_scen(): return lax.ppermute(x, 'scen', [(i, i ^ k) for i in range(scen)])  43.3 us
    ppermute x10, waiting for transfers between devices, flip_z(): return lax.ppermute(x, 'blk', [(i, i ^ 2 * k) for i in range(blk)])  27 us
    ppermute x10, starting transfers between devices, flip_z(): return lax.ppermute(x, 'blk', [(i, i ^ 2 * k) for i in range(blk)])  16.7 us
    ppermute x10, starting transfers between devices, over_scen(): return lax.ppermute(x, 'scen', [(i, i ^ k) for i in range(scen)])  15 us
    unnamed x70, local copies, waits for them, and re-layouts  14.7 us
    pallas_call x1, Pallas kernels, plane_body(): call(functools.partial(product_kernel, leaves, width, parts), out_shape=s...  9.16 us
    pallas_call x4, Pallas kernels, plane_body(): call(functools.partial(sweep_kernel, leaves, width, last, len(ties)), out...  8.99 us
    ppermute x9, waiting for transfers between devices, flip_core(): return lax.ppermute(x, 'blk', [(i, i ^ 1) for i in range(blk)])  8.07 us
  transfers between devices with their start and end apart: 31, of which 20 were waited for; matrix products, arithmetic and copies ran while one was open for 2% of the time, Pallas kernels for 12%

profile of v2, /device:TPU:0, one launch (start us, length us, event | category | flops | bytes accessed | tf_op | source)
XLA Modules:
  0.0 177.2 jit_solution(2865723986567512313)
XLA Ops:
  13.8 3.0 %collective-permute-start.1 = (bf16[1296,512]{1,0:T(8,128)(2,1)S(1)}, bf16[1296,512]{1,0:T(8,128)(2,1)S(1)}, u32[]{:S(2)}, u32[]{:S(2)}) collective-permute-start(bf16[1296,512]{1,0:T(8,128)(2,1)S(1)} %shard_map.94.own_ref.bundle_ref), channel_id=1, source_target_pairs={{0,16},{8,24},{16,0},{24,8},{1,17},{9,25},{17,1},{25,9},{2,18},{10... | collective-permute-start | bytes 3981320 | tf_op jit(solution)/shard_map/ppermute | solution.py:357
  18.4 27.6 %collective-permute-done.1.y_ref = bf16[1296,512]{1,0:T(8,128)(2,1)S(1)} collective-permute-done((bf16[1296,512]{1,0:T(8,128)(2,1)S(1)}, bf16[1296,512]{1,0:T(8,128)(2,1)S(1)}, u32[]{:S(2)}, u32[]{:S(2)}) %collective-permute-start.1) | collective-permute-done | bytes 1327136 | tf_op jit(solution)/shard_map/ppermute | solution.py:357
  46.0 1.8 %collective-permute-start.2 = (bf16[656,512]{1,0:T(8,128)(2,1)S(1)}, bf16[656,512]{1,0:T(8,128)(2,1)S(1)}, u32[]{:S(2)}, u32[]{:S(2)}) collective-permute-start(bf16[656,512]{1,0:T(8,128)(2,1)S(1)} %slice.93), channel_id=1, source_target_pairs={{0,8},{8,0},{16,24},{24,16},{1,9},{9,1},{17,25},{25,17},{2,10},{10... | collective-permute-start | bytes 2015240 | tf_op jit(solution)/shard_map/ppermute | solution.py:357
  54.2 4.7 %shard_map.95 = (bf16[3072,512]{1,0:T(8,128)(2,1)S(1)}, bf16[3072,512]{1,0:T(8,128)(2,1)S(1)}, f32[6,512]{1,0:T(8,128)S(1)}, f32[6,512]{1,0:T(8,128)S(1)}) custom-call(s32[1]{0:T(128)} %bitcast.core_ref, s32[12]{0:T(128)S(1)} %pad_add_fusion.1.parent_ref, f32[12,256]{1,0:T(8,128)S(1)} %pad_maximum_fusion.2.rhs_ref, bf16[4,256,256]{2,1,0:T(8,128)(2,1)S(1)} %copy-done.16, ...), custom_call_target="tpu_custom_call" | custom-call | tf_op jit(solution)/shard_map/pallas_call | solution.py:401
  58.9 3.6 %collective-permute-done.2.db_ref = bf16[656,512]{1,0:T(8,128)(2,1)S(1)} collective-permute-done((bf16[656,512]{1,0:T(8,128)(2,1)S(1)}, bf16[656,512]{1,0:T(8,128)(2,1)S(1)}, u32[]{:S(2)}, u32[]{:S(2)}) %collective-permute-start.2) | collective-permute-done | bytes 671776 | tf_op jit(solution)/shard_map/ppermute | solution.py:357
  62.8 5.5 %collective-permute-done.3.da_ref = bf16[640,512]{1,0:T(8,128)(2,1)S(1)} collective-permute-done((bf16[640,512]{1,0:T(8,128)(2,1)S(1)}, bf16[640,512]{1,0:T(8,128)(2,1)S(1)}, u32[]{:S(2)}, u32[]{:S(2)}) %collective-permute-start.3) | collective-permute-done | bytes 655392 | tf_op jit(solution)/shard_map/ppermute | solution.py:357
  68.3 2.9 %shard_map.96 = (bf16[1024,512]{1,0:T(8,128)(2,1)S(1)}, bf16[1024,512]{1,0:T(8,128)(2,1)S(1)}, f32[2,512]{1,0:T(2,128)S(1)}, f32[2,512]{1,0:T(2,128)S(1)}, f32[2,512]{1,0:T(2,128)S(1)}, /*index=5*/f32[16,256]{1,0:T(8,128)S(1)}) custom-call(s32[1]{0:T(128)} %bitcast.core_ref, s32[16]{0:T(128)S(1)} %pad_add_fusion.parent_ref, ...), custom_call_target="tpu_custom_call" | custom-call | tf_op jit(solution)/shard_map/pallas_call | solution.py:412
  75.9 2.2 %collective-permute-done.7 = f32[16,256]{1,0:T(8,128)S(1)} collective-permute-done((f32[16,256]{1,0:T(8,128)S(1)}, f32[16,256]{1,0:T(8,128)S(1)}, u32[]{:S(2)}, u32[]{:S(2)}) %collective-permute-start.7) | collective-permute-done | bytes 16416 | tf_op jit(solution)/shard_map/ppermute | solution.py:360
  78.1 2.8 %collective-permute-start.8 = (f32[16,256]{1,0:T(8,128)S(1)}, f32[16,256]{1,0:T(8,128)S(1)}, u32[]{:S(2)}, u32[]{:S(2)}) collective-permute-start(f32[16,256]{1,0:T(8,128)S(1)} %add.72.y_ref), channel_id=1, source_target_pairs={{0,4},{1,5},{2,6},{3,7},{4,0},{5,1},{6,2},{7,3},{8,12},{9,13},{10,... | collective-permute-start | bytes 49160 | tf_op jit(solution)/shard_map/ppermute | solution.py:360
  81.0 1.7 collective-permute-done.8.refs_0_.z_ref
  82.8 2.5 %shard_map.98 = (bf16[768,512]{1,0:T(8,128)(2,1)S(1)}, bf16[768,512]{1,0:T(8,128)(2,1)S(1)}, bf16[768,512]{1,0:T(8,128)(2,1)S(1)}, f32[8,128]{1,0:T(8,128)S(1)}) custom-call(s32[3]{0:T(128)S(1)} %pad_add_fusion.2.place_ref, bf16[8,768,512]{2,1,0:T(8,128)(2,1)} %bitcast.8, f32[16,256]{1,0:T(8,128)S(1)} %collective-permute-done.8.refs_0_.z_ref), custom_call_target="tpu_custom_call" | custom-call | tf_op jit(solution)/shard_map/pallas_call | solution.py:288
  88.9 2.4 %shard_map.99 = (f32[2,512]{1,0:T(2,128)S(1)}, f32[16,256]{1,0:T(8,128)S(1)}) custom-call(s32[16]{0:T(128)S(1)} %pad_add_fusion.parent_ref, f32[16,256]{1,0:T(8,128)S(1)} %add.72.y_ref, f32[16,256]{1,0:T(8,128)S(1)} %collective-permute-done.8.refs_0_.z_ref, f32[2,512]{1,0:T(2,128)S(1)} %get-tuple-element.35.reduced_ref, ...), custom_call_target="tpu_custom_call" | custom-call | tf_op jit(solution)/shard_map/pallas_call | solution.py:431
  94.1 3.2 %collective-permute-done.10 = f32[16,256]{1,0:T(8,128)S(1)} collective-permute-done((f32[16,256]{1,0:T(8,128)S(1)}, f32[16,256]{1,0:T(8,128)S(1)}, u32[]{:S(2)}, u32[]{:S(2)}) %collective-permute-start.10) | collective-permute-done | bytes 16416 | tf_op jit(solution)/shard_map/ppermute | solution.py:360
  97.2 2.2 %collective-permute-start.11 = (f32[16,256]{1,0:T(8,128)S(1)}, f32[16,256]{1,0:T(8,128)S(1)}, u32[]{:S(2)}, u32[]{:S(2)}) collective-permute-start(f32[16,256]{1,0:T(8,128)S(1)} %add.77.y_ref), channel_id=1, source_target_pairs={{0,4},{1,5},{2,6},{3,7},{4,0},{5,1},{6,2},{7,3},{8,12},{9,13},{10,... | collective-permute-start | bytes 49160 | tf_op jit(solution)/shard_map/ppermute | solution.py:360
  99.4 3.5 %collective-permute-done.11.z_ref = f32[16,256]{1,0:T(8,128)S(1)} collective-permute-done((f32[16,256]{1,0:T(8,128)S(1)}, f32[16,256]{1,0:T(8,128)S(1)}, u32[]{:S(2)}, u32[]{:S(2)}) %collective-permute-start.11) | collective-permute-done | bytes 16416 | tf_op jit(solution)/shard_map/ppermute | solution.py:360
  103.0 2.4 %shard_map.100 = (f32[2,512]{1,0:T(2,128)S(1)}, f32[16,256]{1,0:T(8,128)S(1)}) custom-call(s32[16]{0:T(128)S(1)} %pad_add_fusion.parent_ref, f32[16,256]{1,0:T(8,128)S(1)} %add.77.y_ref, f32[16,256]{1,0:T(8,128)S(1)} %collective-permute-done.11.z_ref, f32[2,512]{1,0:T(2,128)S(1)} %get-tuple-element.35.reduced_ref, ...), custom_call_target="tpu_custom_call" | custom-call | tf_op jit(solution)/shard_map/pallas_call | solution.py:431
  107.2 3.2 %collective-permute-done.13 = f32[16,256]{1,0:T(8,128)S(1)} collective-permute-done((f32[16,256]{1,0:T(8,128)S(1)}, f32[16,256]{1,0:T(8,128)S(1)}, u32[]{:S(2)}, u32[]{:S(2)}) %collective-permute-start.13) | collective-permute-done | bytes 16416 | tf_op jit(solution)/shard_map/ppermute | solution.py:360
  110.4 2.0 %collective-permute-start.14 = (f32[16,256]{1,0:T(8,128)S(1)}, f32[16,256]{1,0:T(8,128)S(1)}, u32[]{:S(2)}, u32[]{:S(2)}) collective-permute-start(f32[16,256]{1,0:T(8,128)S(1)} %add.79.y_ref), channel_id=1, source_target_pairs={{0,4},{1,5},{2,6},{3,7},{4,0},{5,1},{6,2},{7,3},{8,12},{9,13},{10,... | collective-permute-start | bytes 49160 | tf_op jit(solution)/shard_map/ppermute | solution.py:360
  112.4 2.6 %collective-permute-done.14.z_ref = f32[16,256]{1,0:T(8,128)S(1)} collective-permute-done((f32[16,256]{1,0:T(8,128)S(1)}, f32[16,256]{1,0:T(8,128)S(1)}, u32[]{:S(2)}, u32[]{:S(2)}) %collective-permute-start.14) | collective-permute-done | bytes 16416 | tf_op jit(solution)/shard_map/ppermute | solution.py:360
  115.0 6.7 %collective-permute-done.16.refs_1_.refs_3_ = bf16[768,512]{1,0:T(8,128)(2,1)S(1)} collective-permute-done((bf16[768,512]{1,0:T(8,128)(2,1)S(1)}, bf16[768,512]{1,0:T(8,128)(2,1)S(1)}, u32[]{:S(2)}, u32[]{:S(2)}) %collective-permute-start.16) | collective-permute-done | bytes 786464 | tf_op jit(solution)/shard_map/ppermute | solution.py:357
  121.7 2.4 %shard_map.101 = (f32[2,512]{1,0:T(2,128)S(1)}, f32[16,256]{1,0:T(8,128)S(1)}) custom-call(s32[16]{0:T(128)S(1)} %pad_add_fusion.parent_ref, f32[16,256]{1,0:T(8,128)S(1)} %add.79.y_ref, f32[16,256]{1,0:T(8,128)S(1)} %collective-permute-done.14.z_ref, f32[2,512]{1,0:T(2,128)S(1)} %get-tuple-element.35.reduced_ref, ...), custom_call_target="tpu_custom_call" | custom-call | tf_op jit(solution)/shard_map/pallas_call | solution.py:431
  133.8 2.8 %collective-permute-done.19 = f32[16,256]{1,0:T(8,128)S(1)} collective-permute-done((f32[16,256]{1,0:T(8,128)S(1)}, f32[16,256]{1,0:T(8,128)S(1)}, u32[]{:S(2)}, u32[]{:S(2)}) %collective-permute-start.19) | collective-permute-done | bytes 16416 | tf_op jit(solution)/shard_map/ppermute | solution.py:360
  136.7 2.1 %collective-permute-start.20 = (f32[16,256]{1,0:T(8,128)S(1)}, f32[16,256]{1,0:T(8,128)S(1)}, u32[]{:S(2)}, u32[]{:S(2)}) collective-permute-start(f32[16,256]{1,0:T(8,128)S(1)} %add.81.y_ref), channel_id=1, source_target_pairs={{0,4},{1,5},{2,6},{3,7},{4,0},{5,1},{6,2},{7,3},{8,12},{9,13},{10,... | collective-permute-start | bytes 49160 | tf_op jit(solution)/shard_map/ppermute | solution.py:360
  138.7 2.6 %collective-permute-done.20.z_ref = f32[16,256]{1,0:T(8,128)S(1)} collective-permute-done((f32[16,256]{1,0:T(8,128)S(1)}, f32[16,256]{1,0:T(8,128)S(1)}, u32[]{:S(2)}, u32[]{:S(2)}) %collective-permute-start.20) | collective-permute-done | bytes 16416 | tf_op jit(solution)/shard_map/ppermute | solution.py:360
  141.3 1.9 %copy-done.2 = bf16[3072,512]{1,0:T(8,128)(2,1)S(1)} copy-done((bf16[3072,512]{1,0:T(8,128)(2,1)S(1)}, bf16[3072,512]{1,0:T(8,128)(2,1)}, u32[]{:S(2)}) %copy-start.2) | copy-done | bytes 3145752
  143.2 1.8 %shard_map.103 = (f32[2,512]{1,0:T(2,128)}, f32[4,256]{1,0:T(4,128)S(1)}) custom-call(s32[16]{0:T(128)S(1)} %pad_add_fusion.parent_ref, f32[16,256]{1,0:T(8,128)S(1)} %add.81.y_ref, f32[16,256]{1,0:T(8,128)S(1)} %collective-permute-done.20.z_ref, f32[2,512]{1,0:T(2,128)S(1)} %get-tuple-element.35.reduced_ref, f32[2,512]{1,0:T(2,128)S(1)} %get-tuple-element.36.scaling_ref, ...), custom_call_target="tpu_custom_call" | custom-call | tf_op jit(solution)/shard_map/pallas_call | solution.py:431
  147.1 2.7 %collective-permute-done.22 = f32[4,256]{1,0:T(4,128)S(1)} collective-permute-done((f32[4,256]{1,0:T(4,128)S(1)}, f32[4,256]{1,0:T(4,128)S(1)}, u32[]{:S(2)}, u32[]{:S(2)}) %collective-permute-start.22) | collective-permute-done | bytes 4128 | tf_op jit(solution)/shard_map/ppermute | solution.py:360
  149.8 2.1 %collective-permute-start.23 = (f32[4,256]{1,0:T(4,128)S(1)}, f32[4,256]{1,0:T(4,128)S(1)}, u32[]{:S(2)}, u32[]{:S(2)}) collective-permute-start(f32[4,256]{1,0:T(4,128)S(1)} %add.83.y_ref), channel_id=1, source_target_pairs={{0,4},{1,5},{2,6},{3,7},{4,0},{5,1},{6,2},{7,3},{8,12},{9,13},{10,... | collective-permute-start | bytes 12296 | tf_op jit(solution)/shard_map/ppermute | solution.py:360
  151.9 2.4 %collective-permute-done.23.z_ref = f32[4,256]{1,0:T(4,128)S(1)} collective-permute-done((f32[4,256]{1,0:T(4,128)S(1)}, f32[4,256]{1,0:T(4,128)S(1)}, u32[]{:S(2)}, u32[]{:S(2)}) %collective-permute-start.23) | collective-permute-done | bytes 4128 | tf_op jit(solution)/shard_map/ppermute | solution.py:360
  156.2 2.2 %collective-permute-done.28.refs_9_ = bf16[768,512]{1,0:T(8,128)(2,1)S(1)} collective-permute-done((bf16[768,512]{1,0:T(8,128)(2,1)S(1)}, bf16[768,512]{1,0:T(8,128)(2,1)S(1)}, u32[]{:S(2)}, u32[]{:S(2)}) %collective-permute-start.28) | collective-permute-done | bytes 786464 | tf_op jit(solution)/shard_map/ppermute | solution.py:363
  158.4 2.8 %copy-done.7 = bf16[6144,512]{1,0:T(8,128)(2,1)S(1)} copy-done((bf16[6144,512]{1,0:T(8,128)(2,1)S(1)}, bf16[6144,512]{1,0:T(8,128)(2,1)}, u32[]{:S(2)}) %copy-start.7) | copy-done | bytes 6291480
  161.2 9.2 %shard_map.107 = f32[2,512,1024]{2,1,0:T(8,128)} custom-call(s32[2]{0:T(128)S(1)} %pad_add_fusion.3.info_ref, s32[16]{0:T(128)S(1)} %pad_add_fusion.parent_ref, bf16[3072,512]{1,0:T(8,128)(2,1)S(1)} %copy-done.3, bf16[1024,512]{1,0:T(8,128)(2,1)S(1)} %copy-done.6, bf16[8,768,512]{2,1,0:T(8,128)(2,1)S(1)} %bitcast.9, bf16[8,256,512]{2,1,0:T(8,128)(2,1)S(1)} %bitcast.11, ...), custom_call_target="tpu_custom_call" | custom-call | tf_op jit(solution)/shard_map/pallas_call | solution.py:455
  (147 shorter events, 41.2 us)
Async XLA Ops:
  7.2 75.6 %all-gather.5.cloned.1.call-start = ((), (), s32[]{:S(2)}) async-start(), calls=%async_computation | async-start | bytes 7077888 | tf_op jit(solution)/shard_map/all_gather | solution.py:384
  12.3 36.5 %copy-start.11 = (bf16[1296,512]{1,0:T(8,128)(2,1)}, bf16[1296,512]{1,0:T(8,128)(2,1)S(1)}, u32[]{:S(2)}) copy-start(bf16[1296,512]{1,0:T(8,128)(2,1)S(1)} %shard_map.94.own_ref.bundle_ref) | copy-start | bytes 3981316
  13.8 111.9 %all-gather.7.cloned.1.call-start = ((), (), s32[]{:S(2)}) async-start(), calls=%async_computation.1 | async-start | bytes 2359296 | tf_op jit(solution)/shard_map/all_gather | solution.py:384
  13.8 32.2 %collective-permute-start.1 = (bf16[1296,512]{1,0:T(8,128)(2,1)S(1)}, bf16[1296,512]{1,0:T(8,128)(2,1)S(1)}, u32[]{:S(2)}, u32[]{:S(2)}) collective-permute-start(bf16[1296,512]{1,0:T(8,128)(2,1)S(1)} %shard_map.94.own_ref.bundle_ref), channel_id=1, source_target_pairs={{0,16},{8,24},{16,0},{24,8},{1,17},{9,25},{17,1},{25,9},{2,18},{10... | collective-permute-start | bytes 3981320 | tf_op jit(solution)/shard_map/ppermute | solution.py:357
  16.8 31.1 %collective-permute-start = (bf16[1296,512]{1,0:T(8,128)(2,1)S(1)}, bf16[1296,512]{1,0:T(8,128)(2,1)}, u32[]{:S(2)}, u32[]{:S(2)}) collective-permute-start(bf16[1296,512]{1,0:T(8,128)(2,1)S(1)} %shard_map.94.own_ref.bundle_ref), channel_id=1, source_target_pairs={{0,8},{8,0},{16,24},{24,16},{1,9},{9,1},{17,25},{25,17},{2,10},{10... | collective-permute-start | bytes 3981320 | tf_op jit(solution)/shard_map/ppermute | solution.py:357
  46.0 16.4 %collective-permute-start.2 = (bf16[656,512]{1,0:T(8,128)(2,1)S(1)}, bf16[656,512]{1,0:T(8,128)(2,1)S(1)}, u32[]{:S(2)}, u32[]{:S(2)}) collective-permute-start(bf16[656,512]{1,0:T(8,128)(2,1)S(1)} %slice.93), channel_id=1, source_target_pairs={{0,8},{8,0},{16,24},{24,16},{1,9},{9,1},{17,25},{25,17},{2,10},{10... | collective-permute-start | bytes 2015240 | tf_op jit(solution)/shard_map/ppermute | solution.py:357
  49.8 3.0 %collective-permute-start.5 = (bf16[512,512]{1,0:T(8,128)(2,1)S(1)}, bf16[512,512]{1,0:T(8,128)(2,1)S(1)}, u32[]{:S(2)}, u32[]{:S(2)}) collective-permute-start(bf16[512,512]{1,0:T(8,128)(2,1)S(1)} %pad_maximum_fusion), channel_id=1, source_target_pairs={{0,1},{1,0},{2,3},{3,2},{4,5},{5,4},{6,7},{7,6},{8,9},{9,8},{10,11... | collective-permute-start | bytes 1572872 | tf_op jit(solution)/shard_map/ppermute | solution.py:363
  51.1 17.1 %collective-permute-start.3 = (bf16[640,512]{1,0:T(8,128)(2,1)S(1)}, bf16[640,512]{1,0:T(8,128)(2,1)S(1)}, u32[]{:S(2)}, u32[]{:S(2)}) collective-permute-start(bf16[640,512]{1,0:T(8,128)(2,1)S(1)} %slice.105), channel_id=1, source_target_pairs={{0,16},{8,24},{16,0},{24,8},{1,17},{9,25},{17,1},{25,9},{2,18},{10... | collective-permute-start | bytes 1966088 | tf_op jit(solution)/shard_map/ppermute | solution.py:357
  62.5 5.8 %collective-permute-start.4 = (bf16[256,512]{1,0:T(8,128)(2,1)S(1)}, bf16[256,512]{1,0:T(8,128)(2,1)S(1)}, u32[]{:S(2)}, u32[]{:S(2)}) collective-permute-start(bf16[256,512]{1,0:T(8,128)(2,1)S(1)} %slice.106), channel_id=1, source_target_pairs={{0,1},{1,0},{2,3},{3,2},{4,5},{5,4},{6,7},{7,6},{8,9},{9,8},{10,11... | collective-permute-start | bytes 786440 | tf_op jit(solution)/shard_map/ppermute | solution.py:363
  73.2 1.2 collective-permute-start.6
  74.3 3.8 %collective-permute-start.7 = (f32[16,256]{1,0:T(8,128)S(1)}, f32[16,256]{1,0:T(8,128)S(1)}, u32[]{:S(2)}, u32[]{:S(2)}) collective-permute-start(f32[16,256]{1,0:T(8,128)S(1)} %add.71), channel_id=1, source_target_pairs={{0,2},{1,3},{2,0},{3,1},{4,6},{5,7},{6,4},{7,5},{8,10},{9,11},{10,... | collective-permute-start | bytes 49160 | tf_op jit(solution)/shard_map/ppermute | solution.py:360
  78.1 4.6 %collective-permute-start.8 = (f32[16,256]{1,0:T(8,128)S(1)}, f32[16,256]{1,0:T(8,128)S(1)}, u32[]{:S(2)}, u32[]{:S(2)}) collective-permute-start(f32[16,256]{1,0:T(8,128)S(1)} %add.72.y_ref), channel_id=1, source_target_pairs={{0,4},{1,5},{2,6},{3,7},{4,0},{5,1},{6,2},{7,3},{8,12},{9,13},{10,... | collective-permute-start | bytes 49160 | tf_op jit(solution)/shard_map/ppermute | solution.py:360
  85.3 29.7 %collective-permute-start.15 = (bf16[768,512]{1,0:T(8,128)(2,1)S(1)}, bf16[768,512]{1,0:T(8,128)(2,1)S(1)}, u32[]{:S(2)}, u32[]{:S(2)}) collective-permute-start(bf16[768,512]{1,0:T(8,128)(2,1)S(1)} %get-tuple-element.47), channel_id=1, source_target_pairs={{0,8},{8,0},{16,24},{24,16},{1,9},{9,1},{17,25},{25,17},{2,10},{10... | collective-permute-start | bytes 2359304 | tf_op jit(solution)/shard_map/ppermute | solution.py:357
  86.4 35.3 %collective-permute-start.16 = (bf16[768,512]{1,0:T(8,128)(2,1)S(1)}, bf16[768,512]{1,0:T(8,128)(2,1)S(1)}, u32[]{:S(2)}, u32[]{:S(2)}) collective-permute-start(bf16[768,512]{1,0:T(8,128)(2,1)S(1)} %get-tuple-element.48), channel_id=1, source_target_pairs={{0,16},{8,24},{16,0},{24,8},{1,17},{9,25},{17,1},{25,9},{2,18},{10... | collective-permute-start | bytes 2359304 | tf_op jit(solution)/shard_map/ppermute | solution.py:357
  87.4 34.3 %collective-permute-start.17 = (bf16[768,512]{1,0:T(8,128)(2,1)S(1)}, bf16[768,512]{1,0:T(8,128)(2,1)S(1)}, u32[]{:S(2)}, u32[]{:S(2)}) collective-permute-start(bf16[768,512]{1,0:T(8,128)(2,1)S(1)} %get-tuple-element.49), channel_id=1, source_target_pairs={{0,24},{8,16},{16,8},{24,0},{1,25},{9,17},{17,9},{25,1},{2,26},{10... | collective-permute-start | bytes 2359304 | tf_op jit(solution)/shard_map/ppermute | solution.py:357
  91.3 1.2 collective-permute-start.9
  92.5 4.7 %collective-permute-start.10 = (f32[16,256]{1,0:T(8,128)S(1)}, f32[16,256]{1,0:T(8,128)S(1)}, u32[]{:S(2)}, u32[]{:S(2)}) collective-permute-start(f32[16,256]{1,0:T(8,128)S(1)} %add.76), channel_id=1, source_target_pairs={{0,2},{1,3},{2,0},{3,1},{4,6},{5,7},{6,4},{7,5},{8,10},{9,11},{10,... | collective-permute-start | bytes 49160 | tf_op jit(solution)/shard_map/ppermute | solution.py:360
  97.2 5.7 %collective-permute-start.11 = (f32[16,256]{1,0:T(8,128)S(1)}, f32[16,256]{1,0:T(8,128)S(1)}, u32[]{:S(2)}, u32[]{:S(2)}) collective-permute-start(f32[16,256]{1,0:T(8,128)S(1)} %add.77.y_ref), channel_id=1, source_target_pairs={{0,4},{1,5},{2,6},{3,7},{4,0},{5,1},{6,2},{7,3},{8,12},{9,13},{10,... | collective-permute-start | bytes 49160 | tf_op jit(solution)/shard_map/ppermute | solution.py:360
  105.4 1.2 collective-permute-start.12
  106.6 3.8 %collective-permute-start.13 = (f32[16,256]{1,0:T(8,128)S(1)}, f32[16,256]{1,0:T(8,128)S(1)}, u32[]{:S(2)}, u32[]{:S(2)}) collective-permute-start(f32[16,256]{1,0:T(8,128)S(1)} %add.78), channel_id=1, source_target_pairs={{0,2},{1,3},{2,0},{3,1},{4,6},{5,7},{6,4},{7,5},{8,10},{9,11},{10,... | collective-permute-start | bytes 49160 | tf_op jit(solution)/shard_map/ppermute | solution.py:360
  110.4 4.6 %collective-permute-start.14 = (f32[16,256]{1,0:T(8,128)S(1)}, f32[16,256]{1,0:T(8,128)S(1)}, u32[]{:S(2)}, u32[]{:S(2)}) collective-permute-start(f32[16,256]{1,0:T(8,128)S(1)} %add.79.y_ref), channel_id=1, source_target_pairs={{0,4},{1,5},{2,6},{3,7},{4,0},{5,1},{6,2},{7,3},{8,12},{9,13},{10,... | collective-permute-start | bytes 49160 | tf_op jit(solution)/shard_map/ppermute | solution.py:360
  125.7 28.7 %collective-permute-start.24 = (bf16[2304,512]{1,0:T(8,128)(2,1)}, bf16[2304,512]{1,0:T(8,128)(2,1)}, u32[]{:S(2)}, u32[]{:S(2)}) collective-permute-start(bf16[2304,512]{1,0:T(8,128)(2,1)} %shard_map.104), channel_id=1, source_target_pairs={{0,1},{1,0},{2,3},{3,2},{4,5},{5,4},{6,7},{7,6},{8,9},{9,8},{10,11... | collective-permute-start | bytes 7077896 | tf_op jit(solution)/shard_map/ppermute | solution.py:363
  128.2 26.2 %collective-permute-start.25 = (bf16[256,512]{1,0:T(8,128)(2,1)S(1)}, bf16[256,512]{1,0:T(8,128)(2,1)S(1)}, u32[]{:S(2)}, u32[]{:S(2)}) collective-permute-start(bf16[256,512]{1,0:T(8,128)(2,1)S(1)} %get-tuple-element.56), channel_id=1, source_target_pairs={{0,8},{8,0},{16,24},{24,16},{1,9},{9,1},{17,25},{25,17},{2,10},{10... | collective-permute-start | bytes 786440 | tf_op jit(solution)/shard_map/ppermute | solution.py:357
  129.4 25.0 %collective-permute-start.26 = (bf16[256,512]{1,0:T(8,128)(2,1)S(1)}, bf16[256,512]{1,0:T(8,128)(2,1)S(1)}, u32[]{:S(2)}, u32[]{:S(2)}) collective-permute-start(bf16[256,512]{1,0:T(8,128)(2,1)S(1)} %get-tuple-element.57), channel_id=1, source_target_pairs={{0,16},{8,24},{16,0},{24,8},{1,17},{9,25},{17,1},{25,9},{2,18},{10... | collective-permute-start | bytes 786440 | tf_op jit(solution)/shard_map/ppermute | solution.py:357
  130.3 24.1 %collective-permute-start.27 = (bf16[256,512]{1,0:T(8,128)(2,1)S(1)}, bf16[256,512]{1,0:T(8,128)(2,1)S(1)}, u32[]{:S(2)}, u32[]{:S(2)}) collective-permute-start(bf16[256,512]{1,0:T(8,128)(2,1)S(1)} %get-tuple-element.58), channel_id=1, source_target_pairs={{0,24},{8,16},{16,8},{24,0},{1,25},{9,17},{17,9},{25,1},{2,26},{10... | collective-permute-start | bytes 786440 | tf_op jit(solution)/shard_map/ppermute | solution.py:357
  131.7 1.2 collective-permute-start.18
  132.9 3.7 %collective-permute-start.19 = (f32[16,256]{1,0:T(8,128)S(1)}, f32[16,256]{1,0:T(8,128)S(1)}, u32[]{:S(2)}, u32[]{:S(2)}) collective-permute-start(f32[16,256]{1,0:T(8,128)S(1)} %add.80), channel_id=1, source_target_pairs={{0,2},{1,3},{2,0},{3,1},{4,6},{5,7},{6,4},{7,5},{8,10},{9,11},{10,... | collective-permute-start | bytes 49160 | tf_op jit(solution)/shard_map/ppermute | solution.py:360
  136.7 4.6 %collective-permute-start.20 = (f32[16,256]{1,0:T(8,128)S(1)}, f32[16,256]{1,0:T(8,128)S(1)}, u32[]{:S(2)}, u32[]{:S(2)}) collective-permute-start(f32[16,256]{1,0:T(8,128)S(1)} %add.81.y_ref), channel_id=1, source_target_pairs={{0,4},{1,5},{2,6},{3,7},{4,0},{5,1},{6,2},{7,3},{8,12},{9,13},{10,... | collective-permute-start | bytes 49160 | tf_op jit(solution)/shard_map/ppermute | solution.py:360
  145.0 1.2 collective-permute-start.21
  146.2 3.6 %collective-permute-start.22 = (f32[4,256]{1,0:T(4,128)S(1)}, f32[4,256]{1,0:T(4,128)S(1)}, u32[]{:S(2)}, u32[]{:S(2)}) collective-permute-start(f32[4,256]{1,0:T(4,128)S(1)} %add.82), channel_id=1, source_target_pairs={{0,2},{1,3},{2,0},{3,1},{4,6},{5,7},{6,4},{7,5},{8,10},{9,11},{10,... | collective-permute-start | bytes 12296 | tf_op jit(solution)/shard_map/ppermute | solution.py:360
  149.8 4.6 %collective-permute-start.23 = (f32[4,256]{1,0:T(4,128)S(1)}, f32[4,256]{1,0:T(4,128)S(1)}, u32[]{:S(2)}, u32[]{:S(2)}) collective-permute-start(f32[4,256]{1,0:T(4,128)S(1)} %add.83.y_ref), channel_id=1, source_target_pairs={{0,4},{1,5},{2,6},{3,7},{4,0},{5,1},{6,2},{7,3},{8,12},{9,13},{10,... | collective-permute-start | bytes 12296 | tf_op jit(solution)/shard_map/ppermute | solution.py:360
  156.0 2.4 %collective-permute-start.28 = (bf16[768,512]{1,0:T(8,128)(2,1)S(1)}, bf16[768,512]{1,0:T(8,128)(2,1)S(1)}, u32[]{:S(2)}, u32[]{:S(2)}) collective-permute-start(bf16[768,512]{1,0:T(8,128)(2,1)S(1)} %shard_map.106), channel_id=1, source_target_pairs={{0,1},{1,0},{2,3},{3,2},{4,5},{5,4},{6,7},{7,6},{8,9},{9,8},{10,11... | collective-permute-start | bytes 2359304 | tf_op jit(solution)/shard_map/ppermute | solution.py:363
  (34 other events, 303.9 us)
Sparse Core Ops, SparseCore 0:
  13.9 67.4 all-gather.4
  83.0 28.7 all-gather.6

commit v3 on v2

--- a/solution.py
+++ b/solution.py
@@ -103,12 +103,15 @@
 
 
 def solved_kernel(leaves, width, inverse_ref, bundle_ref, *refs):
-    l = 0
-    for ref in refs:
-        for i in range(ref.shape[0] // width):
-            tile = bundle_ref[pl.ds(l * width, width), :]
-            ref[pl.ds(i * width, width), :] = jnp.dot(inverse_ref[l], tile, preferred_element_type=F32).astype(BF16)
-            l += 1
+    for l in range(leaves):
+        tile = bundle_ref[pl.ds(l * width, width), :]
+        solved = jnp.dot(inverse_ref[l], tile, preferred_element_type=F32).astype(BF16)
+        start = 0
+        for ref in refs:
+            low, high = max(l * width, start), min((l + 1) * width, start + ref.shape[0])
+            if low < high:
+                ref[pl.ds(low - start, high - low), :] = solved[low - l * width:high - l * width]
+            start += ref.shape[0]
 
 
 def node_add(acc, parent, value):
@@ -136,7 +139,7 @@
         l = first_leaf + i
         rows = pl.ds((group * leaves + i) * width, width)
         inv, tile = inv_of(i), tile_of(i)
-        m_ref[rows, :] = tile
+        m_ref[pl.ds(i * width, width), :] = tile
         solved = jnp.dot(inv, tile, preferred_element_type=F32).astype(BF16)
         km_ref[rows, :] = solved
         p = parent_ref[l]
@@ -169,7 +172,7 @@
 
 
 def early_kernel(leaves, width, nodes, core_ref, parent_ref, rhs_ref, inverse_ref, own_ref, x_ref, y_ref, swap_ref, *refs):
-    m_ref, km_ref, diag_ref, right_ref = refs[-4:]
+    m_refs, (km_ref, diag_ref, right_ref) = refs[:3], refs[3:]
     base, cols = leaves * width, own_ref.shape[1]
     for k, ref in enumerate((own_ref, x_ref, y_ref)):
         if k:
@@ -177,7 +180,7 @@
         else:
             inv = lambda i: inverse_ref[i]
         tile = lambda i: ref[pl.ds(i * width, width), :]
-        diag, right = group_work(leaves, width, k * leaves, k, tile, inv, m_ref, km_ref, rhs_ref, parent_ref, nodes, cols)
+        diag, right = group_work(leaves, width, k * leaves, k, tile, inv, m_refs[k], km_ref, rhs_ref, parent_ref, nodes, cols)
         for p in range(nodes):
             diag_ref[pl.ds(k * nodes + p, 1), :] = diag[p]
             right_ref[pl.ds(k * nodes + p, 1), :] = right[p]
@@ -211,8 +214,9 @@
         part_ref[pl.ds(l, 1), :] = row
 
 
-def sweep_kernel(leaves, width, last, ties, parent_ref, y_ref, z_ref, reduced_ref, scaling_ref, diag_ref, x_in_ref, m_ref, km_ref, m3_ref,
-                 km3_ref, *refs):
+def sweep_kernel(leaves, width, last, ties, parent_ref, y_ref, z_ref, reduced_ref, scaling_ref, diag_ref, x_in_ref, m0_ref, m1_ref, m2_ref, m3_ref,
+                 km_ref, km3_ref, *refs):
+    m_refs = (m0_ref, m1_ref, m2_ref, m3_ref)
     x_ref, part_ref = refs[ties:]
     nodes = x_in_ref.shape[0]
     whole = y_ref[...] + z_ref[...]
@@ -222,7 +226,7 @@
         acc = [zero] * nodes
         for i in range(leaves):
             l = k * leaves + i
-            mat = m_ref[pl.ds(l * width, width), :] if k < 3 else m3_ref[pl.ds(i * width, width), :]
+            mat = m_refs[k][pl.ds(i * width, width), :]
             acc = node_add(acc, parent_ref[l], rowdot(whole[l:l + 1, :], mat, False))
         groups.append(acc)
     coupled = tree(groups)
@@ -235,10 +239,15 @@
         new.append(split3(x))
     if last:
         for l in range(leaves):
-            row = image_rows(m_ref, pl.ds(l * width, width), new, parent_ref[l])
+            row = image_rows(m0_ref, pl.ds(l * width, width), new, parent_ref[l])
             part_ref[pl.ds(l, 1), :] = row
     else:
         image(leaves, width, km_ref, km3_ref, new, parent_ref, part_ref)
+
+
+def add_kernel(x_ref, y_ref, tie_ref, out_ref):
+    del tie_ref
+    out_ref[...] = x_ref[...] + y_ref[...]
 
 
 def leaf_kernel(leaves, y_ref, z_ref, rhs_ref, inverse_ref, *refs):
@@ -266,7 +275,15 @@
     )(*blocks, tie)
 
 
-def pick(places, source, ties):
+def in_vmem(x):
+    return pltpu.with_memory_space_constraint(x, pltpu.VMEM)
+
+
+def in_hbm(x):
+    return pltpu.with_memory_space_constraint(x, pltpu.HBM)
+
+
+def pick(info, places, source, ties):
     shape = jax.ShapeDtypeStruct(source.shape[1:], source.dtype)
     count = len(places)
 
@@ -275,7 +292,7 @@
         outs, token_ref = refs[first:first + count], refs[first + count]
         held, sem_in, sem_out = refs[first + count + 1:]
         token_ref[...] = jnp.zeros_like(token_ref)
-        reads = [pltpu.make_async_copy(source_ref.at[place_ref[n]], held.at[n], sem_in.at[n]) for n in range(count)]
+        reads = [pltpu.make_async_copy(source_ref.at[place_ref[places[n]]], held.at[n], sem_in.at[n]) for n in range(count)]
         writes = [pltpu.make_async_copy(held.at[n], outs[n], sem_out.at[n]) for n in range(count)]
         for read in reads:
             read.start()
@@ -292,56 +309,59 @@
         out_specs=[HB] * count + [VM],
         scratch_shapes=[pltpu.VMEM((count,) + shape.shape, shape.dtype), pltpu.SemaphoreType.DMA((count,)),
                         pltpu.SemaphoreType.DMA((count,))],
-        compiler_params=pltpu.CompilerParams(vmem_limit_bytes=48 * MIB),
+        compiler_params=pltpu.CompilerParams(vmem_limit_bytes=12 * MIB),
         cost_estimate=NO_COST,
-    )(jnp.stack(places).astype(jnp.int32), source, *ties)
-
-
-def product_kernel(leaves, width, parts, info_ref, parent_ref, m_hbm, m3_hbm, *refs):
-    count = len(parts)
-    gathered, same, other = refs[:count], refs[count:4 * count], refs[4 * count:5 * count]
-    out_hbm, m_ref, u_ref, acc_ref, sem, out_sem = refs[5 * count:]
-    cols = m_ref.shape[1]
-    base = leaves * width
-    core, column = info_ref[0], info_ref[1]
-    m_copies = [pltpu.make_async_copy(m_hbm, m_ref.at[pl.ds(0, 3 * base)], sem.at[8, 0]),
-                pltpu.make_async_copy(m3_hbm, m_ref.at[pl.ds(3 * base, base)], sem.at[8, 1])]
-    for copy in m_copies:
-        copy.start()
-    loads = {}
-    for side in range(2):
-        place = 2 * column + (core if side == 0 else 1 - core)
-        for k in range(4):
-            for h in range(count):
-                if k == 0:
-                    source = gathered[h].at[place]
-                else:
-                    source = other[h].at[pl.ds((k - 1) * parts[h], parts[h])] if side else same[h * 3 + k - 1]
-                n = side * 4 + k
-                loads[n, h] = pltpu.make_async_copy(source, u_ref.at[n, pl.ds(sum(parts[:h]), parts[h])], sem.at[n, h])
-                loads[n, h].start()
-    acc_ref[...] = jnp.zeros_like(acc_ref)
-    for copy in m_copies:
-        copy.wait()
-    for side in range(2):
-        for k in range(4):
-            n = side * 4 + k
-            for h in range(count):
-                loads[n, h].wait()
-
-            for i in range(leaves):
-                tile = m_ref[pl.ds((k * leaves + i) * width, width), :]
-                unit = u_ref[n, pl.ds(i * width, width), :]
-                value = lax.dot_general(tile, unit, (((0,), (0,)), ((), ())), preferred_element_type=F32)
-                acc_ref[side, parent_ref[k * leaves + i]] += value
-
-        where = core if side == 0 else 1 - core
+    )(info, in_hbm(source), *ties)
+
+
+def leaf_spans(width, start, rows):
+    spans = []
+    while rows:
+        size = min(rows, width - start % width)
+        spans.append((start // width, start, size))
+        start, rows = start + size, rows - size
+    return spans
+
+
+def product_kernel(leaves, width, terms, count, fresh, side, info_ref, parent_ref, *refs):
+    m_refs, sources = refs[:4], refs[4:4 + count]
+    outs, (u_ref, sem, out_sem) = refs[:-3][-2 - (side is not None):], refs[-3:]
+    acc_ref, token_ref = outs[:2]
+    work, late, slot = [], [], 0
+    for k, n, entry, offset, start, rows in terms:
+        if entry is None:
+            ref, offset = sources[n], offset
+        else:
+            copy = pltpu.make_async_copy(sources[n].at[info_ref[entry]], u_ref.at[pl.ds(slot, rows)], sem.at[len(late)])
+            copy.start()
+            late.append(copy)
+            ref, offset = u_ref, slot
+            slot += rows
+        spans = [(k, leaf, at, ref, offset + at - start, size) for leaf, at, size in leaf_spans(width, start, rows)]
+        work = work + spans if entry is not None else spans + work
+    token_ref[...] = jnp.zeros_like(token_ref)
+    if fresh:
+        acc_ref[...] = jnp.zeros_like(acc_ref)
+    for k, leaf, at, ref, offset, size in work:
+        if ref is u_ref:
+            for copy in late:
+                copy.wait()
+            late = []
+        value = lax.dot_general(m_refs[k][pl.ds(at, size), :], ref[pl.ds(offset, size), :], (((0,), (0,)), ((), ())),
+                                preferred_element_type=F32)
+        acc_ref[parent_ref[k * leaves + leaf]] += value
+    if side is not None:
+        nodes, rows, cols = acc_ref.shape
+        where = info_ref[0] if side == 0 else 1 - info_ref[0]
+        size = rows // 4
+        pieces = [(p, pl.ds(i * size, size)) for p in range(nodes) for i in range(4)]
         for half in range(2):
             @pl.when(where == half)
             def _():
-                pltpu.make_async_copy(acc_ref.at[side], out_hbm.at[:, :, pl.ds(half * cols, cols)], out_sem.at[side]).start()
-    for side in range(2):
-        pltpu.make_async_copy(acc_ref.at[side], out_hbm.at[:, :, pl.ds(0, cols)], out_sem.at[side]).wait()
+                for n, (p, at) in enumerate(pieces):
+                    pltpu.make_async_copy(acc_ref.at[p, at], outs[2].at[p, at, pl.ds(half * cols, cols)], out_sem.at[n]).start()
+        for n, (p, at) in enumerate(pieces):
+            pltpu.make_async_copy(acc_ref.at[p, at], outs[2].at[p, at, pl.ds(0, cols)], out_sem.at[n]).wait()
 
 
 def plane_body(scen, blk, link, leaf_inverse, leaf_rhs, node_rhs, node_diag, parent, tile_mask):
@@ -351,7 +371,7 @@
     planes = blk // 2
     s, b = lax.axis_index("scen"), lax.axis_index("blk")
     z, core = b // 2, b % 2
-    core1 = core.reshape(1)
+    info = jnp.stack([core] + [2 * (s ^ k) + c for c in (core, 1 - core) for k in range(scen)]).astype(jnp.int32)
 
     def over_scen(x, k):
         return lax.ppermute(x, "scen", [(i, i ^ k) for i in range(scen)])
@@ -364,7 +384,7 @@
 
     masks = tile_mask.reshape(leaves)
     total = base + width + 4 * leaves
-    cut = base // 2 + width // 2
+    cut = base // 2 + width // 8
     call = functools.partial(pl.pallas_call, cost_estimate=NO_COST, compiler_params=pltpu.CompilerParams(vmem_limit_bytes=16 * MIB))
     struct = jax.ShapeDtypeStruct
     bundle = call(
@@ -373,8 +393,8 @@
         in_specs=[SM, SM, SM, VM, VM, VM],
         out_specs=VM,
         scratch_shapes=[pltpu.VMEM((4 * leaves, cols), F32)],
-    )(core1, masks, parent, link, leaf_inverse, leaf_rhs)
-    parts = [base - base // 4, base // 4]
+    )(info, masks, parent, link, leaf_inverse, leaf_rhs)
+    parts = [5 * base // 8, 3 * base // 8]
     solved = call(
         functools.partial(solved_kernel, leaves, width),
         out_shape=[struct((rows, cols), BF16) for rows in parts],
@@ -398,15 +418,15 @@
     node_shape, part_shape = pltpu.VMEM((nodes, cols), F32), pltpu.VMEM((count, width), F32)
     early_shape, late_shape = pltpu.VMEM((3 * base, cols), BF16), pltpu.VMEM((base, cols), BF16)
     terms_shape = pltpu.VMEM((3 * nodes, cols), F32)
-    m_all, km_all, diag, right = call(
+    *m_all, km_all, diag, right = call(
         functools.partial(early_kernel, leaves, width, nodes),
-        out_shape=[early_shape, early_shape, terms_shape, terms_shape],
+        out_shape=[late_shape] * 3 + [early_shape, terms_shape, terms_shape],
         in_specs=[SM, SM] + [VM] * 6,
-        out_specs=[VM] * 4,
-        compiler_params=pltpu.CompilerParams(vmem_limit_bytes=20 * MIB),
-    )(core1, jnp.concatenate(owners[:3]), rights, leaf_inverse, bundle, bx, by, swap)
+        out_specs=[VM] * 6,
+        compiler_params=pltpu.CompilerParams(vmem_limit_bytes=16 * MIB),
+    )(info, jnp.concatenate(owners[:3]), rights, leaf_inverse, bundle, bx, by, swap)
     def to_columns(gathered, ties):
-        *blocks, token = pick([2 * (s ^ k) + core for k in (1, 2, 3)], gathered, ties)
+        *blocks, token = pick(info, [1 + k for k in (1, 2, 3)], gathered, ties)
         return [over_scen(x, k + 1) for k, x in enumerate(blocks)], token
 
     m3, km3, reduced, scaling, current, part = call(
@@ -415,57 +435,80 @@
         in_specs=[SM, SM] + [VM] * 9,
         out_specs=[VM] * 6,
         compiler_params=pltpu.CompilerParams(vmem_limit_bytes=16 * MIB),
-    )(core1, parents, rights3, node_rhs, node_diag, da, db, swap3, km_all, diag, right)
-
-    def exchange(x):
+    )(info, parents, rights3, node_rhs, node_diag, da, db, swap3, in_vmem(km_all), diag, right)
+
+    def exchange(x, tie=None):
         x = x + flip_core(x)
-        for step in range(planes.bit_length() - 2):
-            x = x + flip_z(x, 1 << step)
-        return x, flip_z(x, planes // 2)
-
-    arrived = exchange(part)
-    first, token = to_columns(gathered[0], [arrived[1]])
-    ties = [token]
+        other = flip_z(x, 1)
+        x = x + other if tie is None else call(
+            add_kernel, out_shape=pltpu.VMEM(x.shape, F32), in_specs=[VM] * 3, out_specs=VM)(x, other, tie)
+        return x, flip_z(x, 2)
+
+    def product(terms, sources, tie, acc=None, side=None, schur=None):
+        held = [term for term in terms if term[2] is not None]
+        dynamic = {term[1] for term in held}
+        extra = [tie] + ([] if acc is None else [in_vmem(acc)]) + ([] if schur is None else [schur])
+        first = 6 + len(sources)
+        aliases = {} if acc is None else {first + 1: 0}
+        if schur is not None:
+            aliases[first + 2] = 2
+        return call(
+            functools.partial(product_kernel, leaves, width, terms, len(sources), acc is None, side),
+            out_shape=[pltpu.VMEM((nodes, cols, cols), F32), pltpu.VMEM((8, 128), F32)]
+            + ([] if side is None else [struct((nodes, cols, 2 * cols), F32)]),
+            in_specs=[SM, SM] + [VM] * 4 + [HB if n in dynamic else VM for n in range(len(sources))]
+            + [VM] * (1 + (acc is not None)) + [HB] * (schur is not None),
+            out_specs=[VM, VM] + [HB] * (side is not None),
+            scratch_shapes=[pltpu.VMEM((max(sum(term[-1] for term in held), 16), cols), BF16),
+                            pltpu.SemaphoreType.DMA((max(len(held), 1),)), pltpu.SemaphoreType.DMA((4 * nodes,))],
+            input_output_aliases=aliases,
+            cost_estimate=pl.CostEstimate(flops=2 * sum(term[-1] for term in terms) * cols * cols, bytes_accessed=2 * MIB,
+                                          transcendentals=0),
+        )(info, parents, *map(in_vmem, (*m_all, m3)), *sources, *extra)
+
+    def line_terms(side):
+        return [(0, 0, 1 + side * scen, 0, 0, parts[0]), (0, 1, 1 + side * scen, 0, parts[0], parts[1])]
+
+    own = [in_hbm(x) for x in gathered]
+    first, token = to_columns(gathered[0], [part])
+    arrived = exchange(part, token)
+    ties = []
     for sweep in range(ITERS):
         last = sweep == ITERS - 1
         current, part = call(
             functools.partial(sweep_kernel, leaves, width, last, len(ties)),
             out_shape=[struct((nodes, cols), F32), pltpu.VMEM((leaves, width), F32)] if last else [node_shape, part_shape],
-            in_specs=[SM] + [VM] * 10 + [VM if tie.dtype == F32 else HB for tie in ties],
+            in_specs=[SM] + [VM] * 12 + [VM if tie.dtype == F32 else HB for tie in ties],
             out_specs=[VM] * 2,
             compiler_params=pltpu.CompilerParams(vmem_limit_bytes=16 * MIB),
-        )(parents, *arrived, reduced, scaling, node_diag, current, m_all, km_all, m3, km3, *ties)
-        arrived = exchange(part)
+        )(parents, *arrived, reduced, scaling, node_diag, current, *map(in_vmem, (*m_all, m3, km_all, km3)), *ties)
         ties = []
-        if sweep == 1:
-            ties = first
-        elif sweep == 2:
-            others = [flip_core(join(first, part))]
+        if sweep == 2:
             second, token = to_columns(gathered[1], [part])
+            arrived = exchange(part, token)
+            others = [flip_core(join(first, arrived[0]))]
+            terms = line_terms(0) + [(k, 1 + k, None, 0, 0, parts[0]) for k in (1, 2, 3)]
+            acc0, token = product(terms, own + first, arrived[0])
             ties = [token]
-    ties = others + second
+        elif last:
+            terms = line_terms(1) + [(k, 2, None, (k - 1) * parts[0], 0, parts[0]) for k in (1, 2, 3)]
+            acc1, token = product(terms, own + others, part)
+            arrived = exchange(part, token)
+            others = [flip_core(join(second, arrived[0]))]
+            terms = [(k, k - 1, None, 0, parts[0], parts[1]) for k in (1, 2, 3)]
+            unused, token, schur = product(terms, second, arrived[0], acc0, 0)
+            ties = [token]
+        else:
+            arrived = exchange(part)
     leaf_solution = call(
         functools.partial(leaf_kernel, leaves),
         out_shape=struct((leaves, width), F32),
-        in_specs=[VM] * 4 + [HB] * len(ties),
+        in_specs=[VM] * 4 + [VM if tie.dtype == F32 else HB for tie in ties],
         out_specs=VM,
     )(*arrived, leaf_rhs, leaf_inverse, *ties)
 
-    others.append(flip_core(join(second, leaf_solution)))
-    schur = call(
-        functools.partial(product_kernel, leaves, width, parts),
-        out_shape=struct((nodes, cols, 2 * cols), F32),
-        in_specs=[SM, SM] + [HB] * (2 + 5 * len(parts)),
-        out_specs=HB,
-        scratch_shapes=[
-            pltpu.VMEM((scen * base, cols), BF16),
-            pltpu.VMEM((8, base, cols), BF16),
-            pltpu.VMEM((2, nodes, cols, cols), F32),
-            pltpu.SemaphoreType.DMA((9, len(parts))),
-            pltpu.SemaphoreType.DMA((2,)),
-        ],
-        compiler_params=pltpu.CompilerParams(vmem_limit_bytes=32 * MIB),
-    )(jnp.stack([core, s]).astype(jnp.int32), parents, m_all, m3, *gathered, *first, *second, *others)
+    terms = [(k, 0, None, (k - 1) * parts[1], parts[0], parts[1]) for k in (1, 2, 3)]
+    unused, token, schur = product(terms, others, leaf_solution, acc1, 1, schur)
     return current, leaf_solution, schur
 
 

time: 178 us -> 165 us (0.927)
  waiting for transfers between devices: 78.5 us -> 60 us
  Pallas kernels: 33.6 us -> 41.9 us
  local copies, waits for them, and re-layouts: 17 us -> 10.2 us
  starting transfers between devices: 32.1 us -> 37.8 us
    ppermute x10, waiting for transfers between devices: 27 us -> 14.6 us  [flip_z(): return lax.ppermute(x, 'blk', [(i, i ^ 2 * k) for i in range(blk)])]
    ppermute x10, waiting for transfers between devices: 43.3 us -> 35.2 us  [over_scen(): return lax.ppermute(x, 'scen', [(i, i ^ k) for i in range(scen)])]
    pallas_call x2 -> x8, Pallas kernels: 13.8 us -> 19.6 us  [the longest x4 15.8 us: product(): call(functools.partial(product_kernel, leaves, width, terms, len(sources)...]
    ppermute x10, starting transfers between devices: 16.7 us -> 22.2 us  [flip_z(): return lax.ppermute(x, 'blk', [(i, i ^ 2 * k) for i in range(blk)])]
    unnamed x70 -> x58, local copies, waits for them, and re-layouts: 14.7 us -> 9.93 us
    pallas_call x2, Pallas kernels: 3.25 us -> 5.38 us  [pick(): pl.pallas_call(kernel, out_shape=[shape] * count + [jax.ShapeDtypeStruct(...]
  transfers between devices with their start and end apart: 31 -> 31, of which waited for: 20 -> 17; matrix products, arithmetic and copies ran while one was open for 2% -> 0% of each run, Pallas kernels for 12% -> 21%
where the time goes in v3:
time: 165 us
  waiting for transfers between devices  60 us (36%)
  Pallas kernels  41.9 us (25%)
  starting transfers between devices  37.8 us (23%)
  between operations  14.6 us (9%)
  local copies, waits for them, and re-layouts  10.2 us (6%)
    ppermute x10, waiting for transfers between devices, over_scen(): return lax.ppermute(x, 'scen', [(i, i ^ k) for i in range(scen)])  35.2 us
    ppermute x10, starting transfers between devices, flip_z(): return lax.ppermute(x, 'blk', [(i, i ^ 2 * k) for i in range(blk)])  22.2 us
    pallas_call x4, Pallas kernels, product(): call(functools.partial(product_kernel, leaves, width, terms, len(sources)...  15.8 us
    ppermute x10, starting transfers between devices, over_scen(): return lax.ppermute(x, 'scen', [(i, i ^ k) for i in range(scen)])  15 us
    ppermute x10, waiting for transfers between devices, flip_z(): return lax.ppermute(x, 'blk', [(i, i ^ 2 * k) for i in range(blk)])  14.6 us
    unnamed x58, local copies, waits for them, and re-layouts  9.93 us
    pallas_call x4, Pallas kernels, plane_body(): call(functools.partial(sweep_kernel, leaves, width, last, len(ties)), out...  9 us
    ppermute x9, waiting for transfers between devices, flip_core(): return lax.ppermute(x, 'blk', [(i, i ^ 1) for i in range(blk)])  8.61 us
  transfers between devices with their start and end apart: 31, of which 17 were waited for; matrix products, arithmetic and copies ran while one was open for 0% of the time, Pallas kernels for 21%

profile of v3, /device:TPU:0, one launch (start us, length us, event | category | flops | bytes accessed | tf_op | source)
XLA Modules:
  0.0 164.9 jit_solution(11012641411583113871)
XLA Ops:
  14.7 3.0 %collective-permute-start.1 = (bf16[1296,512]{1,0:T(8,128)(2,1)S(1)}, bf16[1296,512]{1,0:T(8,128)(2,1)S(1)}, u32[]{:S(2)}, u32[]{:S(2)}) collective-permute-start(bf16[1296,512]{1,0:T(8,128)(2,1)S(1)} %shard_map.94.own_ref.bundle_ref), channel_id=1, source_target_pairs={{0,16},{8,24},{16,0},{24,8},{1,17},{9,25},{17,1},{25,9},{2,18},{10... | collective-permute-start | bytes 3981320 | tf_op jit(solution)/shard_map/ppermute | solution.py:377
  19.2 27.6 %collective-permute-done.1.y_ref = bf16[1296,512]{1,0:T(8,128)(2,1)S(1)} collective-permute-done((bf16[1296,512]{1,0:T(8,128)(2,1)S(1)}, bf16[1296,512]{1,0:T(8,128)(2,1)S(1)}, u32[]{:S(2)}, u32[]{:S(2)}) %collective-permute-start.1) | collective-permute-done | bytes 1327136 | tf_op jit(solution)/shard_map/ppermute | solution.py:377
  46.9 1.8 %collective-permute-start.2 = (bf16[752,512]{1,0:T(8,128)(2,1)S(1)}, bf16[752,512]{1,0:T(8,128)(2,1)S(1)}, u32[]{:S(2)}, u32[]{:S(2)}) collective-permute-start(bf16[752,512]{1,0:T(8,128)(2,1)S(1)} %slice.93), channel_id=1, source_target_pairs={{0,8},{8,0},{16,24},{24,16},{1,9},{9,1},{17,25},{25,17},{2,10},{10... | collective-permute-start | bytes 2310152 | tf_op jit(solution)/shard_map/ppermute | solution.py:377
  48.7 1.6 collective-permute-start.3
  52.4 3.8 %shard_map.95 = (bf16[1024,512]{1,0:T(8,128)(2,1)S(1)}, bf16[1024,512]{1,0:T(8,128)(2,1)S(1)}, bf16[1024,512]{1,0:T(8,128)(2,1)S(1)}, bf16[3072,512]{1,0:T(8,128...) custom-call(s32[9]{0:T(128)S(1)} %stack.39.core_ref.place_ref.info_ref, s32[12]{0:T(128)S(1)} %pad_add_fusion.1.parent_ref, ...), custom_call_target="tpu_custom_call" | custom-call | tf_op jit(solution)/shard_map/pallas_call | solution.py:421
  59.2 6.3 %collective-permute-done.2.db_ref = bf16[752,512]{1,0:T(8,128)(2,1)S(1)} collective-permute-done((bf16[752,512]{1,0:T(8,128)(2,1)S(1)}, bf16[752,512]{1,0:T(8,128)(2,1)S(1)}, u32[]{:S(2)}, u32[]{:S(2)}) %collective-permute-start.2) | collective-permute-done | bytes 770080 | tf_op jit(solution)/shard_map/ppermute | solution.py:377
  67.1 2.9 %shard_map.96 = (bf16[1024,512]{1,0:T(8,128)(2,1)S(1)}, bf16[1024,512]{1,0:T(8,128)(2,1)S(1)}, f32[2,512]{1,0:T(2,128)S(1)}, f32[2,512]{1,0:T(2,128)S(1)}, f32[2,512]{1,0:T(2,128)S(1)}, /*index=5*/f32[16,256]{1,0:T(8,128)S(1)}) custom-call(s32[9]{0:T(128)S(1)} %stack.39.core_ref.place_ref.info_ref, s32[16]{0:T(128)S(1)} %pad_add_fusion.parent_ref, ...), custom_call_target="tpu_custom_call" | custom-call | tf_op jit(solution)/shard_map/pallas_call | solution.py:432
  72.8 3.2 %shard_map.98 = (bf16[640,512]{1,0:T(8,128)(2,1)}, bf16[640,512]{1,0:T(8,128)(2,1)}, bf16[640,512]{1,0:T(8,128)(2,1)}, f32[8,128]{1,0:T(8,128)S(1)}) custom-call(s32[9]{0:T(128)S(1)} %stack.39.core_ref.place_ref.info_ref, bf16[8,640,512]{2,1,0:T(8,128)(2,1)} %bitcast.13, f32[16,256]{1,0:T(8,128)S(1)} %get-tuple-element.43.refs_0_), custom_call_target="tpu_custom_call" | custom-call | tf_op jit(solution)/shard_map/pallas_call | solution.py:305
  81.5 3.0 %collective-permute-done.7.y_ref = f32[16,256]{1,0:T(8,128)S(1)} collective-permute-done((f32[16,256]{1,0:T(8,128)S(1)}, f32[16,256]{1,0:T(8,128)S(1)}, u32[]{:S(2)}, u32[]{:S(2)}) %collective-permute-start.7) | collective-permute-done | bytes 16416 | tf_op jit(solution)/shard_map/ppermute | solution.py:380
  84.5 2.0 %collective-permute-start.8 = (f32[16,256]{1,0:T(8,128)S(1)}, f32[16,256]{1,0:T(8,128)S(1)}, u32[]{:S(2)}, u32[]{:S(2)}) collective-permute-start(f32[16,256]{1,0:T(8,128)S(1)} %shard_map.99.y_ref), channel_id=1, source_target_pairs={{0,4},{1,5},{2,6},{3,7},{4,0},{5,1},{6,2},{7,3},{8,12},{9,13},{10,... | collective-permute-start | bytes 49160 | tf_op jit(solution)/shard_map/ppermute | solution.py:380
  86.5 3.2 %collective-permute-done.8.z_ref = f32[16,256]{1,0:T(8,128)S(1)} collective-permute-done((f32[16,256]{1,0:T(8,128)S(1)}, f32[16,256]{1,0:T(8,128)S(1)}, u32[]{:S(2)}, u32[]{:S(2)}) %collective-permute-start.8) | collective-permute-done | bytes 16416 | tf_op jit(solution)/shard_map/ppermute | solution.py:380
  89.7 2.4 %shard_map.100 = (f32[2,512]{1,0:T(2,128)S(1)}, f32[16,256]{1,0:T(8,128)S(1)}) custom-call(s32[16]{0:T(128)S(1)} %pad_add_fusion.parent_ref, f32[16,256]{1,0:T(8,128)S(1)} %shard_map.99.y_ref, f32[16,256]{1,0:T(8,128)S(1)} %collective-permute-done.8.z_ref, f32[2,512]{1,0:T(2,128)S(1)} %get-tuple-element.46.reduced_ref, ...), custom_call_target="tpu_custom_call" | custom-call | tf_op jit(solution)/shard_map/pallas_call | solution.py:478
  94.9 2.6 %collective-permute-done.10 = f32[16,256]{1,0:T(8,128)S(1)} collective-permute-done((f32[16,256]{1,0:T(8,128)S(1)}, f32[16,256]{1,0:T(8,128)S(1)}, u32[]{:S(2)}, u32[]{:S(2)}) %collective-permute-start.10) | collective-permute-done | bytes 16416 | tf_op jit(solution)/shard_map/ppermute | solution.py:380
  97.5 3.1 %collective-permute-start.11 = (f32[16,256]{1,0:T(8,128)S(1)}, f32[16,256]{1,0:T(8,128)S(1)}, u32[]{:S(2)}, u32[]{:S(2)}) collective-permute-start(f32[16,256]{1,0:T(8,128)S(1)} %add.84.y_ref), channel_id=1, source_target_pairs={{0,4},{1,5},{2,6},{3,7},{4,0},{5,1},{6,2},{7,3},{8,12},{9,13},{10,... | collective-permute-start | bytes 49160 | tf_op jit(solution)/shard_map/ppermute | solution.py:380
  100.6 2.3 %collective-permute-done.11.z_ref = f32[16,256]{1,0:T(8,128)S(1)} collective-permute-done((f32[16,256]{1,0:T(8,128)S(1)}, f32[16,256]{1,0:T(8,128)S(1)}, u32[]{:S(2)}, u32[]{:S(2)}) %collective-permute-start.11) | collective-permute-done | bytes 16416 | tf_op jit(solution)/shard_map/ppermute | solution.py:380
  102.9 2.4 %shard_map.101 = (f32[2,512]{1,0:T(2,128)S(1)}, f32[16,256]{1,0:T(8,128)S(1)}) custom-call(s32[16]{0:T(128)S(1)} %pad_add_fusion.parent_ref, f32[16,256]{1,0:T(8,128)S(1)} %add.84.y_ref, f32[16,256]{1,0:T(8,128)S(1)} %collective-permute-done.11.z_ref, f32[2,512]{1,0:T(2,128)S(1)} %get-tuple-element.46.reduced_ref, ...), custom_call_target="tpu_custom_call" | custom-call | tf_op jit(solution)/shard_map/pallas_call | solution.py:478
  106.6 2.1 %collective-permute-start.13 = (f32[16,256]{1,0:T(8,128)S(1)}, f32[16,256]{1,0:T(8,128)S(1)}, u32[]{:S(2)}, u32[]{:S(2)}) collective-permute-start(f32[16,256]{1,0:T(8,128)S(1)} %add.85), channel_id=1, source_target_pairs={{0,2},{1,3},{2,0},{3,1},{4,6},{5,7},{6,4},{7,5},{8,10},{9,11},{10,... | collective-permute-start | bytes 49160 | tf_op jit(solution)/shard_map/ppermute | solution.py:380
  108.7 1.7 %collective-permute-done.13 = f32[16,256]{1,0:T(8,128)S(1)} collective-permute-done((f32[16,256]{1,0:T(8,128)S(1)}, f32[16,256]{1,0:T(8,128)S(1)}, u32[]{:S(2)}, u32[]{:S(2)}) %collective-permute-start.13) | collective-permute-done | bytes 16416 | tf_op jit(solution)/shard_map/ppermute | solution.py:380
  110.4 3.5 %collective-permute-start.14 = (f32[16,256]{1,0:T(8,128)S(1)}, f32[16,256]{1,0:T(8,128)S(1)}, u32[]{:S(2)}, u32[]{:S(2)}) collective-permute-start(f32[16,256]{1,0:T(8,128)S(1)} %add.86.y_ref), channel_id=1, source_target_pairs={{0,4},{1,5},{2,6},{3,7},{4,0},{5,1},{6,2},{7,3},{8,12},{9,13},{10,... | collective-permute-start | bytes 49160 | tf_op jit(solution)/shard_map/ppermute | solution.py:380
  113.9 1.7 %collective-permute-done.14.z_ref = f32[16,256]{1,0:T(8,128)S(1)} collective-permute-done((f32[16,256]{1,0:T(8,128)S(1)}, f32[16,256]{1,0:T(8,128)S(1)}, u32[]{:S(2)}, u32[]{:S(2)}) %collective-permute-start.14) | collective-permute-done | bytes 16416 | tf_op jit(solution)/shard_map/ppermute | solution.py:380
  115.6 2.4 %shard_map.102 = (f32[2,512]{1,0:T(2,128)S(1)}, f32[16,256]{1,0:T(8,128)S(1)}) custom-call(s32[16]{0:T(128)S(1)} %pad_add_fusion.parent_ref, f32[16,256]{1,0:T(8,128)S(1)} %add.86.y_ref, f32[16,256]{1,0:T(8,128)S(1)} %collective-permute-done.14.z_ref, f32[2,512]{1,0:T(2,128)S(1)} %get-tuple-element.46.reduced_ref, ...), custom_call_target="tpu_custom_call" | custom-call | tf_op jit(solution)/shard_map/pallas_call | solution.py:478
  119.3 2.0 %collective-permute-start.16 = (f32[16,256]{1,0:T(8,128)S(1)}, f32[16,256]{1,0:T(8,128)S(1)}, u32[]{:S(2)}, u32[]{:S(2)}) collective-permute-start(f32[16,256]{1,0:T(8,128)S(1)} %add.87.x_ref), channel_id=1, source_target_pairs={{0,2},{1,3},{2,0},{3,1},{4,6},{5,7},{6,4},{7,5},{8,10},{9,11},{10,... | collective-permute-start | bytes 49160 | tf_op jit(solution)/shard_map/ppermute | solution.py:380
  121.3 2.2 %shard_map.103 = (bf16[384,512]{1,0:T(8,128)(2,1)S(1)}, bf16[384,512]{1,0:T(8,128)(2,1)S(1)}, bf16[384,512]{1,0:T(8,128)(2,1)S(1)}, f32[8,128]{1,0:T(8,128)S(1)}) custom-call(s32[9]{0:T(128)S(1)} %stack.39.core_ref.place_ref.info_ref, bf16[8,384,512]{2,1,0:T(8,128)(2,1)} %bitcast.16, f32[16,256]{1,0:T(8,128)S(1)} %get-tuple-element.58.refs_0_), custom_call_target="tpu_custom_call" | custom-call | tf_op jit(solution)/shard_map/pallas_call | solution.py:305
  123.5 1.8 %shard_map.107 = bf16[1920,512]{1,0:T(8,128)(2,1)S(1)} custom-call(bf16[640,512]{1,0:T(8,128)(2,1)} %collective-permute-done.18.refs_6_.refs_0_, bf16[640,512]{1,0:T(8,128)(2,1)} %collective-permute-done.19.refs_7_.refs_1_, bf16[640,512]{1,0:T(8,128)(2,1)} %collective-permute-done.20.refs_8_.refs_2_, f32[16,256]{1,0:T(8,128)S(1)} %shard_map.104.refs_9_.y_ref.refs_3_), custom_call_target="tpu_custom_call" | custom-call | tf_op jit(solution)/shard_map/pallas_call | solution.py:268
  125.4 1.9 %collective-permute-start.25 = (bf16[384,512]{1,0:T(8,128)(2,1)S(1)}, bf16[384,512]{1,0:T(8,128)(2,1)S(1)}, u32[]{:S(2)}, u32[]{:S(2)}) collective-permute-start(bf16[384,512]{1,0:T(8,128)(2,1)S(1)} %get-tuple-element.69), channel_id=1, source_target_pairs={{0,8},{8,0},{16,24},{24,16},{1,9},{9,1},{17,25},{25,17},{2,10},{10... | collective-permute-start | bytes 1179656 | tf_op jit(solution)/shard_map/ppermute | solution.py:377
  128.9 2.9 %collective-permute-start.17 = (f32[16,256]{1,0:T(8,128)S(1)}, f32[16,256]{1,0:T(8,128)S(1)}, u32[]{:S(2)}, u32[]{:S(2)}) collective-permute-start(f32[16,256]{1,0:T(8,128)S(1)} %shard_map.104.refs_9_.y_ref.refs_3_), channel_id=1, source_target_pairs={{0,4},{1,5},{2,6},{3,7},{4,0},{5,1},{6,2},{7,3},{8,12},{9,13},{10,... | collective-permute-start | bytes 49160 | tf_op jit(solution)/shard_map/ppermute | solution.py:380
  131.9 5.1 %shard_map.105 = (f32[2,512,512]{2,1,0:T(8,128)S(1)}, f32[8,128]{1,0:T(8,128)S(1)}) custom-call(s32[9]{0:T(128)S(1)} %stack.39.core_ref.place_ref.info_ref, s32[16]{0:T(128)S(1)} %pad_add_fusion.parent_ref, bf16[1024,512]{1,0:T(8,128)(2,1)S(1)} %copy-done.2, bf16[1024,512]{1,0:T(8,128)(2,1)S(1)} %copy-done.5, bf16[1024,512]{1,0:T(8,128)(2,1)S(1)} %copy-done.8, ...), custom_call_target="tpu_custom_call" | custom-call | flops 1543503872 | bytes 2097152 | tf_op jit(solution)/shard_map/pallas_call | solution.py:455
  137.0 1.8 %shard_map.106 = (f32[2,512]{1,0:T(2,128)}, f32[4,256]{1,0:T(4,128)S(1)}) custom-call(s32[16]{0:T(128)S(1)} %pad_add_fusion.parent_ref, f32[16,256]{1,0:T(8,128)S(1)} %shard_map.104.refs_9_.y_ref.refs_3_, f32[16,256]{1,0:T(8,128)S(1)} %collective-permute-done.17.z_ref, f32[2,512]{1,0:T(2,128)S(1)} %get-tuple-element.46.reduced_ref, ...), custom_call_target="tpu_custom_call" | custom-call | tf_op jit(solution)/shard_map/pallas_call | solution.py:478
  141.4 4.2 %shard_map.108 = (f32[2,512,512]{2,1,0:T(8,128)S(1)}, f32[8,128]{1,0:T(8,128)S(1)}) custom-call(s32[9]{0:T(128)S(1)} %stack.39.core_ref.place_ref.info_ref, s32[16]{0:T(128)S(1)} %pad_add_fusion.parent_ref, bf16[1024,512]{1,0:T(8,128)(2,1)S(1)} %copy-done.2, bf16[1024,512]{1,0:T(8,128)(2,1)S(1)} %copy-done.5, bf16[1024,512]{1,0:T(8,128)(2,1)S(1)} %copy-done.8, ...), custom_call_target="tpu_custom_call" | custom-call | flops 1543503872 | bytes 2097152 | tf_op jit(solution)/shard_map/pallas_call | solution.py:455
  147.0 3.0 %collective-permute-start.24 = (f32[4,256]{1,0:T(4,128)S(1)}, f32[4,256]{1,0:T(4,128)S(1)}, u32[]{:S(2)}, u32[]{:S(2)}) collective-permute-start(f32[4,256]{1,0:T(4,128)S(1)} %shard_map.109.refs_7_.y_ref.refs_3_), channel_id=1, source_target_pairs={{0,4},{1,5},{2,6},{3,7},{4,0},{5,1},{6,2},{7,3},{8,12},{9,13},{10,... | collective-permute-start | bytes 12296 | tf_op jit(solution)/shard_map/ppermute | solution.py:380
  150.0 2.9 %shard_map.110 = (f32[2,512,512]{2,1,0:T(8,128)S(1)}, f32[8,128]{1,0:T(8,128)S(1)}, f32[2,512,1024]{2,1,0:T(8,128)}) custom-call(s32[9]{0:T(128)S(1)} %stack.39.core_ref.place_ref.info_ref, s32[16]{0:T(128)S(1)} %pad_add_fusion.parent_ref, bf16[1024,512]{1,0:T(8,128)(2,1)S(1)} %copy-done.2, ...), custom_call_target="tpu_custom_call", output_to_operand_aliasing={{0}: (10, {})} | custom-call | flops 603979776 | bytes 2097152 | tf_op jit(solution)/shard_map/pallas_call | solution.py:455
  154.5 3.6 %shard_map.113 = (f32[2,512,512]{2,1,0:T(8,128)S(1)}, f32[8,128]{1,0:T(8,128)}, f32[2,512,1024]{2,1,0:T(8,128)}) custom-call(s32[9]{0:T(128)S(1)} %stack.39.core_ref.place_ref.info_ref, s32[16]{0:T(128)S(1)} %pad_add_fusion.parent_ref, bf16[1024,512]{1,0:T(8,128)(2,1)S(1)} %copy-done.2, ...), custom_call_target="tpu_custom_call", output_to_operand_aliasing={{0}: (8, {}), {2}: (9, {})} | custom-call | flops 603979776 | bytes 2097152 | tf_op jit(solution)/shard_map/pallas_call | solution.py:455
  (137 shorter events, 36.3 us)
Async XLA Ops:
  7.2 65.6 %all-gather.5.cloned.1.call-start = ((), (), s32[]{:S(2)}) async-start(), calls=%async_computation | async-start | bytes 5898240 | tf_op jit(solution)/shard_map/all_gather | solution.py:404
  13.9 107.4 %all-gather.7.cloned.1.call-start = ((), (), s32[]{:S(2)}) async-start(), calls=%async_computation.1 | async-start | bytes 3538944 | tf_op jit(solution)/shard_map/all_gather | solution.py:404
  14.7 37.7 %copy-start.18 = (bf16[4,256,256]{2,1,0:T(8,128)(2,1)S(1)}, bf16[4,256,256]{2,1,0:T(8,128)(2,1)}, u32[]{:S(2)}) copy-start(bf16[4,256,256]{2,1,0:T(8,128)(2,1)} %inverse_ref.7) | copy-start | bytes 1572868
  14.7 32.2 %collective-permute-start.1 = (bf16[1296,512]{1,0:T(8,128)(2,1)S(1)}, bf16[1296,512]{1,0:T(8,128)(2,1)S(1)}, u32[]{:S(2)}, u32[]{:S(2)}) collective-permute-start(bf16[1296,512]{1,0:T(8,128)(2,1)S(1)} %shard_map.94.own_ref.bundle_ref), channel_id=1, source_target_pairs={{0,16},{8,24},{16,0},{24,8},{1,17},{9,25},{17,1},{25,9},{2,18},{10... | collective-permute-start | bytes 3981320 | tf_op jit(solution)/shard_map/ppermute | solution.py:377
  17.7 31.0 %collective-permute-start = (bf16[1296,512]{1,0:T(8,128)(2,1)S(1)}, bf16[1296,512]{1,0:T(8,128)(2,1)S(1)}, u32[]{:S(2)}, u32[]{:S(2)}) collective-permute-start(bf16[1296,512]{1,0:T(8,128)(2,1)S(1)} %shard_map.94.own_ref.bundle_ref), channel_id=1, source_target_pairs={{0,8},{8,0},{16,24},{24,16},{1,9},{9,1},{17,25},{25,17},{2,10},{10... | collective-permute-start | bytes 3981320 | tf_op jit(solution)/shard_map/ppermute | solution.py:377
  46.9 18.5 %collective-permute-start.2 = (bf16[752,512]{1,0:T(8,128)(2,1)S(1)}, bf16[752,512]{1,0:T(8,128)(2,1)S(1)}, u32[]{:S(2)}, u32[]{:S(2)}) collective-permute-start(bf16[752,512]{1,0:T(8,128)(2,1)S(1)} %slice.93), channel_id=1, source_target_pairs={{0,8},{8,0},{16,24},{24,16},{1,9},{9,1},{17,25},{25,17},{2,10},{10... | collective-permute-start | bytes 2310152 | tf_op jit(solution)/shard_map/ppermute | solution.py:377
  48.7 17.1 %collective-permute-start.3 = (bf16[544,512]{1,0:T(8,128)(2,1)S(1)}, bf16[544,512]{1,0:T(8,128)(2,1)S(1)}, u32[]{:S(2)}, u32[]{:S(2)}) collective-permute-start(bf16[544,512]{1,0:T(8,128)(2,1)S(1)} %slice.105), channel_id=1, source_target_pairs={{0,16},{8,24},{16,0},{24,8},{1,17},{9,25},{17,1},{25,9},{2,18},{10... | collective-permute-start | bytes 1671176 | tf_op jit(solution)/shard_map/ppermute | solution.py:377
  50.4 2.0 %collective-permute-start.5 = (bf16[512,512]{1,0:T(8,128)(2,1)S(1)}, bf16[512,512]{1,0:T(8,128)(2,1)S(1)}, u32[]{:S(2)}, u32[]{:S(2)}) collective-permute-start(bf16[512,512]{1,0:T(8,128)(2,1)S(1)} %pad_maximum_fusion), channel_id=1, source_target_pairs={{0,1},{1,0},{2,3},{3,2},{4,5},{5,4},{6,7},{7,6},{8,9},{9,8},{10,11... | collective-permute-start | bytes 1572872 | tf_op jit(solution)/shard_map/ppermute | solution.py:383
  65.5 1.6 collective-permute-start.4
  76.0 47.5 %collective-permute-start.18 = (bf16[640,512]{1,0:T(8,128)(2,1)}, bf16[640,512]{1,0:T(8,128)(2,1)}, u32[]{:S(2)}, u32[]{:S(2)}) collective-permute-start(bf16[640,512]{1,0:T(8,128)(2,1)} %get-tuple-element.62), channel_id=1, source_target_pairs={{0,8},{8,0},{16,24},{24,16},{1,9},{9,1},{17,25},{25,17},{2,10},{10... | collective-permute-start | bytes 1966088 | tf_op jit(solution)/shard_map/ppermute | solution.py:377
  77.6 45.9 %collective-permute-start.19 = (bf16[640,512]{1,0:T(8,128)(2,1)}, bf16[640,512]{1,0:T(8,128)(2,1)}, u32[]{:S(2)}, u32[]{:S(2)}) collective-permute-start(bf16[640,512]{1,0:T(8,128)(2,1)} %get-tuple-element.63), channel_id=1, source_target_pairs={{0,16},{8,24},{16,0},{24,8},{1,17},{9,25},{17,1},{25,9},{2,18},{10... | collective-permute-start | bytes 1966088 | tf_op jit(solution)/shard_map/ppermute | solution.py:377
  79.0 44.5 %collective-permute-start.20 = (bf16[640,512]{1,0:T(8,128)(2,1)}, bf16[640,512]{1,0:T(8,128)(2,1)}, u32[]{:S(2)}, u32[]{:S(2)}) collective-permute-start(bf16[640,512]{1,0:T(8,128)(2,1)} %get-tuple-element.64), channel_id=1, source_target_pairs={{0,24},{8,16},{16,8},{24,0},{1,25},{9,17},{17,9},{25,1},{2,26},{10... | collective-permute-start | bytes 1966088 | tf_op jit(solution)/shard_map/ppermute | solution.py:377
  79.6 1.2 collective-permute-start.6
  80.8 3.7 %collective-permute-start.7 = (f32[16,256]{1,0:T(8,128)S(1)}, f32[16,256]{1,0:T(8,128)S(1)}, u32[]{:S(2)}, u32[]{:S(2)}) collective-permute-start(f32[16,256]{1,0:T(8,128)S(1)} %add.82.x_ref), channel_id=1, source_target_pairs={{0,2},{1,3},{2,0},{3,1},{4,6},{5,7},{6,4},{7,5},{8,10},{9,11},{10,... | collective-permute-start | bytes 49160 | tf_op jit(solution)/shard_map/ppermute | solution.py:380
  84.5 5.2 %collective-permute-start.8 = (f32[16,256]{1,0:T(8,128)S(1)}, f32[16,256]{1,0:T(8,128)S(1)}, u32[]{:S(2)}, u32[]{:S(2)}) collective-permute-start(f32[16,256]{1,0:T(8,128)S(1)} %shard_map.99.y_ref), channel_id=1, source_target_pairs={{0,4},{1,5},{2,6},{3,7},{4,0},{5,1},{6,2},{7,3},{8,12},{9,13},{10,... | collective-permute-start | bytes 49160 | tf_op jit(solution)/shard_map/ppermute | solution.py:380
  92.1 1.2 collective-permute-start.9
  93.4 4.1 %collective-permute-start.10 = (f32[16,256]{1,0:T(8,128)S(1)}, f32[16,256]{1,0:T(8,128)S(1)}, u32[]{:S(2)}, u32[]{:S(2)}) collective-permute-start(f32[16,256]{1,0:T(8,128)S(1)} %add.83), channel_id=1, source_target_pairs={{0,2},{1,3},{2,0},{3,1},{4,6},{5,7},{6,4},{7,5},{8,10},{9,11},{10,... | collective-permute-start | bytes 49160 | tf_op jit(solution)/shard_map/ppermute | solution.py:380
  97.5 5.4 %collective-permute-start.11 = (f32[16,256]{1,0:T(8,128)S(1)}, f32[16,256]{1,0:T(8,128)S(1)}, u32[]{:S(2)}, u32[]{:S(2)}) collective-permute-start(f32[16,256]{1,0:T(8,128)S(1)} %add.84.y_ref), channel_id=1, source_target_pairs={{0,4},{1,5},{2,6},{3,7},{4,0},{5,1},{6,2},{7,3},{8,12},{9,13},{10,... | collective-permute-start | bytes 49160 | tf_op jit(solution)/shard_map/ppermute | solution.py:380
  105.3 1.2 collective-permute-start.12
  106.6 3.8 %collective-permute-start.13 = (f32[16,256]{1,0:T(8,128)S(1)}, f32[16,256]{1,0:T(8,128)S(1)}, u32[]{:S(2)}, u32[]{:S(2)}) collective-permute-start(f32[16,256]{1,0:T(8,128)S(1)} %add.85), channel_id=1, source_target_pairs={{0,2},{1,3},{2,0},{3,1},{4,6},{5,7},{6,4},{7,5},{8,10},{9,11},{10,... | collective-permute-start | bytes 49160 | tf_op jit(solution)/shard_map/ppermute | solution.py:380
  110.4 5.2 %collective-permute-start.14 = (f32[16,256]{1,0:T(8,128)S(1)}, f32[16,256]{1,0:T(8,128)S(1)}, u32[]{:S(2)}, u32[]{:S(2)}) collective-permute-start(f32[16,256]{1,0:T(8,128)S(1)} %add.86.y_ref), channel_id=1, source_target_pairs={{0,4},{1,5},{2,6},{3,7},{4,0},{5,1},{6,2},{7,3},{8,12},{9,13},{10,... | collective-permute-start | bytes 49160 | tf_op jit(solution)/shard_map/ppermute | solution.py:380
  118.0 1.2 collective-permute-start.15
  119.3 4.2 %collective-permute-start.16 = (f32[16,256]{1,0:T(8,128)S(1)}, f32[16,256]{1,0:T(8,128)S(1)}, u32[]{:S(2)}, u32[]{:S(2)}) collective-permute-start(f32[16,256]{1,0:T(8,128)S(1)} %add.87.x_ref), channel_id=1, source_target_pairs={{0,2},{1,3},{2,0},{3,1},{4,6},{5,7},{6,4},{7,5},{8,10},{9,11},{10,... | collective-permute-start | bytes 49160 | tf_op jit(solution)/shard_map/ppermute | solution.py:380
  125.3 16.1 %collective-permute-start.23 = (bf16[1920,512]{1,0:T(8,128)(2,1)S(1)}, bf16[1920,512]{1,0:T(8,128)(2,1)S(1)}, u32[]{:S(2)}, u32[]{:S(2)}) collective-permute-start(bf16[1920,512]{1,0:T(8,128)(2,1)S(1)} %shard_map.107), channel_id=1, source_target_pairs={{0,1},{1,0},{2,3},{3,2},{4,5},{5,4},{6,7},{7,6},{8,9},{9,8},{10,11... | collective-permute-start | bytes 5898248 | tf_op jit(solution)/shard_map/ppermute | solution.py:383
  125.4 20.2 %collective-permute-start.25 = (bf16[384,512]{1,0:T(8,128)(2,1)S(1)}, bf16[384,512]{1,0:T(8,128)(2,1)S(1)}, u32[]{:S(2)}, u32[]{:S(2)}) collective-permute-start(bf16[384,512]{1,0:T(8,128)(2,1)S(1)} %get-tuple-element.69), channel_id=1, source_target_pairs={{0,8},{8,0},{16,24},{24,16},{1,9},{9,1},{17,25},{25,17},{2,10},{10... | collective-permute-start | bytes 1179656 | tf_op jit(solution)/shard_map/ppermute | solution.py:377
  127.2 19.6 %collective-permute-start.26 = (bf16[384,512]{1,0:T(8,128)(2,1)S(1)}, bf16[384,512]{1,0:T(8,128)(2,1)S(1)}, u32[]{:S(2)}, u32[]{:S(2)}) collective-permute-start(bf16[384,512]{1,0:T(8,128)(2,1)S(1)} %get-tuple-element.70), channel_id=1, source_target_pairs={{0,16},{8,24},{16,0},{24,8},{1,17},{9,25},{17,1},{25,9},{2,18},{10... | collective-permute-start | bytes 1179656 | tf_op jit(solution)/shard_map/ppermute | solution.py:377
  128.8 18.1 %collective-permute-start.27 = (bf16[384,512]{1,0:T(8,128)(2,1)S(1)}, bf16[384,512]{1,0:T(8,128)(2,1)S(1)}, u32[]{:S(2)}, u32[]{:S(2)}) collective-permute-start(bf16[384,512]{1,0:T(8,128)(2,1)S(1)} %get-tuple-element.71), channel_id=1, source_target_pairs={{0,24},{8,16},{16,8},{24,0},{1,25},{9,17},{17,9},{25,1},{2,26},{10... | collective-permute-start | bytes 1179656 | tf_op jit(solution)/shard_map/ppermute | solution.py:377
  128.9 8.1 %collective-permute-start.17 = (f32[16,256]{1,0:T(8,128)S(1)}, f32[16,256]{1,0:T(8,128)S(1)}, u32[]{:S(2)}, u32[]{:S(2)}) collective-permute-start(f32[16,256]{1,0:T(8,128)S(1)} %shard_map.104.refs_9_.y_ref.refs_3_), channel_id=1, source_target_pairs={{0,4},{1,5},{2,6},{3,7},{4,0},{5,1},{6,2},{7,3},{8,12},{9,13},{10,... | collective-permute-start | bytes 49160 | tf_op jit(solution)/shard_map/ppermute | solution.py:380
  138.8 1.2 collective-permute-start.21
  140.0 5.6 %collective-permute-start.22 = (f32[4,256]{1,0:T(4,128)S(1)}, f32[4,256]{1,0:T(4,128)S(1)}, u32[]{:S(2)}, u32[]{:S(2)}) collective-permute-start(f32[4,256]{1,0:T(4,128)S(1)} %add.88.x_ref), channel_id=1, source_target_pairs={{0,2},{1,3},{2,0},{3,1},{4,6},{5,7},{6,4},{7,5},{8,10},{9,11},{10,... | collective-permute-start | bytes 12296 | tf_op jit(solution)/shard_map/ppermute | solution.py:380
  146.9 6.9 %collective-permute-start.28 = (bf16[1152,512]{1,0:T(8,128)(2,1)S(1)}, bf16[1152,512]{1,0:T(8,128)(2,1)S(1)}, u32[]{:S(2)}, u32[]{:S(2)}) collective-permute-start(bf16[1152,512]{1,0:T(8,128)(2,1)S(1)} %shard_map.112), channel_id=1, source_target_pairs={{0,1},{1,0},{2,3},{3,2},{4,5},{5,4},{6,7},{7,6},{8,9},{9,8},{10,11... | collective-permute-start | bytes 3538952 | tf_op jit(solution)/shard_map/ppermute | solution.py:383
  147.0 5.9 %collective-permute-start.24 = (f32[4,256]{1,0:T(4,128)S(1)}, f32[4,256]{1,0:T(4,128)S(1)}, u32[]{:S(2)}, u32[]{:S(2)}) collective-permute-start(f32[4,256]{1,0:T(4,128)S(1)} %shard_map.109.refs_7_.y_ref.refs_3_), channel_id=1, source_target_pairs={{0,4},{1,5},{2,6},{3,7},{4,0},{5,1},{6,2},{7,3},{8,12},{9,13},{10,... | collective-permute-start | bytes 12296 | tf_op jit(solution)/shard_map/ppermute | solution.py:380
  (28 other events, 284.3 us)
Sparse Core Ops, SparseCore 0:
  14.0 58.7 all-gather.4
  74.4 38.4 all-gather.6

commit v4 on v3

--- a/solution.py
+++ b/solution.py
@@ -124,12 +124,36 @@
     return groups[0]
 
 
-def image_rows(mat_ref, at, split, parent):
-    lhs = split[0]
-    for q in range(1, len(split)):
-        lhs = jnp.where(parent == q, split[q].astype(F32), lhs.astype(F32)).astype(BF16)
-    out = lax.dot_general(lhs, mat_ref[at, :], (((1,), (1,)), ((), ())), preferred_element_type=F32)
-    return jnp.sum(out, axis=0, keepdims=True)
+def stack3(values):
+    count = -(-3 * len(values) // 8) * 8
+    row = lax.broadcasted_iota(jnp.int32, (count, values[0].shape[1]), 0)
+    out = jnp.zeros(row.shape, F32)
+    for p, value in enumerate(values):
+        for j in range(3):
+            term = value.astype(BF16).astype(F32)
+            out = jnp.where(row == 3 * p + j, jnp.broadcast_to(term, row.shape), out)
+            value = value - term
+    return out.astype(BF16)
+
+
+def unstack3(out, count):
+    return [out[3 * p:3 * p + 1] + out[3 * p + 1:3 * p + 2] + out[3 * p + 2:3 * p + 3] for p in range(count)]
+
+
+def spread_group(leaves, width, first, whole, mat, parent_ref, nodes):
+    values = [jnp.concatenate([jnp.where(parent_ref[first + i] == p, whole[first + i:first + i + 1, :], 0.0) for i in range(leaves)],
+                              axis=1) for p in range(nodes)]
+    return unstack3(jnp.dot(stack3(values), mat, preferred_element_type=F32), nodes)
+
+
+def image_group(leaves, width, first, mat, stacked, nodes, parent_ref, part_ref):
+    out = unstack3(lax.dot_general(stacked, mat, (((1,), (1,)), ((), ())), preferred_element_type=F32), nodes)
+    for i in range(leaves):
+        lanes = slice(i * width, (i + 1) * width)
+        value = out[0][:, lanes]
+        for p in range(1, nodes):
+            value = jnp.where(parent_ref[first + i] == p, out[p][:, lanes], value)
+        part_ref[pl.ds(first + i, 1), :] = value
 
 
 def group_work(leaves, width, first_leaf, group, tile_of, inv_of, m_ref, km_ref, rhs_ref, parent_ref, nodes, cols):
@@ -202,16 +226,16 @@
         scaling = node_diag_ref[at, :] + diag[p]
         reduced_ref[at, :] = reduced
         scaling_ref[at, :] = scaling
-        start.append(split3(reduced / scaling))
-        x_ref[at, :] = reduced / scaling
+        start.append(reduced / scaling)
+        x_ref[at, :] = start[p]
     image(leaves, width, early_ref, km_ref, start, parent_ref, part_ref)
 
 
-def image(leaves, width, early_ref, late_ref, split, parent_ref, part_ref):
-    for l in range(4 * leaves):
-        ref, at = (early_ref, l) if l < 3 * leaves else (late_ref, l - 3 * leaves)
-        row = image_rows(ref, pl.ds(at * width, width), split, parent_ref[l])
-        part_ref[pl.ds(l, 1), :] = row
+def image(leaves, width, early_ref, late_ref, values, parent_ref, part_ref):
+    stacked, base = stack3(values), leaves * width
+    for k in range(4):
+        mat = early_ref[pl.ds(k * base, base), :] if k < 3 else late_ref[...]
+        image_group(leaves, width, k * leaves, mat, stacked, len(values), parent_ref, part_ref)
 
 
 def sweep_kernel(leaves, width, last, ties, parent_ref, y_ref, z_ref, reduced_ref, scaling_ref, diag_ref, x_in_ref, m0_ref, m1_ref, m2_ref, m3_ref,
@@ -220,15 +244,7 @@
     x_ref, part_ref = refs[ties:]
     nodes = x_in_ref.shape[0]
     whole = y_ref[...] + z_ref[...]
-    zero = jnp.zeros((1, x_in_ref.shape[1]), F32)
-    groups = []
-    for k in range(4):
-        acc = [zero] * nodes
-        for i in range(leaves):
-            l = k * leaves + i
-            mat = m_refs[k][pl.ds(i * width, width), :]
-            acc = node_add(acc, parent_ref[l], rowdot(whole[l:l + 1, :], mat, False))
-        groups.append(acc)
+    groups = [spread_group(leaves, width, k * leaves, whole, m_refs[k][...], parent_ref, nodes) for k in range(4)]
     coupled = tree(groups)
     new = []
     for p in range(nodes):
@@ -236,11 +252,9 @@
         x = x_in_ref[at, :]
         x = x + damping * (reduced_ref[at, :] - diag_ref[at, :] * x - coupled[p]) / scaling_ref[at, :]
         x_ref[at, :] = x
-        new.append(split3(x))
+        new.append(x)
     if last:
-        for l in range(leaves):
-            row = image_rows(m0_ref, pl.ds(l * width, width), new, parent_ref[l])
-            part_ref[pl.ds(l, 1), :] = row
+        image_group(leaves, width, 0, m_refs[0][...], stack3(new), nodes, parent_ref, part_ref)
     else:
         image(leaves, width, km_ref, km3_ref, new, parent_ref, part_ref)
 
@@ -393,14 +407,14 @@
         in_specs=[SM, SM, SM, VM, VM, VM],
         out_specs=VM,
         scratch_shapes=[pltpu.VMEM((4 * leaves, cols), F32)],
-    )(info, masks, parent, link, leaf_inverse, leaf_rhs)
+    )(info, in_hbm(masks), in_hbm(parent), in_hbm(link), in_hbm(leaf_inverse), in_hbm(leaf_rhs))
     parts = [5 * base // 8, 3 * base // 8]
     solved = call(
         functools.partial(solved_kernel, leaves, width),
         out_shape=[struct((rows, cols), BF16) for rows in parts],
         in_specs=[VM, VM],
         out_specs=[VM] * len(parts),
-    )(leaf_inverse, bundle)
+    )(in_hbm(leaf_inverse), bundle)
     gathered = [lax.all_gather(part, "blk") for part in solved]
 
     bx, by = over_scen(bundle, 1), over_scen(bundle, 2)
@@ -431,7 +445,7 @@
 
     m3, km3, reduced, scaling, current, part = call(
         functools.partial(late_kernel, leaves, width, cut),
-        out_shape=[late_shape, late_shape, node_shape, node_shape, node_shape, part_shape],
+        out_shape=[pltpu.HBM((base, cols), BF16)] * 2 + [node_shape, node_shape, node_shape, part_shape],
         in_specs=[SM, SM] + [VM] * 9,
         out_specs=[VM] * 6,
         compiler_params=pltpu.CompilerParams(vmem_limit_bytes=16 * MIB),

time: 165 us -> 161 us (0.976)
  starting transfers between devices: 37.8 us -> 24.5 us
  waiting for transfers between devices: 60 us -> 72.4 us
  local copies, waits for them, and re-layouts: 10.2 us -> 3.99 us
  Pallas kernels: 41.9 us -> 44.5 us
    ppermute x10, starting transfers between devices: 22.2 us -> 8.93 us  [flip_z(): return lax.ppermute(x, 'blk', [(i, i ^ 2 * k) for i in range(blk)])]
    ppermute x10, waiting for transfers between devices: 14.6 us -> 25.1 us  [flip_z(): return lax.ppermute(x, 'blk', [(i, i ^ 2 * k) for i in range(blk)])]
    unnamed x58 -> x44, local copies, waits for them, and re-layouts: 9.93 us -> 3.76 us
  transfers between devices with their start and end apart: 31 -> 31, of which waited for: 17 -> 18; matrix products, arithmetic and copies ran while one was open for 0% -> 0% of each run, Pallas kernels for 21% -> 22%
where the time goes in v4:
time: 161 us
  waiting for transfers between devices  72.4 us (45%)
  Pallas kernels  44.5 us (28%)
  starting transfers between devices  24.5 us (15%)
  between operations  14.5 us (9%)
  local copies, waits for them, and re-layouts  3.99 us (2%)
    ppermute x10, waiting for transfers between devices, over_scen(): return lax.ppermute(x, 'scen', [(i, i ^ k) for i in range(scen)])  35.8 us
    ppermute x10, waiting for transfers between devices, flip_z(): return lax.ppermute(x, 'blk', [(i, i ^ 2 * k) for i in range(blk)])  25.1 us
    pallas_call x4, Pallas kernels, product(): call(functools.partial(product_kernel, leaves, width, terms, len(sources)...  15.8 us
    ppermute x10, starting transfers between devices, over_scen(): return lax.ppermute(x, 'scen', [(i, i ^ k) for i in range(scen)])  15 us
    pallas_call x4, Pallas kernels, plane_body(): call(functools.partial(sweep_kernel, leaves, width, last, len(ties)), out...  8.96 us
    ppermute x10, starting transfers between devices, flip_z(): return lax.ppermute(x, 'blk', [(i, i ^ 2 * k) for i in range(blk)])  8.93 us
    ppermute x9, waiting for transfers between devices, flip_core(): return lax.ppermute(x, 'blk', [(i, i ^ 1) for i in range(blk)])  8.63 us
    pallas_call x2, Pallas kernels, pick(): pl.pallas_call(kernel, out_shape=[shape] * count + [jax.ShapeDtypeStruct(...  5.36 us
  transfers between devices with their start and end apart: 31, of which 18 were waited for; matrix products, arithmetic and copies ran while one was open for 0% of the time, Pallas kernels for 22%

profile of v4, /device:TPU:0, one launch (start us, length us, event | category | flops | bytes accessed | tf_op | source)
XLA Modules:
  0.0 160.5 jit_solution(13031593035267109480)
XLA Ops:
  7.3 1.7 %shard_map.94.own_ref.bundle_ref = bf16[1296,512]{1,0:T(8,128)(2,1)S(1)} custom-call(s32[9]{0:T(128)S(1)} %stack.39.core_ref.place_ref.info_ref, s32[4]{0:T(128)} %bitcast.18, s32[4]{0:T(128)} %parent_ref.1, bf16[4,256,512]{2,1,0:T(8,128)(2,1)} %link_ref.1, bf16[4,256,256]{2,1,0:T(8,128)(2,1)} %inverse_ref.7, f32[4,256]{1,0:T(4,128)} %rhs_ref.3), custom_call_target="tpu_custom_call" | custom-call | tf_op jit(solution)/shard_map/pallas_call | solution.py:404
  9.0 2.7 %shard_map.97 = (bf16[640,512]{1,0:T(8,128)(2,1)}, bf16[384,512]{1,0:T(8,128)(2,1)}) custom-call(bf16[4,256,256]{2,1,0:T(8,128)(2,1)} %inverse_ref.7, bf16[1296,512]{1,0:T(8,128)(2,1)S(1)} %shard_map.94.own_ref.bundle_ref), custom_call_target="tpu_custom_call" | custom-call | tf_op jit(solution)/shard_map/pallas_call | solution.py:412
  12.6 3.0 %collective-permute-start.1 = (bf16[1296,512]{1,0:T(8,128)(2,1)S(1)}, bf16[1296,512]{1,0:T(8,128)(2,1)S(1)}, u32[]{:S(2)}, u32[]{:S(2)}) collective-permute-start(bf16[1296,512]{1,0:T(8,128)(2,1)S(1)} %shard_map.94.own_ref.bundle_ref), channel_id=1, source_target_pairs={{0,16},{8,24},{16,0},{24,8},{1,17},{9,25},{17,1},{25,9},{2,18},{10... | collective-permute-start | bytes 3981320 | tf_op jit(solution)/shard_map/ppermute | solution.py:391
  17.1 27.6 %collective-permute-done.1.y_ref = bf16[1296,512]{1,0:T(8,128)(2,1)S(1)} collective-permute-done((bf16[1296,512]{1,0:T(8,128)(2,1)S(1)}, bf16[1296,512]{1,0:T(8,128)(2,1)S(1)}, u32[]{:S(2)}, u32[]{:S(2)}) %collective-permute-start.1) | collective-permute-done | bytes 1327136 | tf_op jit(solution)/shard_map/ppermute | solution.py:391
  44.8 1.8 %collective-permute-start.2 = (bf16[752,512]{1,0:T(8,128)(2,1)S(1)}, bf16[752,512]{1,0:T(8,128)(2,1)S(1)}, u32[]{:S(2)}, u32[]{:S(2)}) collective-permute-start(bf16[752,512]{1,0:T(8,128)(2,1)S(1)} %slice.93), channel_id=1, source_target_pairs={{0,8},{8,0},{16,24},{24,16},{1,9},{9,1},{17,25},{25,17},{2,10},{10... | collective-permute-start | bytes 2310152 | tf_op jit(solution)/shard_map/ppermute | solution.py:391
  46.6 1.6 collective-permute-start.3
  50.3 3.8 %shard_map.95 = (bf16[1024,512]{1,0:T(8,128)(2,1)S(1)}, bf16[1024,512]{1,0:T(8,128)(2,1)S(1)}, bf16[1024,512]{1,0:T(8,128)(2,1)S(1)}, bf16[3072,512]{1,0:T(8,128...) custom-call(s32[9]{0:T(128)S(1)} %stack.39.core_ref.place_ref.info_ref, s32[12]{0:T(128)S(1)} %pad_add_fusion.1.parent_ref, ...), custom_call_target="tpu_custom_call" | custom-call | tf_op jit(solution)/shard_map/pallas_call | solution.py:435
  57.1 6.2 %collective-permute-done.2.db_ref = bf16[752,512]{1,0:T(8,128)(2,1)S(1)} collective-permute-done((bf16[752,512]{1,0:T(8,128)(2,1)S(1)}, bf16[752,512]{1,0:T(8,128)(2,1)S(1)}, u32[]{:S(2)}, u32[]{:S(2)}) %collective-permute-start.2) | collective-permute-done | bytes 770080 | tf_op jit(solution)/shard_map/ppermute | solution.py:391
  65.0 3.6 %shard_map.96 = (bf16[1024,512]{1,0:T(8,128)(2,1)}, bf16[1024,512]{1,0:T(8,128)(2,1)}, f32[2,512]{1,0:T(2,128)S(1)}, f32[2,512]{1,0:T(2,128)S(1)}, f32[2,512]{1,0:T(2,128)S(1)}, /*index=5*/f32[16,256]{1,0:T(8,128)S(1)}) custom-call(s32[9]{0:T(128)S(1)} %stack.39.core_ref.place_ref.info_ref, s32[16]{0:T(128)S(1)} %pad_add_fusion.parent_ref, ...), custom_call_target="tpu_custom_call" | custom-call | tf_op jit(solution)/shard_map/pallas_call | solution.py:446
  68.6 2.1 %all-gather.5.cloned.1.call-done = bf16[5120,512]{1,0:T(8,128)(2,1)} async-done(((bf16[640,512]{1,0:T(8,128)(2,1)}), bf16[5120,512]{1,0:T(8,128)(2,1)}) %all-gather.5.cloned.1.call-update) | async-done | bytes 5242896 | tf_op jit(solution)/shard_map/all_gather | solution.py:418
  70.7 3.2 %shard_map.98 = (bf16[640,512]{1,0:T(8,128)(2,1)}, bf16[640,512]{1,0:T(8,128)(2,1)}, bf16[640,512]{1,0:T(8,128)(2,1)}, f32[8,128]{1,0:T(8,128)S(1)}) custom-call(s32[9]{0:T(128)S(1)} %stack.39.core_ref.place_ref.info_ref, bf16[8,640,512]{2,1,0:T(8,128)(2,1)} %bitcast.12, f32[16,256]{1,0:T(8,128)S(1)} %get-tuple-element.43.refs_0_), custom_call_target="tpu_custom_call" | custom-call | tf_op jit(solution)/shard_map/pallas_call | solution.py:319
  78.6 3.7 %collective-permute-done.7.y_ref = f32[16,256]{1,0:T(8,128)S(1)} collective-permute-done((f32[16,256]{1,0:T(8,128)S(1)}, f32[16,256]{1,0:T(8,128)S(1)}, u32[]{:S(2)}, u32[]{:S(2)}) %collective-permute-start.7) | collective-permute-done | bytes 16416 | tf_op jit(solution)/shard_map/ppermute | solution.py:394
  83.6 4.0 %collective-permute-done.8.z_ref = f32[16,256]{1,0:T(8,128)S(1)} collective-permute-done((f32[16,256]{1,0:T(8,128)S(1)}, f32[16,256]{1,0:T(8,128)S(1)}, u32[]{:S(2)}, u32[]{:S(2)}) %collective-permute-start.8) | collective-permute-done | bytes 16416 | tf_op jit(solution)/shard_map/ppermute | solution.py:394
  87.6 2.4 %shard_map.100 = (f32[2,512]{1,0:T(2,128)S(1)}, f32[16,256]{1,0:T(8,128)S(1)}) custom-call(s32[16]{0:T(128)S(1)} %pad_add_fusion.parent_ref, f32[16,256]{1,0:T(8,128)S(1)} %shard_map.99.y_ref, f32[16,256]{1,0:T(8,128)S(1)} %collective-permute-done.8.z_ref, f32[2,512]{1,0:T(2,128)S(1)} %get-tuple-element.46.reduced_ref, ...), custom_call_target="tpu_custom_call" | custom-call | tf_op jit(solution)/shard_map/pallas_call | solution.py:492
  91.3 4.7 %collective-permute-done.10 = f32[16,256]{1,0:T(8,128)S(1)} collective-permute-done((f32[16,256]{1,0:T(8,128)S(1)}, f32[16,256]{1,0:T(8,128)S(1)}, u32[]{:S(2)}, u32[]{:S(2)}) %collective-permute-start.10) | collective-permute-done | bytes 16416 | tf_op jit(solution)/shard_map/ppermute | solution.py:394
  96.4 4.7 %collective-permute-done.11.z_ref = f32[16,256]{1,0:T(8,128)S(1)} collective-permute-done((f32[16,256]{1,0:T(8,128)S(1)}, f32[16,256]{1,0:T(8,128)S(1)}, u32[]{:S(2)}, u32[]{:S(2)}) %collective-permute-start.11) | collective-permute-done | bytes 16416 | tf_op jit(solution)/shard_map/ppermute | solution.py:394
  101.1 2.4 %shard_map.101 = (f32[2,512]{1,0:T(2,128)S(1)}, f32[16,256]{1,0:T(8,128)S(1)}) custom-call(s32[16]{0:T(128)S(1)} %pad_add_fusion.parent_ref, f32[16,256]{1,0:T(8,128)S(1)} %add.84.y_ref, f32[16,256]{1,0:T(8,128)S(1)} %collective-permute-done.11.z_ref, f32[2,512]{1,0:T(2,128)S(1)} %get-tuple-element.46.reduced_ref, ...), custom_call_target="tpu_custom_call" | custom-call | tf_op jit(solution)/shard_map/pallas_call | solution.py:492
  104.7 3.7 %collective-permute-done.13 = f32[16,256]{1,0:T(8,128)S(1)} collective-permute-done((f32[16,256]{1,0:T(8,128)S(1)}, f32[16,256]{1,0:T(8,128)S(1)}, u32[]{:S(2)}, u32[]{:S(2)}) %collective-permute-start.13) | collective-permute-done | bytes 16416 | tf_op jit(solution)/shard_map/ppermute | solution.py:394
  108.5 1.7 %collective-permute-start.14 = (f32[16,256]{1,0:T(8,128)S(1)}, f32[16,256]{1,0:T(8,128)S(1)}, u32[]{:S(2)}, u32[]{:S(2)}) collective-permute-start(f32[16,256]{1,0:T(8,128)S(1)} %add.86.y_ref), channel_id=1, source_target_pairs={{0,4},{1,5},{2,6},{3,7},{4,0},{5,1},{6,2},{7,3},{8,12},{9,13},{10,... | collective-permute-start | bytes 49160 | tf_op jit(solution)/shard_map/ppermute | solution.py:394
  110.1 3.0 %collective-permute-done.14.z_ref = f32[16,256]{1,0:T(8,128)S(1)} collective-permute-done((f32[16,256]{1,0:T(8,128)S(1)}, f32[16,256]{1,0:T(8,128)S(1)}, u32[]{:S(2)}, u32[]{:S(2)}) %collective-permute-start.14) | collective-permute-done | bytes 16416 | tf_op jit(solution)/shard_map/ppermute | solution.py:394
  113.1 2.4 %shard_map.102 = (f32[2,512]{1,0:T(2,128)S(1)}, f32[16,256]{1,0:T(8,128)S(1)}) custom-call(s32[16]{0:T(128)S(1)} %pad_add_fusion.parent_ref, f32[16,256]{1,0:T(8,128)S(1)} %add.86.y_ref, f32[16,256]{1,0:T(8,128)S(1)} %collective-permute-done.14.z_ref, f32[2,512]{1,0:T(2,128)S(1)} %get-tuple-element.46.reduced_ref, ...), custom_call_target="tpu_custom_call" | custom-call | tf_op jit(solution)/shard_map/pallas_call | solution.py:492
  117.2 2.2 %shard_map.103 = (bf16[384,512]{1,0:T(8,128)(2,1)S(1)}, bf16[384,512]{1,0:T(8,128)(2,1)S(1)}, bf16[384,512]{1,0:T(8,128)(2,1)S(1)}, f32[8,128]{1,0:T(8,128)S(1)}) custom-call(s32[9]{0:T(128)S(1)} %stack.39.core_ref.place_ref.info_ref, bf16[8,384,512]{2,1,0:T(8,128)(2,1)} %bitcast.15, f32[16,256]{1,0:T(8,128)S(1)} %get-tuple-element.58.refs_0_), custom_call_target="tpu_custom_call" | custom-call | tf_op jit(solution)/shard_map/pallas_call | solution.py:319
  120.6 1.6 %shard_map.107 = bf16[1920,512]{1,0:T(8,128)(2,1)S(1)} custom-call(bf16[640,512]{1,0:T(8,128)(2,1)} %collective-permute-done.18.refs_6_.refs_0_, bf16[640,512]{1,0:T(8,128)(2,1)} %collective-permute-done.19.refs_7_.refs_1_, bf16[640,512]{1,0:T(8,128)(2,1)} %collective-permute-done.20.refs_8_.refs_2_, f32[16,256]{1,0:T(8,128)S(1)} %shard_map.104.refs_9_.y_ref.refs_3_), custom_call_target="tpu_custom_call" | custom-call | tf_op jit(solution)/shard_map/pallas_call | solution.py:282
  122.2 1.6 collective-permute-start.25
  125.8 1.9 %collective-permute-start.17 = (f32[16,256]{1,0:T(8,128)S(1)}, f32[16,256]{1,0:T(8,128)S(1)}, u32[]{:S(2)}, u32[]{:S(2)}) collective-permute-start(f32[16,256]{1,0:T(8,128)S(1)} %shard_map.104.refs_9_.y_ref.refs_3_), channel_id=1, source_target_pairs={{0,4},{1,5},{2,6},{3,7},{4,0},{5,1},{6,2},{7,3},{8,12},{9,13},{10,... | collective-permute-start | bytes 49160 | tf_op jit(solution)/shard_map/ppermute | solution.py:394
  127.8 5.1 %shard_map.105 = (f32[2,512,512]{2,1,0:T(8,128)S(1)}, f32[8,128]{1,0:T(8,128)S(1)}) custom-call(s32[9]{0:T(128)S(1)} %stack.39.core_ref.place_ref.info_ref, s32[16]{0:T(128)S(1)} %pad_add_fusion.parent_ref, bf16[1024,512]{1,0:T(8,128)(2,1)S(1)} %copy-done.2, bf16[1024,512]{1,0:T(8,128)(2,1)S(1)} %copy-done.5, bf16[1024,512]{1,0:T(8,128)(2,1)S(1)} %copy-done.8, ...), custom_call_target="tpu_custom_call" | custom-call | flops 1543503872 | bytes 2097152 | tf_op jit(solution)/shard_map/pallas_call | solution.py:469
  132.9 1.8 %shard_map.106 = (f32[2,512]{1,0:T(2,128)}, f32[4,256]{1,0:T(4,128)S(1)}) custom-call(s32[16]{0:T(128)S(1)} %pad_add_fusion.parent_ref, f32[16,256]{1,0:T(8,128)S(1)} %shard_map.104.refs_9_.y_ref.refs_3_, f32[16,256]{1,0:T(8,128)S(1)} %collective-permute-done.17.z_ref, f32[2,512]{1,0:T(2,128)S(1)} %get-tuple-element.46.reduced_ref, ...), custom_call_target="tpu_custom_call" | custom-call | tf_op jit(solution)/shard_map/pallas_call | solution.py:492
  137.3 4.2 %shard_map.108 = (f32[2,512,512]{2,1,0:T(8,128)S(1)}, f32[8,128]{1,0:T(8,128)S(1)}) custom-call(s32[9]{0:T(128)S(1)} %stack.39.core_ref.place_ref.info_ref, s32[16]{0:T(128)S(1)} %pad_add_fusion.parent_ref, bf16[1024,512]{1,0:T(8,128)(2,1)S(1)} %copy-done.2, bf16[1024,512]{1,0:T(8,128)(2,1)S(1)} %copy-done.5, bf16[1024,512]{1,0:T(8,128)(2,1)S(1)} %copy-done.8, ...), custom_call_target="tpu_custom_call" | custom-call | flops 1543503872 | bytes 2097152 | tf_op jit(solution)/shard_map/pallas_call | solution.py:469
  141.5 2.0 %collective-permute-done.26.refs_5_.refs_1_ = bf16[384,512]{1,0:T(8,128)(2,1)S(1)} collective-permute-done((bf16[384,512]{1,0:T(8,128)(2,1)S(1)}, bf16[384,512]{1,0:T(8,128)(2,1)S(1)}, u32[]{:S(2)}, u32[]{:S(2)}) %collective-permute-start.26) | collective-permute-done | bytes 393248 | tf_op jit(solution)/shard_map/ppermute | solution.py:391
  143.6 2.0 %collective-permute-start.24 = (f32[4,256]{1,0:T(4,128)S(1)}, f32[4,256]{1,0:T(4,128)S(1)}, u32[]{:S(2)}, u32[]{:S(2)}) collective-permute-start(f32[4,256]{1,0:T(4,128)S(1)} %shard_map.109.refs_7_.y_ref.refs_3_), channel_id=1, source_target_pairs={{0,4},{1,5},{2,6},{3,7},{4,0},{5,1},{6,2},{7,3},{8,12},{9,13},{10,... | collective-permute-start | bytes 12296 | tf_op jit(solution)/shard_map/ppermute | solution.py:394
  145.6 2.9 %shard_map.110 = (f32[2,512,512]{2,1,0:T(8,128)S(1)}, f32[8,128]{1,0:T(8,128)S(1)}, f32[2,512,1024]{2,1,0:T(8,128)}) custom-call(s32[9]{0:T(128)S(1)} %stack.39.core_ref.place_ref.info_ref, s32[16]{0:T(128)S(1)} %pad_add_fusion.parent_ref, bf16[1024,512]{1,0:T(8,128)(2,1)S(1)} %copy-done.2, ...), custom_call_target="tpu_custom_call", output_to_operand_aliasing={{0}: (10, {})} | custom-call | flops 603979776 | bytes 2097152 | tf_op jit(solution)/shard_map/pallas_call | solution.py:469
  150.1 3.6 %shard_map.113 = (f32[2,512,512]{2,1,0:T(8,128)S(1)}, f32[8,128]{1,0:T(8,128)}, f32[2,512,1024]{2,1,0:T(8,128)}) custom-call(s32[9]{0:T(128)S(1)} %stack.39.core_ref.place_ref.info_ref, s32[16]{0:T(128)S(1)} %pad_add_fusion.parent_ref, bf16[1024,512]{1,0:T(8,128)(2,1)S(1)} %copy-done.2, ...), custom_call_target="tpu_custom_call", output_to_operand_aliasing={{0}: (8, {}), {2}: (9, {})} | custom-call | flops 603979776 | bytes 2097152 | tf_op jit(solution)/shard_map/pallas_call | solution.py:469
  (123 shorter events, 27.0 us)
Async XLA Ops:
  7.2 63.5 %all-gather.5.cloned.1.call-start = ((), (), s32[]{:S(2)}) async-start(), calls=%async_computation | async-start | bytes 5898240 | tf_op jit(solution)/shard_map/all_gather | solution.py:418
  11.8 105.4 %all-gather.7.cloned.1.call-start = ((), (), s32[]{:S(2)}) async-start(), calls=%async_computation.1 | async-start | bytes 3538944 | tf_op jit(solution)/shard_map/all_gather | solution.py:418
  12.5 37.7 %copy-start.15 = (bf16[4,256,256]{2,1,0:T(8,128)(2,1)S(1)}, bf16[4,256,256]{2,1,0:T(8,128)(2,1)}, u32[]{:S(2)}) copy-start(bf16[4,256,256]{2,1,0:T(8,128)(2,1)} %inverse_ref.7) | copy-start | bytes 1572868
  12.6 32.2 %collective-permute-start.1 = (bf16[1296,512]{1,0:T(8,128)(2,1)S(1)}, bf16[1296,512]{1,0:T(8,128)(2,1)S(1)}, u32[]{:S(2)}, u32[]{:S(2)}) collective-permute-start(bf16[1296,512]{1,0:T(8,128)(2,1)S(1)} %shard_map.94.own_ref.bundle_ref), channel_id=1, source_target_pairs={{0,16},{8,24},{16,0},{24,8},{1,17},{9,25},{17,1},{25,9},{2,18},{10... | collective-permute-start | bytes 3981320 | tf_op jit(solution)/shard_map/ppermute | solution.py:391
  15.6 31.0 %collective-permute-start = (bf16[1296,512]{1,0:T(8,128)(2,1)S(1)}, bf16[1296,512]{1,0:T(8,128)(2,1)S(1)}, u32[]{:S(2)}, u32[]{:S(2)}) collective-permute-start(bf16[1296,512]{1,0:T(8,128)(2,1)S(1)} %shard_map.94.own_ref.bundle_ref), channel_id=1, source_target_pairs={{0,8},{8,0},{16,24},{24,16},{1,9},{9,1},{17,25},{25,17},{2,10},{10... | collective-permute-start | bytes 3981320 | tf_op jit(solution)/shard_map/ppermute | solution.py:391
  44.8 18.5 %collective-permute-start.2 = (bf16[752,512]{1,0:T(8,128)(2,1)S(1)}, bf16[752,512]{1,0:T(8,128)(2,1)S(1)}, u32[]{:S(2)}, u32[]{:S(2)}) collective-permute-start(bf16[752,512]{1,0:T(8,128)(2,1)S(1)} %slice.93), channel_id=1, source_target_pairs={{0,8},{8,0},{16,24},{24,16},{1,9},{9,1},{17,25},{25,17},{2,10},{10... | collective-permute-start | bytes 2310152 | tf_op jit(solution)/shard_map/ppermute | solution.py:391
  46.6 17.1 %collective-permute-start.3 = (bf16[544,512]{1,0:T(8,128)(2,1)S(1)}, bf16[544,512]{1,0:T(8,128)(2,1)S(1)}, u32[]{:S(2)}, u32[]{:S(2)}) collective-permute-start(bf16[544,512]{1,0:T(8,128)(2,1)S(1)} %slice.105), channel_id=1, source_target_pairs={{0,16},{8,24},{16,0},{24,8},{1,17},{9,25},{17,1},{25,9},{2,18},{10... | collective-permute-start | bytes 1671176 | tf_op jit(solution)/shard_map/ppermute | solution.py:391
  48.3 2.0 %collective-permute-start.5 = (bf16[512,512]{1,0:T(8,128)(2,1)S(1)}, bf16[512,512]{1,0:T(8,128)(2,1)S(1)}, u32[]{:S(2)}, u32[]{:S(2)}) collective-permute-start(bf16[512,512]{1,0:T(8,128)(2,1)S(1)} %pad_maximum_fusion), channel_id=1, source_target_pairs={{0,1},{1,0},{2,3},{3,2},{4,5},{5,4},{6,7},{7,6},{8,9},{9,8},{10,11... | collective-permute-start | bytes 1572872 | tf_op jit(solution)/shard_map/ppermute | solution.py:397
  63.3 1.6 collective-permute-start.4
  73.9 46.6 %collective-permute-start.18 = (bf16[640,512]{1,0:T(8,128)(2,1)}, bf16[640,512]{1,0:T(8,128)(2,1)}, u32[]{:S(2)}, u32[]{:S(2)}) collective-permute-start(bf16[640,512]{1,0:T(8,128)(2,1)} %get-tuple-element.62), channel_id=1, source_target_pairs={{0,8},{8,0},{16,24},{24,16},{1,9},{9,1},{17,25},{25,17},{2,10},{10... | collective-permute-start | bytes 1966088 | tf_op jit(solution)/shard_map/ppermute | solution.py:391
  75.4 45.1 %collective-permute-start.19 = (bf16[640,512]{1,0:T(8,128)(2,1)}, bf16[640,512]{1,0:T(8,128)(2,1)}, u32[]{:S(2)}, u32[]{:S(2)}) collective-permute-start(bf16[640,512]{1,0:T(8,128)(2,1)} %get-tuple-element.63), channel_id=1, source_target_pairs={{0,16},{8,24},{16,0},{24,8},{1,17},{9,25},{17,1},{25,9},{2,18},{10... | collective-permute-start | bytes 1966088 | tf_op jit(solution)/shard_map/ppermute | solution.py:391
  76.9 43.6 %collective-permute-start.20 = (bf16[640,512]{1,0:T(8,128)(2,1)}, bf16[640,512]{1,0:T(8,128)(2,1)}, u32[]{:S(2)}, u32[]{:S(2)}) collective-permute-start(bf16[640,512]{1,0:T(8,128)(2,1)} %get-tuple-element.64), channel_id=1, source_target_pairs={{0,24},{8,16},{16,8},{24,0},{1,25},{9,17},{17,9},{25,1},{2,26},{10... | collective-permute-start | bytes 1966088 | tf_op jit(solution)/shard_map/ppermute | solution.py:391
  77.4 1.2 collective-permute-start.6
  78.6 3.7 %collective-permute-start.7 = (f32[16,256]{1,0:T(8,128)S(1)}, f32[16,256]{1,0:T(8,128)S(1)}, u32[]{:S(2)}, u32[]{:S(2)}) collective-permute-start(f32[16,256]{1,0:T(8,128)S(1)} %add.82.x_ref), channel_id=1, source_target_pairs={{0,2},{1,3},{2,0},{3,1},{4,6},{5,7},{6,4},{7,5},{8,10},{9,11},{10,... | collective-permute-start | bytes 49160 | tf_op jit(solution)/shard_map/ppermute | solution.py:394
  82.4 5.2 %collective-permute-start.8 = (f32[16,256]{1,0:T(8,128)S(1)}, f32[16,256]{1,0:T(8,128)S(1)}, u32[]{:S(2)}, u32[]{:S(2)}) collective-permute-start(f32[16,256]{1,0:T(8,128)S(1)} %shard_map.99.y_ref), channel_id=1, source_target_pairs={{0,4},{1,5},{2,6},{3,7},{4,0},{5,1},{6,2},{7,3},{8,12},{9,13},{10,... | collective-permute-start | bytes 49160 | tf_op jit(solution)/shard_map/ppermute | solution.py:394
  90.0 1.2 collective-permute-start.9
  91.3 4.7 %collective-permute-start.10 = (f32[16,256]{1,0:T(8,128)S(1)}, f32[16,256]{1,0:T(8,128)S(1)}, u32[]{:S(2)}, u32[]{:S(2)}) collective-permute-start(f32[16,256]{1,0:T(8,128)S(1)} %add.83), channel_id=1, source_target_pairs={{0,2},{1,3},{2,0},{3,1},{4,6},{5,7},{6,4},{7,5},{8,10},{9,11},{10,... | collective-permute-start | bytes 49160 | tf_op jit(solution)/shard_map/ppermute | solution.py:394
  96.0 5.1 %collective-permute-start.11 = (f32[16,256]{1,0:T(8,128)S(1)}, f32[16,256]{1,0:T(8,128)S(1)}, u32[]{:S(2)}, u32[]{:S(2)}) collective-permute-start(f32[16,256]{1,0:T(8,128)S(1)} %add.84.y_ref), channel_id=1, source_target_pairs={{0,4},{1,5},{2,6},{3,7},{4,0},{5,1},{6,2},{7,3},{8,12},{9,13},{10,... | collective-permute-start | bytes 49160 | tf_op jit(solution)/shard_map/ppermute | solution.py:394
  103.5 1.2 collective-permute-start.12
  104.7 3.7 %collective-permute-start.13 = (f32[16,256]{1,0:T(8,128)S(1)}, f32[16,256]{1,0:T(8,128)S(1)}, u32[]{:S(2)}, u32[]{:S(2)}) collective-permute-start(f32[16,256]{1,0:T(8,128)S(1)} %add.85), channel_id=1, source_target_pairs={{0,2},{1,3},{2,0},{3,1},{4,6},{5,7},{6,4},{7,5},{8,10},{9,11},{10,... | collective-permute-start | bytes 49160 | tf_op jit(solution)/shard_map/ppermute | solution.py:394
  108.5 4.7 %collective-permute-start.14 = (f32[16,256]{1,0:T(8,128)S(1)}, f32[16,256]{1,0:T(8,128)S(1)}, u32[]{:S(2)}, u32[]{:S(2)}) collective-permute-start(f32[16,256]{1,0:T(8,128)S(1)} %add.86.y_ref), channel_id=1, source_target_pairs={{0,4},{1,5},{2,6},{3,7},{4,0},{5,1},{6,2},{7,3},{8,12},{9,13},{10,... | collective-permute-start | bytes 49160 | tf_op jit(solution)/shard_map/ppermute | solution.py:394
  115.5 1.2 collective-permute-start.15
  116.8 3.7 %collective-permute-start.16 = (f32[16,256]{1,0:T(8,128)S(1)}, f32[16,256]{1,0:T(8,128)S(1)}, u32[]{:S(2)}, u32[]{:S(2)}) collective-permute-start(f32[16,256]{1,0:T(8,128)S(1)} %add.87.x_ref), channel_id=1, source_target_pairs={{0,2},{1,3},{2,0},{3,1},{4,6},{5,7},{6,4},{7,5},{8,10},{9,11},{10,... | collective-permute-start | bytes 49160 | tf_op jit(solution)/shard_map/ppermute | solution.py:394
  122.2 15.1 %collective-permute-start.23 = (bf16[1920,512]{1,0:T(8,128)(2,1)S(1)}, bf16[1920,512]{1,0:T(8,128)(2,1)S(1)}, u32[]{:S(2)}, u32[]{:S(2)}) collective-permute-start(bf16[1920,512]{1,0:T(8,128)(2,1)S(1)} %shard_map.107), channel_id=1, source_target_pairs={{0,1},{1,0},{2,3},{3,2},{4,5},{5,4},{6,7},{7,6},{8,9},{9,8},{10,11... | collective-permute-start | bytes 5898248 | tf_op jit(solution)/shard_map/ppermute | solution.py:397
  122.2 19.2 %collective-permute-start.25 = (bf16[384,512]{1,0:T(8,128)(2,1)S(1)}, bf16[384,512]{1,0:T(8,128)(2,1)S(1)}, u32[]{:S(2)}, u32[]{:S(2)}) collective-permute-start(bf16[384,512]{1,0:T(8,128)(2,1)S(1)} %get-tuple-element.69), channel_id=1, source_target_pairs={{0,8},{8,0},{16,24},{24,16},{1,9},{9,1},{17,25},{25,17},{2,10},{10... | collective-permute-start | bytes 1179656 | tf_op jit(solution)/shard_map/ppermute | solution.py:391
  123.8 19.6 %collective-permute-start.26 = (bf16[384,512]{1,0:T(8,128)(2,1)S(1)}, bf16[384,512]{1,0:T(8,128)(2,1)S(1)}, u32[]{:S(2)}, u32[]{:S(2)}) collective-permute-start(bf16[384,512]{1,0:T(8,128)(2,1)S(1)} %get-tuple-element.70), channel_id=1, source_target_pairs={{0,16},{8,24},{16,0},{24,8},{1,17},{9,25},{17,1},{25,9},{2,18},{10... | collective-permute-start | bytes 1179656 | tf_op jit(solution)/shard_map/ppermute | solution.py:391
  125.3 18.1 %collective-permute-start.27 = (bf16[384,512]{1,0:T(8,128)(2,1)S(1)}, bf16[384,512]{1,0:T(8,128)(2,1)S(1)}, u32[]{:S(2)}, u32[]{:S(2)}) collective-permute-start(bf16[384,512]{1,0:T(8,128)(2,1)S(1)} %get-tuple-element.71), channel_id=1, source_target_pairs={{0,24},{8,16},{16,8},{24,0},{1,25},{9,17},{17,9},{25,1},{2,26},{10... | collective-permute-start | bytes 1179656 | tf_op jit(solution)/shard_map/ppermute | solution.py:391
  125.8 7.1 %collective-permute-start.17 = (f32[16,256]{1,0:T(8,128)S(1)}, f32[16,256]{1,0:T(8,128)S(1)}, u32[]{:S(2)}, u32[]{:S(2)}) collective-permute-start(f32[16,256]{1,0:T(8,128)S(1)} %shard_map.104.refs_9_.y_ref.refs_3_), channel_id=1, source_target_pairs={{0,4},{1,5},{2,6},{3,7},{4,0},{5,1},{6,2},{7,3},{8,12},{9,13},{10,... | collective-permute-start | bytes 49160 | tf_op jit(solution)/shard_map/ppermute | solution.py:394
  134.7 1.2 collective-permute-start.21
  135.9 5.6 %collective-permute-start.22 = (f32[4,256]{1,0:T(4,128)S(1)}, f32[4,256]{1,0:T(4,128)S(1)}, u32[]{:S(2)}, u32[]{:S(2)}) collective-permute-start(f32[4,256]{1,0:T(4,128)S(1)} %add.88.x_ref), channel_id=1, source_target_pairs={{0,2},{1,3},{2,0},{3,1},{4,6},{5,7},{6,4},{7,5},{8,10},{9,11},{10,... | collective-permute-start | bytes 12296 | tf_op jit(solution)/shard_map/ppermute | solution.py:394
  143.5 5.9 %collective-permute-start.28 = (bf16[1152,512]{1,0:T(8,128)(2,1)S(1)}, bf16[1152,512]{1,0:T(8,128)(2,1)S(1)}, u32[]{:S(2)}, u32[]{:S(2)}) collective-permute-start(bf16[1152,512]{1,0:T(8,128)(2,1)S(1)} %shard_map.112), channel_id=1, source_target_pairs={{0,1},{1,0},{2,3},{3,2},{4,5},{5,4},{6,7},{7,6},{8,9},{9,8},{10,11... | collective-permute-start | bytes 3538952 | tf_op jit(solution)/shard_map/ppermute | solution.py:397
  143.6 5.0 %collective-permute-start.24 = (f32[4,256]{1,0:T(4,128)S(1)}, f32[4,256]{1,0:T(4,128)S(1)}, u32[]{:S(2)}, u32[]{:S(2)}) collective-permute-start(f32[4,256]{1,0:T(4,128)S(1)} %shard_map.109.refs_7_.y_ref.refs_3_), channel_id=1, source_target_pairs={{0,4},{1,5},{2,6},{3,7},{4,0},{5,1},{6,2},{7,3},{8,12},{9,13},{10,... | collective-permute-start | bytes 12296 | tf_op jit(solution)/shard_map/ppermute | solution.py:394
  (21 other events, 278.9 us)
Sparse Core Ops, SparseCore 0:
  11.9 58.7 all-gather.4
  72.3 38.4 all-gather.6

commit v5 on v4

--- a/solution.py
+++ b/solution.py
@@ -522,7 +522,7 @@
     )(*arrived, leaf_rhs, leaf_inverse, *ties)
 
     terms = [(k, 0, None, (k - 1) * parts[1], parts[0], parts[1]) for k in (1, 2, 3)]
-    unused, token, schur = product(terms, others, leaf_solution, acc1, 1, schur)
+    unused, token, schur = product(terms, others, arrived[0], acc1, 1, schur)
     return current, leaf_solution, schur
 
 

time: 161 us -> 160 us (level)
    unnamed x44 -> x42, local copies, waits for them, and re-layouts: 3.76 us -> 3.05 us
where the time goes in v5:
time: 160 us
  waiting for transfers between devices  72.4 us (45%)
  Pallas kernels  44.5 us (28%)
  starting transfers between devices  24.5 us (15%)
  between operations  14.5 us (9%)
  local copies, waits for them, and re-layouts  3.28 us (2%)
    ppermute x10, waiting for transfers between devices, over_scen(): return lax.ppermute(x, 'scen', [(i, i ^ k) for i in range(scen)])  35.8 us
    ppermute x10, waiting for transfers between devices, flip_z(): return lax.ppermute(x, 'blk', [(i, i ^ 2 * k) for i in range(blk)])  25.1 us
    pallas_call x4, Pallas kernels, product(): call(functools.partial(product_kernel, leaves, width, terms, len(sources)...  15.8 us
    ppermute x10, starting transfers between devices, over_scen(): return lax.ppermute(x, 'scen', [(i, i ^ k) for i in range(scen)])  15 us
    pallas_call x4, Pallas kernels, plane_body(): call(functools.partial(sweep_kernel, leaves, width, last, len(ties)), out...  8.96 us
    ppermute x10, starting transfers between devices, flip_z(): return lax.ppermute(x, 'blk', [(i, i ^ 2 * k) for i in range(blk)])  8.95 us
    ppermute x9, waiting for transfers between devices, flip_core(): return lax.ppermute(x, 'blk', [(i, i ^ 1) for i in range(blk)])  8.63 us
    pallas_call x2, Pallas kernels, pick(): pl.pallas_call(kernel, out_shape=[shape] * count + [jax.ShapeDtypeStruct(...  5.36 us
  transfers between devices with their start and end apart: 31, of which 18 were waited for; matrix products, arithmetic and copies ran while one was open for 0% of the time, Pallas kernels for 22%

profile of v5, /device:TPU:0, one launch (start us, length us, event | category | flops | bytes accessed | tf_op | source)
XLA Modules:
  0.0 159.8 jit_solution(1835520641134785375)
XLA Ops:
  7.3 1.7 %shard_map.94.own_ref.bundle_ref = bf16[1296,512]{1,0:T(8,128)(2,1)S(1)} custom-call(s32[9]{0:T(128)S(1)} %stack.39.core_ref.place_ref.info_ref, s32[4]{0:T(128)} %bitcast.18, s32[4]{0:T(128)} %parent_ref.1, bf16[4,256,512]{2,1,0:T(8,128)(2,1)} %link_ref.1, bf16[4,256,256]{2,1,0:T(8,128)(2,1)} %inverse_ref.7, f32[4,256]{1,0:T(4,128)} %rhs_ref.3), custom_call_target="tpu_custom_call" | custom-call | tf_op jit(solution)/shard_map/pallas_call | solution.py:404
  9.0 2.7 %shard_map.97 = (bf16[640,512]{1,0:T(8,128)(2,1)}, bf16[384,512]{1,0:T(8,128)(2,1)}) custom-call(bf16[4,256,256]{2,1,0:T(8,128)(2,1)} %inverse_ref.7, bf16[1296,512]{1,0:T(8,128)(2,1)S(1)} %shard_map.94.own_ref.bundle_ref), custom_call_target="tpu_custom_call" | custom-call | tf_op jit(solution)/shard_map/pallas_call | solution.py:412
  12.6 3.0 %collective-permute-start.1 = (bf16[1296,512]{1,0:T(8,128)(2,1)S(1)}, bf16[1296,512]{1,0:T(8,128)(2,1)S(1)}, u32[]{:S(2)}, u32[]{:S(2)}) collective-permute-start(bf16[1296,512]{1,0:T(8,128)(2,1)S(1)} %shard_map.94.own_ref.bundle_ref), channel_id=1, source_target_pairs={{0,16},{8,24},{16,0},{24,8},{1,17},{9,25},{17,1},{25,9},{2,18},{10... | collective-permute-start | bytes 3981320 | tf_op jit(solution)/shard_map/ppermute | solution.py:391
  17.1 27.6 %collective-permute-done.1.y_ref = bf16[1296,512]{1,0:T(8,128)(2,1)S(1)} collective-permute-done((bf16[1296,512]{1,0:T(8,128)(2,1)S(1)}, bf16[1296,512]{1,0:T(8,128)(2,1)S(1)}, u32[]{:S(2)}, u32[]{:S(2)}) %collective-permute-start.1) | collective-permute-done | bytes 1327136 | tf_op jit(solution)/shard_map/ppermute | solution.py:391
  44.8 1.8 %collective-permute-start.2 = (bf16[752,512]{1,0:T(8,128)(2,1)S(1)}, bf16[752,512]{1,0:T(8,128)(2,1)S(1)}, u32[]{:S(2)}, u32[]{:S(2)}) collective-permute-start(bf16[752,512]{1,0:T(8,128)(2,1)S(1)} %slice.93), channel_id=1, source_target_pairs={{0,8},{8,0},{16,24},{24,16},{1,9},{9,1},{17,25},{25,17},{2,10},{10... | collective-permute-start | bytes 2310152 | tf_op jit(solution)/shard_map/ppermute | solution.py:391
  46.6 1.6 collective-permute-start.3
  50.3 3.8 %shard_map.95 = (bf16[1024,512]{1,0:T(8,128)(2,1)S(1)}, bf16[1024,512]{1,0:T(8,128)(2,1)S(1)}, bf16[1024,512]{1,0:T(8,128)(2,1)S(1)}, bf16[3072,512]{1,0:T(8,128...) custom-call(s32[9]{0:T(128)S(1)} %stack.39.core_ref.place_ref.info_ref, s32[12]{0:T(128)S(1)} %pad_add_fusion.1.parent_ref, ...), custom_call_target="tpu_custom_call" | custom-call | tf_op jit(solution)/shard_map/pallas_call | solution.py:435
  57.1 6.2 %collective-permute-done.2.db_ref = bf16[752,512]{1,0:T(8,128)(2,1)S(1)} collective-permute-done((bf16[752,512]{1,0:T(8,128)(2,1)S(1)}, bf16[752,512]{1,0:T(8,128)(2,1)S(1)}, u32[]{:S(2)}, u32[]{:S(2)}) %collective-permute-start.2) | collective-permute-done | bytes 770080 | tf_op jit(solution)/shard_map/ppermute | solution.py:391
  65.0 3.6 %shard_map.96 = (bf16[1024,512]{1,0:T(8,128)(2,1)}, bf16[1024,512]{1,0:T(8,128)(2,1)}, f32[2,512]{1,0:T(2,128)S(1)}, f32[2,512]{1,0:T(2,128)S(1)}, f32[2,512]{1,0:T(2,128)S(1)}, /*index=5*/f32[16,256]{1,0:T(8,128)S(1)}) custom-call(s32[9]{0:T(128)S(1)} %stack.39.core_ref.place_ref.info_ref, s32[16]{0:T(128)S(1)} %pad_add_fusion.parent_ref, ...), custom_call_target="tpu_custom_call" | custom-call | tf_op jit(solution)/shard_map/pallas_call | solution.py:446
  68.6 2.1 %all-gather.5.cloned.1.call-done = bf16[5120,512]{1,0:T(8,128)(2,1)} async-done(((bf16[640,512]{1,0:T(8,128)(2,1)}), bf16[5120,512]{1,0:T(8,128)(2,1)}) %all-gather.5.cloned.1.call-update) | async-done | bytes 5242896 | tf_op jit(solution)/shard_map/all_gather | solution.py:418
  70.7 3.2 %shard_map.98 = (bf16[640,512]{1,0:T(8,128)(2,1)}, bf16[640,512]{1,0:T(8,128)(2,1)}, bf16[640,512]{1,0:T(8,128)(2,1)}, f32[8,128]{1,0:T(8,128)S(1)}) custom-call(s32[9]{0:T(128)S(1)} %stack.39.core_ref.place_ref.info_ref, bf16[8,640,512]{2,1,0:T(8,128)(2,1)} %bitcast.12, f32[16,256]{1,0:T(8,128)S(1)} %get-tuple-element.43.refs_0_), custom_call_target="tpu_custom_call" | custom-call | tf_op jit(solution)/shard_map/pallas_call | solution.py:319
  78.7 3.7 %collective-permute-done.7.y_ref = f32[16,256]{1,0:T(8,128)S(1)} collective-permute-done((f32[16,256]{1,0:T(8,128)S(1)}, f32[16,256]{1,0:T(8,128)S(1)}, u32[]{:S(2)}, u32[]{:S(2)}) %collective-permute-start.7) | collective-permute-done | bytes 16416 | tf_op jit(solution)/shard_map/ppermute | solution.py:394
  83.6 4.0 %collective-permute-done.8.z_ref = f32[16,256]{1,0:T(8,128)S(1)} collective-permute-done((f32[16,256]{1,0:T(8,128)S(1)}, f32[16,256]{1,0:T(8,128)S(1)}, u32[]{:S(2)}, u32[]{:S(2)}) %collective-permute-start.8) | collective-permute-done | bytes 16416 | tf_op jit(solution)/shard_map/ppermute | solution.py:394
  87.6 2.4 %shard_map.100 = (f32[2,512]{1,0:T(2,128)S(1)}, f32[16,256]{1,0:T(8,128)S(1)}) custom-call(s32[16]{0:T(128)S(1)} %pad_add_fusion.parent_ref, f32[16,256]{1,0:T(8,128)S(1)} %shard_map.99.y_ref, f32[16,256]{1,0:T(8,128)S(1)} %collective-permute-done.8.z_ref, f32[2,512]{1,0:T(2,128)S(1)} %get-tuple-element.46.reduced_ref, ...), custom_call_target="tpu_custom_call" | custom-call | tf_op jit(solution)/shard_map/pallas_call | solution.py:492
  91.3 4.7 %collective-permute-done.10 = f32[16,256]{1,0:T(8,128)S(1)} collective-permute-done((f32[16,256]{1,0:T(8,128)S(1)}, f32[16,256]{1,0:T(8,128)S(1)}, u32[]{:S(2)}, u32[]{:S(2)}) %collective-permute-start.10) | collective-permute-done | bytes 16416 | tf_op jit(solution)/shard_map/ppermute | solution.py:394
  96.4 4.7 %collective-permute-done.11.z_ref = f32[16,256]{1,0:T(8,128)S(1)} collective-permute-done((f32[16,256]{1,0:T(8,128)S(1)}, f32[16,256]{1,0:T(8,128)S(1)}, u32[]{:S(2)}, u32[]{:S(2)}) %collective-permute-start.11) | collective-permute-done | bytes 16416 | tf_op jit(solution)/shard_map/ppermute | solution.py:394
  101.1 2.4 %shard_map.101 = (f32[2,512]{1,0:T(2,128)S(1)}, f32[16,256]{1,0:T(8,128)S(1)}) custom-call(s32[16]{0:T(128)S(1)} %pad_add_fusion.parent_ref, f32[16,256]{1,0:T(8,128)S(1)} %add.84.y_ref, f32[16,256]{1,0:T(8,128)S(1)} %collective-permute-done.11.z_ref, f32[2,512]{1,0:T(2,128)S(1)} %get-tuple-element.46.reduced_ref, ...), custom_call_target="tpu_custom_call" | custom-call | tf_op jit(solution)/shard_map/pallas_call | solution.py:492
  104.7 3.7 %collective-permute-done.13 = f32[16,256]{1,0:T(8,128)S(1)} collective-permute-done((f32[16,256]{1,0:T(8,128)S(1)}, f32[16,256]{1,0:T(8,128)S(1)}, u32[]{:S(2)}, u32[]{:S(2)}) %collective-permute-start.13) | collective-permute-done | bytes 16416 | tf_op jit(solution)/shard_map/ppermute | solution.py:394
  108.5 1.7 %collective-permute-start.14 = (f32[16,256]{1,0:T(8,128)S(1)}, f32[16,256]{1,0:T(8,128)S(1)}, u32[]{:S(2)}, u32[]{:S(2)}) collective-permute-start(f32[16,256]{1,0:T(8,128)S(1)} %add.86.y_ref), channel_id=1, source_target_pairs={{0,4},{1,5},{2,6},{3,7},{4,0},{5,1},{6,2},{7,3},{8,12},{9,13},{10,... | collective-permute-start | bytes 49160 | tf_op jit(solution)/shard_map/ppermute | solution.py:394
  110.1 3.0 %collective-permute-done.14.z_ref = f32[16,256]{1,0:T(8,128)S(1)} collective-permute-done((f32[16,256]{1,0:T(8,128)S(1)}, f32[16,256]{1,0:T(8,128)S(1)}, u32[]{:S(2)}, u32[]{:S(2)}) %collective-permute-start.14) | collective-permute-done | bytes 16416 | tf_op jit(solution)/shard_map/ppermute | solution.py:394
  113.2 2.4 %shard_map.102 = (f32[2,512]{1,0:T(2,128)S(1)}, f32[16,256]{1,0:T(8,128)S(1)}) custom-call(s32[16]{0:T(128)S(1)} %pad_add_fusion.parent_ref, f32[16,256]{1,0:T(8,128)S(1)} %add.86.y_ref, f32[16,256]{1,0:T(8,128)S(1)} %collective-permute-done.14.z_ref, f32[2,512]{1,0:T(2,128)S(1)} %get-tuple-element.46.reduced_ref, ...), custom_call_target="tpu_custom_call" | custom-call | tf_op jit(solution)/shard_map/pallas_call | solution.py:492
  117.2 2.2 %shard_map.103 = (bf16[384,512]{1,0:T(8,128)(2,1)S(1)}, bf16[384,512]{1,0:T(8,128)(2,1)S(1)}, bf16[384,512]{1,0:T(8,128)(2,1)S(1)}, f32[8,128]{1,0:T(8,128)S(1)}) custom-call(s32[9]{0:T(128)S(1)} %stack.39.core_ref.place_ref.info_ref, bf16[8,384,512]{2,1,0:T(8,128)(2,1)} %bitcast.15, f32[16,256]{1,0:T(8,128)S(1)} %get-tuple-element.58.refs_0_), custom_call_target="tpu_custom_call" | custom-call | tf_op jit(solution)/shard_map/pallas_call | solution.py:319
  120.6 1.6 %shard_map.107 = bf16[1920,512]{1,0:T(8,128)(2,1)S(1)} custom-call(bf16[640,512]{1,0:T(8,128)(2,1)} %collective-permute-done.18.refs_6_.refs_0_, bf16[640,512]{1,0:T(8,128)(2,1)} %collective-permute-done.19.refs_7_.refs_1_, bf16[640,512]{1,0:T(8,128)(2,1)} %collective-permute-done.20.refs_8_.refs_2_, f32[16,256]{1,0:T(8,128)S(1)} %shard_map.104.refs_9_.y_ref.refs_3_), custom_call_target="tpu_custom_call" | custom-call | tf_op jit(solution)/shard_map/pallas_call | solution.py:282
  122.3 1.5 collective-permute-start.25
  125.8 1.9 %collective-permute-start.17 = (f32[16,256]{1,0:T(8,128)S(1)}, f32[16,256]{1,0:T(8,128)S(1)}, u32[]{:S(2)}, u32[]{:S(2)}) collective-permute-start(f32[16,256]{1,0:T(8,128)S(1)} %shard_map.104.refs_9_.y_ref.refs_3_), channel_id=1, source_target_pairs={{0,4},{1,5},{2,6},{3,7},{4,0},{5,1},{6,2},{7,3},{8,12},{9,13},{10,... | collective-permute-start | bytes 49160 | tf_op jit(solution)/shard_map/ppermute | solution.py:394
  127.8 5.1 %shard_map.105 = (f32[2,512,512]{2,1,0:T(8,128)S(1)}, f32[8,128]{1,0:T(8,128)S(1)}) custom-call(s32[9]{0:T(128)S(1)} %stack.39.core_ref.place_ref.info_ref, s32[16]{0:T(128)S(1)} %pad_add_fusion.parent_ref, bf16[1024,512]{1,0:T(8,128)(2,1)S(1)} %copy-done.2, bf16[1024,512]{1,0:T(8,128)(2,1)S(1)} %copy-done.5, bf16[1024,512]{1,0:T(8,128)(2,1)S(1)} %copy-done.8, ...), custom_call_target="tpu_custom_call" | custom-call | flops 1543503872 | bytes 2097152 | tf_op jit(solution)/shard_map/pallas_call | solution.py:469
  132.9 1.8 %shard_map.106 = (f32[2,512]{1,0:T(2,128)}, f32[4,256]{1,0:T(4,128)S(1)}) custom-call(s32[16]{0:T(128)S(1)} %pad_add_fusion.parent_ref, f32[16,256]{1,0:T(8,128)S(1)} %shard_map.104.refs_9_.y_ref.refs_3_, f32[16,256]{1,0:T(8,128)S(1)} %collective-permute-done.17.z_ref, f32[2,512]{1,0:T(2,128)S(1)} %get-tuple-element.46.reduced_ref, ...), custom_call_target="tpu_custom_call" | custom-call | tf_op jit(solution)/shard_map/pallas_call | solution.py:492
  137.3 4.2 %shard_map.108 = (f32[2,512,512]{2,1,0:T(8,128)S(1)}, f32[8,128]{1,0:T(8,128)S(1)}) custom-call(s32[9]{0:T(128)S(1)} %stack.39.core_ref.place_ref.info_ref, s32[16]{0:T(128)S(1)} %pad_add_fusion.parent_ref, bf16[1024,512]{1,0:T(8,128)(2,1)S(1)} %copy-done.2, bf16[1024,512]{1,0:T(8,128)(2,1)S(1)} %copy-done.5, bf16[1024,512]{1,0:T(8,128)(2,1)S(1)} %copy-done.8, ...), custom_call_target="tpu_custom_call" | custom-call | flops 1543503872 | bytes 2097152 | tf_op jit(solution)/shard_map/pallas_call | solution.py:469
  141.5 1.9 %collective-permute-done.26.refs_5_.refs_1_ = bf16[384,512]{1,0:T(8,128)(2,1)S(1)} collective-permute-done((bf16[384,512]{1,0:T(8,128)(2,1)S(1)}, bf16[384,512]{1,0:T(8,128)(2,1)S(1)}, u32[]{:S(2)}, u32[]{:S(2)}) %collective-permute-start.26) | collective-permute-done | bytes 393248 | tf_op jit(solution)/shard_map/ppermute | solution.py:391
  143.6 2.0 %collective-permute-start.24 = (f32[4,256]{1,0:T(4,128)S(1)}, f32[4,256]{1,0:T(4,128)S(1)}, u32[]{:S(2)}, u32[]{:S(2)}) collective-permute-start(f32[4,256]{1,0:T(4,128)S(1)} %shard_map.109.refs_7_.y_ref.refs_3_.refs_5_), channel_id=1, source_target_pairs={{0,4},{1,5},{2,6},{3,7},{4,0},{5,1},{6,2},{7,3},{8,12},{9,13},{10,... | collective-permute-start | bytes 12296 | tf_op jit(solution)/shard_map/ppermute | solution.py:394
  145.6 2.9 %shard_map.110 = (f32[2,512,512]{2,1,0:T(8,128)S(1)}, f32[8,128]{1,0:T(8,128)S(1)}, f32[2,512,1024]{2,1,0:T(8,128)}) custom-call(s32[9]{0:T(128)S(1)} %stack.39.core_ref.place_ref.info_ref, s32[16]{0:T(128)S(1)} %pad_add_fusion.parent_ref, bf16[1024,512]{1,0:T(8,128)(2,1)S(1)} %copy-done.2, ...), custom_call_target="tpu_custom_call", output_to_operand_aliasing={{0}: (10, {})} | custom-call | flops 603979776 | bytes 2097152 | tf_op jit(solution)/shard_map/pallas_call | solution.py:469
  149.4 3.6 %shard_map.113 = (f32[2,512,512]{2,1,0:T(8,128)S(1)}, f32[8,128]{1,0:T(8,128)}, f32[2,512,1024]{2,1,0:T(8,128)}) custom-call(s32[9]{0:T(128)S(1)} %stack.39.core_ref.place_ref.info_ref, s32[16]{0:T(128)S(1)} %pad_add_fusion.parent_ref, bf16[1024,512]{1,0:T(8,128)(2,1)S(1)} %copy-done.2, ...), custom_call_target="tpu_custom_call", output_to_operand_aliasing={{0}: (8, {}), {2}: (9, {})} | custom-call | flops 603979776 | bytes 2097152 | tf_op jit(solution)/shard_map/pallas_call | solution.py:469
  (121 shorter events, 26.3 us)
Async XLA Ops:
  7.2 63.5 %all-gather.5.cloned.1.call-start = ((), (), s32[]{:S(2)}) async-start(), calls=%async_computation | async-start | bytes 5898240 | tf_op jit(solution)/shard_map/all_gather | solution.py:418
  11.8 105.4 %all-gather.7.cloned.1.call-start = ((), (), s32[]{:S(2)}) async-start(), calls=%async_computation.1 | async-start | bytes 3538944 | tf_op jit(solution)/shard_map/all_gather | solution.py:418
  12.6 37.7 %copy-start.15 = (bf16[4,256,256]{2,1,0:T(8,128)(2,1)S(1)}, bf16[4,256,256]{2,1,0:T(8,128)(2,1)}, u32[]{:S(2)}) copy-start(bf16[4,256,256]{2,1,0:T(8,128)(2,1)} %inverse_ref.7) | copy-start | bytes 1572868
  12.6 32.2 %collective-permute-start.1 = (bf16[1296,512]{1,0:T(8,128)(2,1)S(1)}, bf16[1296,512]{1,0:T(8,128)(2,1)S(1)}, u32[]{:S(2)}, u32[]{:S(2)}) collective-permute-start(bf16[1296,512]{1,0:T(8,128)(2,1)S(1)} %shard_map.94.own_ref.bundle_ref), channel_id=1, source_target_pairs={{0,16},{8,24},{16,0},{24,8},{1,17},{9,25},{17,1},{25,9},{2,18},{10... | collective-permute-start | bytes 3981320 | tf_op jit(solution)/shard_map/ppermute | solution.py:391
  15.6 31.0 %collective-permute-start = (bf16[1296,512]{1,0:T(8,128)(2,1)S(1)}, bf16[1296,512]{1,0:T(8,128)(2,1)S(1)}, u32[]{:S(2)}, u32[]{:S(2)}) collective-permute-start(bf16[1296,512]{1,0:T(8,128)(2,1)S(1)} %shard_map.94.own_ref.bundle_ref), channel_id=1, source_target_pairs={{0,8},{8,0},{16,24},{24,16},{1,9},{9,1},{17,25},{25,17},{2,10},{10... | collective-permute-start | bytes 3981320 | tf_op jit(solution)/shard_map/ppermute | solution.py:391
  44.8 18.5 %collective-permute-start.2 = (bf16[752,512]{1,0:T(8,128)(2,1)S(1)}, bf16[752,512]{1,0:T(8,128)(2,1)S(1)}, u32[]{:S(2)}, u32[]{:S(2)}) collective-permute-start(bf16[752,512]{1,0:T(8,128)(2,1)S(1)} %slice.93), channel_id=1, source_target_pairs={{0,8},{8,0},{16,24},{24,16},{1,9},{9,1},{17,25},{25,17},{2,10},{10... | collective-permute-start | bytes 2310152 | tf_op jit(solution)/shard_map/ppermute | solution.py:391
  46.6 17.1 %collective-permute-start.3 = (bf16[544,512]{1,0:T(8,128)(2,1)S(1)}, bf16[544,512]{1,0:T(8,128)(2,1)S(1)}, u32[]{:S(2)}, u32[]{:S(2)}) collective-permute-start(bf16[544,512]{1,0:T(8,128)(2,1)S(1)} %slice.105), channel_id=1, source_target_pairs={{0,16},{8,24},{16,0},{24,8},{1,17},{9,25},{17,1},{25,9},{2,18},{10... | collective-permute-start | bytes 1671176 | tf_op jit(solution)/shard_map/ppermute | solution.py:391
  48.3 2.0 %collective-permute-start.5 = (bf16[512,512]{1,0:T(8,128)(2,1)S(1)}, bf16[512,512]{1,0:T(8,128)(2,1)S(1)}, u32[]{:S(2)}, u32[]{:S(2)}) collective-permute-start(bf16[512,512]{1,0:T(8,128)(2,1)S(1)} %pad_maximum_fusion), channel_id=1, source_target_pairs={{0,1},{1,0},{2,3},{3,2},{4,5},{5,4},{6,7},{7,6},{8,9},{9,8},{10,11... | collective-permute-start | bytes 1572872 | tf_op jit(solution)/shard_map/ppermute | solution.py:397
  63.4 1.6 %collective-permute-start.4 = (bf16[256,512]{1,0:T(8,128)(2,1)S(1)}, bf16[256,512]{1,0:T(8,128)(2,1)S(1)}, u32[]{:S(2)}, u32[]{:S(2)}) collective-permute-start(bf16[256,512]{1,0:T(8,128)(2,1)S(1)} %slice.106), channel_id=1, source_target_pairs={{0,1},{1,0},{2,3},{3,2},{4,5},{5,4},{6,7},{7,6},{8,9},{9,8},{10,11... | collective-permute-start | bytes 786440 | tf_op jit(solution)/shard_map/ppermute | solution.py:397
  73.9 46.6 %collective-permute-start.18 = (bf16[640,512]{1,0:T(8,128)(2,1)}, bf16[640,512]{1,0:T(8,128)(2,1)}, u32[]{:S(2)}, u32[]{:S(2)}) collective-permute-start(bf16[640,512]{1,0:T(8,128)(2,1)} %get-tuple-element.62), channel_id=1, source_target_pairs={{0,8},{8,0},{16,24},{24,16},{1,9},{9,1},{17,25},{25,17},{2,10},{10... | collective-permute-start | bytes 1966088 | tf_op jit(solution)/shard_map/ppermute | solution.py:391
  75.5 45.1 %collective-permute-start.19 = (bf16[640,512]{1,0:T(8,128)(2,1)}, bf16[640,512]{1,0:T(8,128)(2,1)}, u32[]{:S(2)}, u32[]{:S(2)}) collective-permute-start(bf16[640,512]{1,0:T(8,128)(2,1)} %get-tuple-element.63), channel_id=1, source_target_pairs={{0,16},{8,24},{16,0},{24,8},{1,17},{9,25},{17,1},{25,9},{2,18},{10... | collective-permute-start | bytes 1966088 | tf_op jit(solution)/shard_map/ppermute | solution.py:391
  76.9 43.6 %collective-permute-start.20 = (bf16[640,512]{1,0:T(8,128)(2,1)}, bf16[640,512]{1,0:T(8,128)(2,1)}, u32[]{:S(2)}, u32[]{:S(2)}) collective-permute-start(bf16[640,512]{1,0:T(8,128)(2,1)} %get-tuple-element.64), channel_id=1, source_target_pairs={{0,24},{8,16},{16,8},{24,0},{1,25},{9,17},{17,9},{25,1},{2,26},{10... | collective-permute-start | bytes 1966088 | tf_op jit(solution)/shard_map/ppermute | solution.py:391
  77.5 1.2 collective-permute-start.6
  78.7 3.7 %collective-permute-start.7 = (f32[16,256]{1,0:T(8,128)S(1)}, f32[16,256]{1,0:T(8,128)S(1)}, u32[]{:S(2)}, u32[]{:S(2)}) collective-permute-start(f32[16,256]{1,0:T(8,128)S(1)} %add.82.x_ref), channel_id=1, source_target_pairs={{0,2},{1,3},{2,0},{3,1},{4,6},{5,7},{6,4},{7,5},{8,10},{9,11},{10,... | collective-permute-start | bytes 49160 | tf_op jit(solution)/shard_map/ppermute | solution.py:394
  82.4 5.2 %collective-permute-start.8 = (f32[16,256]{1,0:T(8,128)S(1)}, f32[16,256]{1,0:T(8,128)S(1)}, u32[]{:S(2)}, u32[]{:S(2)}) collective-permute-start(f32[16,256]{1,0:T(8,128)S(1)} %shard_map.99.y_ref), channel_id=1, source_target_pairs={{0,4},{1,5},{2,6},{3,7},{4,0},{5,1},{6,2},{7,3},{8,12},{9,13},{10,... | collective-permute-start | bytes 49160 | tf_op jit(solution)/shard_map/ppermute | solution.py:394
  90.0 1.2 collective-permute-start.9
  91.3 4.7 %collective-permute-start.10 = (f32[16,256]{1,0:T(8,128)S(1)}, f32[16,256]{1,0:T(8,128)S(1)}, u32[]{:S(2)}, u32[]{:S(2)}) collective-permute-start(f32[16,256]{1,0:T(8,128)S(1)} %add.83), channel_id=1, source_target_pairs={{0,2},{1,3},{2,0},{3,1},{4,6},{5,7},{6,4},{7,5},{8,10},{9,11},{10,... | collective-permute-start | bytes 49160 | tf_op jit(solution)/shard_map/ppermute | solution.py:394
  96.0 5.1 %collective-permute-start.11 = (f32[16,256]{1,0:T(8,128)S(1)}, f32[16,256]{1,0:T(8,128)S(1)}, u32[]{:S(2)}, u32[]{:S(2)}) collective-permute-start(f32[16,256]{1,0:T(8,128)S(1)} %add.84.y_ref), channel_id=1, source_target_pairs={{0,4},{1,5},{2,6},{3,7},{4,0},{5,1},{6,2},{7,3},{8,12},{9,13},{10,... | collective-permute-start | bytes 49160 | tf_op jit(solution)/shard_map/ppermute | solution.py:394
  103.5 1.2 collective-permute-start.12
  104.7 3.7 %collective-permute-start.13 = (f32[16,256]{1,0:T(8,128)S(1)}, f32[16,256]{1,0:T(8,128)S(1)}, u32[]{:S(2)}, u32[]{:S(2)}) collective-permute-start(f32[16,256]{1,0:T(8,128)S(1)} %add.85), channel_id=1, source_target_pairs={{0,2},{1,3},{2,0},{3,1},{4,6},{5,7},{6,4},{7,5},{8,10},{9,11},{10,... | collective-permute-start | bytes 49160 | tf_op jit(solution)/shard_map/ppermute | solution.py:394
  108.5 4.7 %collective-permute-start.14 = (f32[16,256]{1,0:T(8,128)S(1)}, f32[16,256]{1,0:T(8,128)S(1)}, u32[]{:S(2)}, u32[]{:S(2)}) collective-permute-start(f32[16,256]{1,0:T(8,128)S(1)} %add.86.y_ref), channel_id=1, source_target_pairs={{0,4},{1,5},{2,6},{3,7},{4,0},{5,1},{6,2},{7,3},{8,12},{9,13},{10,... | collective-permute-start | bytes 49160 | tf_op jit(solution)/shard_map/ppermute | solution.py:394
  115.5 1.2 collective-permute-start.15
  116.8 3.7 %collective-permute-start.16 = (f32[16,256]{1,0:T(8,128)S(1)}, f32[16,256]{1,0:T(8,128)S(1)}, u32[]{:S(2)}, u32[]{:S(2)}) collective-permute-start(f32[16,256]{1,0:T(8,128)S(1)} %add.87.x_ref), channel_id=1, source_target_pairs={{0,2},{1,3},{2,0},{3,1},{4,6},{5,7},{6,4},{7,5},{8,10},{9,11},{10,... | collective-permute-start | bytes 49160 | tf_op jit(solution)/shard_map/ppermute | solution.py:394
  122.2 15.1 %collective-permute-start.23 = (bf16[1920,512]{1,0:T(8,128)(2,1)S(1)}, bf16[1920,512]{1,0:T(8,128)(2,1)S(1)}, u32[]{:S(2)}, u32[]{:S(2)}) collective-permute-start(bf16[1920,512]{1,0:T(8,128)(2,1)S(1)} %shard_map.107), channel_id=1, source_target_pairs={{0,1},{1,0},{2,3},{3,2},{4,5},{5,4},{6,7},{7,6},{8,9},{9,8},{10,11... | collective-permute-start | bytes 5898248 | tf_op jit(solution)/shard_map/ppermute | solution.py:397
  122.3 19.2 %collective-permute-start.25 = (bf16[384,512]{1,0:T(8,128)(2,1)S(1)}, bf16[384,512]{1,0:T(8,128)(2,1)S(1)}, u32[]{:S(2)}, u32[]{:S(2)}) collective-permute-start(bf16[384,512]{1,0:T(8,128)(2,1)S(1)} %get-tuple-element.69), channel_id=1, source_target_pairs={{0,8},{8,0},{16,24},{24,16},{1,9},{9,1},{17,25},{25,17},{2,10},{10... | collective-permute-start | bytes 1179656 | tf_op jit(solution)/shard_map/ppermute | solution.py:391
  123.8 19.6 %collective-permute-start.26 = (bf16[384,512]{1,0:T(8,128)(2,1)S(1)}, bf16[384,512]{1,0:T(8,128)(2,1)S(1)}, u32[]{:S(2)}, u32[]{:S(2)}) collective-permute-start(bf16[384,512]{1,0:T(8,128)(2,1)S(1)} %get-tuple-element.70), channel_id=1, source_target_pairs={{0,16},{8,24},{16,0},{24,8},{1,17},{9,25},{17,1},{25,9},{2,18},{10... | collective-permute-start | bytes 1179656 | tf_op jit(solution)/shard_map/ppermute | solution.py:391
  125.3 18.1 %collective-permute-start.27 = (bf16[384,512]{1,0:T(8,128)(2,1)S(1)}, bf16[384,512]{1,0:T(8,128)(2,1)S(1)}, u32[]{:S(2)}, u32[]{:S(2)}) collective-permute-start(bf16[384,512]{1,0:T(8,128)(2,1)S(1)} %get-tuple-element.71), channel_id=1, source_target_pairs={{0,24},{8,16},{16,8},{24,0},{1,25},{9,17},{17,9},{25,1},{2,26},{10... | collective-permute-start | bytes 1179656 | tf_op jit(solution)/shard_map/ppermute | solution.py:391
  125.8 7.1 %collective-permute-start.17 = (f32[16,256]{1,0:T(8,128)S(1)}, f32[16,256]{1,0:T(8,128)S(1)}, u32[]{:S(2)}, u32[]{:S(2)}) collective-permute-start(f32[16,256]{1,0:T(8,128)S(1)} %shard_map.104.refs_9_.y_ref.refs_3_), channel_id=1, source_target_pairs={{0,4},{1,5},{2,6},{3,7},{4,0},{5,1},{6,2},{7,3},{8,12},{9,13},{10,... | collective-permute-start | bytes 49160 | tf_op jit(solution)/shard_map/ppermute | solution.py:394
  134.7 1.2 collective-permute-start.21
  135.9 5.6 %collective-permute-start.22 = (f32[4,256]{1,0:T(4,128)S(1)}, f32[4,256]{1,0:T(4,128)S(1)}, u32[]{:S(2)}, u32[]{:S(2)}) collective-permute-start(f32[4,256]{1,0:T(4,128)S(1)} %add.88.x_ref), channel_id=1, source_target_pairs={{0,2},{1,3},{2,0},{3,1},{4,6},{5,7},{6,4},{7,5},{8,10},{9,11},{10,... | collective-permute-start | bytes 12296 | tf_op jit(solution)/shard_map/ppermute | solution.py:394
  143.5 5.9 %collective-permute-start.28 = (bf16[1152,512]{1,0:T(8,128)(2,1)S(1)}, bf16[1152,512]{1,0:T(8,128)(2,1)S(1)}, u32[]{:S(2)}, u32[]{:S(2)}) collective-permute-start(bf16[1152,512]{1,0:T(8,128)(2,1)S(1)} %shard_map.112), channel_id=1, source_target_pairs={{0,1},{1,0},{2,3},{3,2},{4,5},{5,4},{6,7},{7,6},{8,9},{9,8},{10,11... | collective-permute-start | bytes 3538952 | tf_op jit(solution)/shard_map/ppermute | solution.py:397
  143.6 5.0 %collective-permute-start.24 = (f32[4,256]{1,0:T(4,128)S(1)}, f32[4,256]{1,0:T(4,128)S(1)}, u32[]{:S(2)}, u32[]{:S(2)}) collective-permute-start(f32[4,256]{1,0:T(4,128)S(1)} %shard_map.109.refs_7_.y_ref.refs_3_.refs_5_), channel_id=1, source_target_pairs={{0,4},{1,5},{2,6},{3,7},{4,0},{5,1},{6,2},{7,3},{8,12},{9,13},{10,... | collective-permute-start | bytes 12296 | tf_op jit(solution)/shard_map/ppermute | solution.py:394
  (20 other events, 278.2 us)
Sparse Core Ops, SparseCore 0:
  11.9 58.7 all-gather.4
  72.3 38.4 all-gather.6
